TPU v7x, 256 devices: a whole 4x4x8 slice. The times are simulated.
256 devices in a mesh: blk: 64 (over z, y, x_hi), mp: 4 (over x_lo, core).
Axes of the slice: x: 4 (x_hi: 2, x_lo: 2; x = x_hi * 2 + x_lo), y: 4, z: 8, core: 2. Of those that a mesh axis runs over, the one named last changes fastest.
Arguments:
- dna_ids: int32 [24576, 16], P('blk'), may hold values from 0 to 4095
- meth_ids: int32 [24576, 16], P('blk'), may hold values from 0 to 511
- pair_index: int32 [24576], P('blk'), may hold values from 0 to 24575, each once
- dna_table: bfloat16 [4096, 1024], P(None, 'mp'), may hold values from -6 to 6
- meth_table: bfloat16 [512, 768], replicated, may hold values from -6 to 6
- dna_proj: bfloat16 [1024, 512], P('mp'), may hold values from -0.1875 to 0.1875
- meth_proj: bfloat16 [768, 512], replicated, may hold values from -0.21875 to 0.21875
- logit_scale: float32 [1], replicated, may hold values from 40 to 64
- logit_bias: float32 [1], replicated, may hold values from -8 to -6
Outputs:
- grad_dna_proj: float32 [1024, 512], P('mp')
- grad_meth_proj: float32 [768, 512], replicated
Inputs may be any that keep to these rules, and one draw needn't show every extreme that they name: `pair_index`: every methylation window is paired with exactly one DNA window.
All inputs are finite; a program needn't handle non-finite values.
Results may differ from a plain program's by a relative error of at most 0.00085.
Values may be sent and summed in bfloat16 or wider, within the bound.
A program may use at most 128 MiB of HBM per device.

v0:
```python
import jax
import jax.numpy as jnp
from jax import lax
from jax.sharding import PartitionSpec as P

epsilon = 1e-06


def pool_rows(lookup, token_ids):
    gathered = jnp.take(lookup, token_ids, axis=0).astype(jnp.float32)
    return jnp.mean(gathered, axis=1).astype(jnp.bfloat16)


def normal_parts(raw_rows):
    inverse = lax.rsqrt(jnp.sum(raw_rows * raw_rows, axis=1, keepdims=True) + epsilon)
    return (inverse, raw_rows * inverse)


def normal_grad(inverse, unit_rows, upstream):
    inner = jnp.sum(unit_rows * upstream, axis=1, keepdims=True)
    return (inverse * (upstream - unit_rows * inner)).astype(jnp.bfloat16)


def contract_rows(left, right):
    return lax.dot_general(
        left, right, (((0,), (0,)), ((), ())), preferred_element_type=jnp.float32
    )


def per_device(
    dna_ids,
    meth_ids,
    pair_index,
    dna_table,
    meth_table,
    dna_proj,
    meth_proj,
    logit_scale,
    logit_bias,
):
    group_rows = dna_ids.shape[0]
    own_rows = group_rows // lax.axis_size("mp")
    mp_slot = lax.axis_index("mp")
    dna_pooled = pool_rows(dna_table, dna_ids)
    dna_partial = jnp.dot(dna_pooled, dna_proj, preferred_element_type=jnp.float32)
    dna_raw = lax.psum(dna_partial, "mp")
    dna_inverse, dna_unit = normal_parts(dna_raw)
    dna_rows = dna_unit.astype(jnp.bfloat16)
    own_ids = lax.dynamic_slice_in_dim(meth_ids, mp_slot * own_rows, own_rows, 0)
    meth_pooled = pool_rows(meth_table, own_ids)
    meth_inverse, meth_unit = normal_parts(
        jnp.dot(meth_pooled, meth_proj, preferred_element_type=jnp.float32)
    )
    meth_rows = meth_unit.astype(jnp.bfloat16)
    scale_value = logit_scale[0]
    bias_value = logit_bias[0]
    column_block = lax.all_gather(meth_rows, "blk", axis=0, tiled=True)
    logits = (
        scale_value * jnp.dot(dna_rows, column_block.T, preferred_element_type=jnp.float32)
        + bias_value
    )
    position = jnp.arange(column_block.shape[0], dtype=jnp.int32)
    anchor = position // own_rows * group_rows + mp_slot * own_rows + position % own_rows
    labels = (pair_index[:, None] == anchor[None, :]).astype(jnp.float32)
    grad_tile = (jax.nn.sigmoid(logits) - labels).astype(jnp.bfloat16)
    row_acc = jnp.dot(grad_tile, column_block, preferred_element_type=jnp.float32)
    col_acc = contract_rows(grad_tile, dna_rows)
    row_acc, col_acc = (row_acc, col_acc)
    col_part = lax.psum_scatter(col_acc, "blk", scatter_dimension=0, tiled=True)
    meth_back = normal_grad(meth_inverse, meth_unit, scale_value * col_part)
    meth_term = contract_rows(meth_pooled, meth_back)
    row_sum, meth_group = lax.psum((row_acc, meth_term), "mp")
    dna_back = normal_grad(dna_inverse, dna_unit, scale_value * row_sum)
    dna_term = contract_rows(dna_pooled, dna_back)
    grad_dna_proj, grad_meth_proj = lax.psum((dna_term, meth_group), "blk")
    return (grad_dna_proj, grad_meth_proj)


def solution(mesh):
    placed = (
        P("blk", None),
        P("blk", None),
        P("blk"),
        P(None, "mp"),
        P(),
        P("mp", None),
        P(),
        P(),
        P(),
    )
    return jax.shard_map(
        per_device, mesh=mesh, in_specs=placed, out_specs=(P("mp", None), P()), check_vma=False
    )
```

profile of v0, /device:TPU:8, one launch (start us, length us, event | category | flops | bytes accessed | tf_op | source)
XLA Modules:
  0.0 1833.9 jit_solution(11987944832849880575)
XLA Ops:
  8.0 0.0 copy-start
  8.0 0.0 all-reduce.6.cloned.1.call-start
  8.1 0.9 compare_and_fusion
  8.9 0.7 compare_select_fusion
  9.7 0.8 copy.13
  10.5 0.1 copy.14
  10.6 0.1 reshape.51
  10.7 0.0 copy-done
  10.7 0.0 copy-start.5
  10.7 24.9 %gather_fusion = bf16[6144,256]{1,0:T(8,128)(2,1)} fusion(bf16[4096,256]{1,0:T(8,128)(2,1)S(1)} %copy-done, s32[6144]{0:T(1024)S(1)} %broadcast_clamp_fusion), kind=kCustom, calls=%fused_computation | custom fusion | bytes 6316032 | tf_op jit(solution)/shard_map/jit(_take)/gather | solution.py:10
  35.7 4.1 convert_reduce_fusion
  39.8 1.1 fusion.8
  40.9 0.0 all-reduce.6.cloned.1.call-update
  41.0 0.0 all-gather.2.cloned.1.call-start
  41.0 0.8 compare_and_fusion.1
  41.8 0.1 copy.15
  41.9 0.1 copy.16
  42.0 0.1 reshape.59
  42.1 0.0 copy-done.1
  42.1 5.7 gather_fusion.1
  47.8 3.0 convert_reduce_fusion.1
  50.8 0.0 copy-start.4
  50.8 0.7 copy-done.4
  51.5 1.5 multiply_reduce_fusion.3
  53.0 0.7 multiply_convert_fusion.6
  53.7 0.0 all-gather.2.cloned.1.call-update
  53.8 0.0 reduce-scatter.2.cloned.1.call-start
  55.1 33.7 %all-reduce.6.cloned.1.call-done = f32[384,512]{1,0:T(8,128)} async-done(((f32[384,512]{1,0:T(8,128)}), f32[384,512]{1,0:T(8,128)}) %all-reduce.6.cloned.1.call-update) | async-done | bytes 786448 | tf_op jit(solution)/shard_map/psum | solution.py:46
  88.8 1.3 multiply_reduce_fusion.1
  90.1 105.0 %all-gather.2.cloned.1.call-done = bf16[6144,512]{1,0:T(8,128)(2,1)} async-done(((bf16[96,512]{1,0:T(8,128)(2,1)}), bf16[6144,512]{1,0:T(8,128)(2,1)}) %all-gather.2.cloned.1.call-update) | async-done | bytes 6291472 | tf_op jit(solution)/shard_map/all_gather | solution.py:57
  195.1 6.9 subtract_convert_fusion
  202.1 2.1 copy-done.3
  204.2 6.5 fusion.24
  210.7 0.0 reduce-scatter.2.cloned.1.call-update
  210.7 0.0 all-reduce.10.cloned.1.call-start
  210.8 7.7 fusion.25
  218.5 826.9 %reduce-scatter.2.cloned.1.call-done = f32[96,512]{1,0:T(8,128)} async-done(((f32[6144,512]{1,0:T(8,128)}), f32[96,512]{1,0:T(8,128)}) %reduce-scatter.2.cloned.1.call-update) | async-done | bytes 196624 | tf_op jit(solution)/shard_map/reduce_scatter | solution.py:69
  1045.4 1.1 multiply_reduce_fusion.2
  1046.5 2.6 fusion.4
  1049.1 0.0 all-reduce.10.cloned.1.call-update
  1049.1 0.0 all-reduce.8.cloned.1.call-start
  1049.2 65.1 %all-reduce.10.cloned.1.call-done = (f32[384,512]{1,0:T(8,128)}, f32[768,512]{1,0:T(8,128)}) async-done(((f32[384,512]{1,0:T(8,128)}, f32[768,512]{1,0:T(8,128)}), (f32[384,512]{1,0:T(8,128)}, f32[768,512]{1,0:T(8,128)})) %all-reduce.10.cloned.1.call-update) | async-done | bytes 2359312 | tf_op jit(solution)/shard_map/psum | solution.py:72
  1114.3 1.4 multiply_reduce_fusion
  1115.6 2.4 fusion
  1118.0 0.0 all-reduce.8.cloned.1.call-update
  1118.0 703.8 %all-reduce.8.cloned.1.call-done = (f32[256,512]{1,0:T(8,128)}, f32[768,512]{1,0:T(8,128)}) async-done(((f32[256,512]{1,0:T(8,128)}, f32[768,512]{1,0:T(8,128)}), (f32[256,512]{1,0:T(8,128)}, f32[768,512]{1,0:T(8,128)})) %all-reduce.8.cloned.1.call-update) | async-done | bytes 2097168 | tf_op jit(solution)/shard_map/psum | solution.py:75
  1821.8 1.9 copy.24
  1823.7 2.7 copy.25
  (12 shorter events, 0.1 us)
Async XLA Ops:
  8.0 2.7 copy-start
  8.0 80.8 %all-reduce.6.cloned.1.call-start = ((), (), s32[]{:S(2)}) async-start(), calls=%async_computation.1 | async-start | bytes 1572864 | tf_op jit(solution)/shard_map/psum | solution.py:46
  10.7 29.0 %copy-start.5 = (bf16[256,512]{1,0:T(8,128)(2,1)S(1)}, bf16[256,512]{1,0:T(8,128)(2,1)}, u32[]{:S(2)}) copy-start(bf16[256,512]{1,0:T(8,128)(2,1)} %param.14) | copy-start | bytes 786436
  35.7 6.5 copy-start.1
  41.0 154.1 %all-gather.2.cloned.1.call-start = ((), (), s32[]{:S(2)}) async-start(), calls=%async_computation.2 | async-start | bytes 6389760 | tf_op jit(solution)/shard_map/all_gather | solution.py:57
  47.8 147.3 %copy-start.6 = (s32[384]{0:T(512)S(1)}, s32[384]{0:T(512)}, u32[]{:S(2)}) copy-start(s32[384]{0:T(512)} %param.11) | copy-start | bytes 4612
  50.8 0.7 copy-start.4
  53.8 991.6 %reduce-scatter.2.cloned.1.call-start = ((), (), s32[]{:S(2)}) async-start(), calls=%async_computation.3 | async-start | bytes 12779520 | tf_op jit(solution)/shard_map/reduce_scatter | solution.py:69
  195.1 9.1 copy-start.2
  202.0 2.2 copy-start.3
  210.7 903.6 %all-reduce.10.cloned.1.call-start = ((), (), s32[]{:S(2)}) async-start(), calls=%async_computation.5 | async-start | bytes 4718592 | tf_op jit(solution)/shard_map/psum | solution.py:72
  1049.1 772.7 %all-reduce.8.cloned.1.call-start = ((), (), s32[]{:S(2)}) async-start(), calls=%async_computation.4 | async-start | bytes 4194304 | tf_op jit(solution)/shard_map/psum | solution.py:75
Sparse Core Ops, SparseCore 0:
  41.1 47.6 all-reduce.5
  1049.2 64.9 all-reduce.9
Sparse Core Ops, SparseCore 1:
  53.8 141.2 all-gather.1
  210.8 834.5 reduce-scatter.1
  1118.1 703.6 all-reduce.7
where the time goes:
time: 1830 us
  waiting for transfers between devices  1730 us (95%)
  local copies, waits for them, and re-layouts  39.3 us (2%)
  matrix products  28.8 us (2%)
    reduce_scatter x1, waiting for transfers between devices, per_device(): col_part = lax.psum_scatter(col_acc, 'blk', scatter_dimension=0, tiled=True)  827 us
    psum x1, waiting for transfers between devices, per_device(): grad_dna_proj, grad_meth_proj = lax.psum((dna_term, meth_group), 'blk')  704 us
    all_gather x1, waiting for transfers between devices, per_device(): column_block = lax.all_gather(meth_rows, 'blk', axis=0, tiled=True)  105 us
    psum x1, waiting for transfers between devices, per_device(): row_sum, meth_group = lax.psum((row_acc, meth_term), 'mp')  65.1 us
  transfers between devices with their start and end apart: 5, of which 5 were waited for; matrix products, arithmetic and copies ran while one was open for 1% of the time, Pallas kernels for 0%

commit v1 on v0

v1 whole, which is shorter than its diff:
```python
import jax
import jax.numpy as jnp
from jax import lax
from jax.experimental import pallas as pl
from jax.experimental.pallas import tpu as pltpu
from jax.sharding import PartitionSpec as P

MESH = pl.DeviceIdType.MESH
F32 = jnp.float32
BF16 = jnp.bfloat16
EPS = 1e-06

PAIR_DEV = 384
ROWS = 2 * PAIR_DEV
COLS = 8 * PAIR_DEV
E = 512
D_SLICE = 256
D_METH = 768
VOCAB_DNA = 4096
VOCAB_METH = 512
CHUNK = 512
M_HALF = 384
N_COPIES = 64

NT = (((1,), (1,)), ((), ()))


def place():
    blk, mp = lax.axis_index("blk"), lax.axis_index("mp")
    z = lax.div(blk, 8)
    y = lax.rem(lax.div(blk, 2), 4)
    x = lax.rem(blk, 2) * 2 + lax.div(mp, 2)
    return blk, mp, z, y, x, lax.rem(mp, 2)


def device_at(z, y, x, core):
    return (z * 8 + y * 2 + lax.div(x, 2), lax.rem(x, 2) * 2 + core)


def signal(device):
    pl.semaphore_signal(
        pltpu.get_barrier_semaphore(), inc=1, device_id=device, device_id_type=MESH
    )


def send(src, dst, send_sem, recv_sem, device):
    return pltpu.make_async_remote_copy(
        src_ref=src,
        dst_ref=dst,
        send_sem=send_sem,
        recv_sem=recv_sem,
        device_id=device,
        device_id_type=MESH,
    )


def step_kernel(
    dna_ids,
    meth_ids,
    pairs,
    dna_table_hbm,
    meth_table_hbm,
    dna_proj,
    meth_proj_hbm,
    scale_ref,
    bias_ref,
    d_out,
    m_out,
    dna_table,
    meth_table,
    meth_proj,
    dna_tokens,
    counts,
    ids_all,
    pair_all,
    pair_wide,
    dna_pooled,
    dna_projt,
    meth_tablet,
    meth_projt,
    meth_counts,
    meth_pooled,
    meth_unit,
    meth_rows,
    meth_inv,
    dna_unit,
    dna_inv,
    dna_rowst,
    dna_rows,
    row_acc,
    m_acc,
    m_sib,
    m_first,
    m_first_in,
    m_second,
    m_second_in,
    back_all,
    back_sib,
    back_half,
    back_in,
    d_first,
    d_first_in,
    third,
    third_in,
    third_all,
    m_all,
    d_slab,
    d_fin,
    ids_send,
    ids_recv,
    send_sems,
    recv_sems,
    local_sems,
):
    blk, mp, z, y, x, core = place()
    x_hi = lax.div(x, 2)
    sibling = device_at(z, y, x, 1 - core)
    ring = [device_at(z, y, lax.rem(x + o, 4), core) for o in range(4)]
    cross = [device_at(z, y, lax.rem(x + o, 4), 1 - core) for o in range(4)]
    along_y = [device_at(z, lax.rem(y + o, 4), x, core) for o in range(4)]
    along_z = [device_at(lax.rem(z + o, 8), y, x, core) for o in range(8)]
    slot = lax.rem(blk, 8)
    block = x_hi * 4 + mp
    taken = []

    def post(src, dst, device):
        n = len(taken)
        copy = send(src, dst, send_sems.at[n], recv_sems.at[n], device)
        taken.append(copy)
        return copy

    fetch = [
        pltpu.make_async_copy(src, dst, local_sems.at[1 + n])
        for n, (src, dst) in enumerate(
            ((dna_table_hbm, dna_table), (meth_table_hbm, meth_table), (meth_proj_hbm, meth_proj))
        )
    ]
    for copy in fetch:
        copy.start()

    targets = [device_at(s, mp, lax.div(z, 2), lax.rem(z, 2)) for s in range(8)]
    sources = [device_at(block, s // 2, (s % 2) * 2 + lax.div(y, 2), lax.rem(y, 2)) for s in range(8)]

    def is_me(device):
        return jnp.logical_and(device[0] == blk, device[1] == mp)

    for s in range(8):

        @pl.when(jnp.logical_not(is_me(sources[s])))
        def _():
            signal(sources[s])

    for o in (1, 2, 3):
        signal(ring[o])
        signal(cross[o])
        signal(along_y[o])
    for o in range(1, 8):
        signal(along_z[o])
    signal(sibling)
    to_self = jnp.logical_and(mp == y, block == z).astype(jnp.int32)
    pl.semaphore_wait(pltpu.get_barrier_semaphore(), 25 - to_self)

    def ids_copy(s):
        lanes = pl.ds(pl.multiple_of(slot * PAIR_DEV, 128), PAIR_DEV)
        return send(meth_ids, ids_all.at[:, lanes], ids_send.at[s], ids_recv.at[slot], targets[s])

    def ids_arrival(s):
        lanes = pl.ds(s * PAIR_DEV, PAIR_DEV)
        return send(meth_ids, ids_all.at[:, lanes], ids_send.at[s], ids_recv.at[s], sources[s])

    for s in range(8):

        @pl.when(jnp.logical_not(is_me(targets[s])))
        def _():
            ids_copy(s).start()

        @pl.when(is_me(targets[s]))
        def _():
            lanes = pl.ds(pl.multiple_of(slot * PAIR_DEV, 128), PAIR_DEV)
            local = pltpu.make_async_copy(meth_ids, ids_all.at[:, lanes], local_sems.at[0])
            local.start()
            local.wait()

    pair_copy = post(pairs, pair_all.at[x_hi], ring[2])
    pair_copy.start()
    pair_all[x_hi] = pairs[...]

    dna_projt[mp] = dna_proj[...].T
    toward = 1 + 2 * core
    far = device_at(z, y, lax.rem(x + toward, 4), core)
    other_mp = lax.rem(mp + 2, 4)
    proj_far = post(dna_projt.at[mp], dna_projt.at[mp], far)
    proj_sib = post(dna_projt.at[mp], dna_projt.at[mp], sibling)
    proj_fwd = post(dna_projt.at[other_mp], dna_projt.at[other_mp], sibling)
    proj_far.start()
    proj_sib.start()

    dna_tokens[...] = dna_ids[...].T

    def count_dna(i, carry):
        rows = pl.ds(pl.multiple_of(i * 16, 16), 16)
        ids = dna_tokens[rows, :]
        place_of = jnp.bitwise_and(ids, VOCAB_DNA // 4 - 1)
        amount = jnp.left_shift(1, jnp.right_shift(ids, 10) * 8)
        lane = lax.broadcasted_iota(jnp.int32, (16, VOCAB_DNA // 4), 1)
        total = jnp.zeros((16, VOCAB_DNA // 4), jnp.int32)
        for t in range(16):
            total = total + jnp.where(lane == place_of[:, t : t + 1], amount[:, t : t + 1], 0)
        for f in range(4):
            field = jnp.bitwise_and(jnp.right_shift(total, 8 * f), 255)
            counts[rows, f * 1024 : (f + 1) * 1024] = field.astype(F32).astype(BF16)
        return carry

    lax.fori_loop(0, PAIR_DEV // 16, count_dna, 0)
    fetch[0].wait()
    pooled = jnp.dot(counts[...], dna_table[...], preferred_element_type=F32) * 0.0625
    own_lanes = pl.ds(pl.multiple_of(x_hi * PAIR_DEV, 128), PAIR_DEV)
    dna_pooled[mp, :, own_lanes] = pooled.T.astype(BF16)

    def pool_block(x_of, core_of):
        lanes = pl.ds(pl.multiple_of(lax.div(x_of, 2) * PAIR_DEV, 128), PAIR_DEV)
        return dna_pooled.at[lax.rem(x_of, 2) * 2 + core_of, :, lanes]

    own = pool_block(x, core)
    pool_far = [post(own, own, ring[o]) for o in (1, 2, 3)]
    pool_sib = post(own, own, sibling)
    for copy in pool_far:
        copy.start()
    pool_sib.start()

    landed = [pool_block(lax.rem(x + 4 - o, 4), core) for o in (1, 2, 3)]
    pool_fwd = [post(part, part, sibling) for part in landed]

    fetch[1].wait()
    fetch[2].wait()
    meth_tablet[...] = meth_table[...].T
    meth_projt[...] = meth_proj[...].T
    for s in range(8):

        @pl.when(jnp.logical_not(is_me(sources[s])))
        def _():
            ids_arrival(s).wait_recv()

    def count_meth(i, carry):
        lanes = pl.ds(pl.multiple_of(i * 128, 128), 128)
        ids = ids_all[:, lanes]
        place_of = jnp.bitwise_and(ids, 127)
        amount = jnp.left_shift(1, jnp.right_shift(ids, 7) * 8)
        row = lax.broadcasted_iota(jnp.int32, (128, 128), 0)
        total = jnp.zeros((128, 128), jnp.int32)
        for t in range(16):
            total = total + jnp.where(row == place_of[t : t + 1, :], amount[t : t + 1, :], 0)
        for f in range(4):
            field = jnp.bitwise_and(jnp.right_shift(total, 8 * f), 255)
            meth_counts[f * 128 : (f + 1) * 128, lanes] = field.astype(F32).astype(BF16)
        return carry

    lax.fori_loop(0, COLS // 128, count_meth, 0)

    def embed_meth(i, carry):
        lanes = pl.ds(pl.multiple_of(i * CHUNK, 128), CHUNK)
        pooled_m = jnp.dot(meth_tablet[...], meth_counts[:, lanes], preferred_element_type=F32)
        pooled_m = (pooled_m * 0.0625).astype(BF16)
        meth_pooled[:, lanes] = pooled_m
        raw = jnp.dot(meth_projt[...], pooled_m, preferred_element_type=F32)
        inverse = lax.rsqrt(jnp.sum(raw * raw, axis=0, keepdims=True) + EPS)
        unit = raw * inverse
        meth_inv[:, lanes] = inverse
        meth_unit[:, lanes] = unit
        meth_rows[:, lanes] = unit.astype(BF16)
        return carry

    half = COLS // CHUNK // 2
    lax.fori_loop(0, half, embed_meth, 0)
    proj_far.wait_recv()
    proj_fwd.start()
    for o in (1, 3):
        pool_far[o - 1].wait_recv()
        pool_fwd[o - 1].start()
    lax.fori_loop(half, 2 * half, embed_meth, 0)
    pool_far[1].wait_recv()
    pool_fwd[1].start()
    proj_sib.wait_recv()
    proj_fwd.wait_recv()
    pair_copy.wait_recv()
    for h in range(2):
        words = pair_all[h]
        for a in range(3):
            wide = jnp.broadcast_to(words[a : a + 1, :], (128, 128))
            first = h * PAIR_DEV + a * 128
            pair_wide[first : first + 128, :] = wide.T
    pool_sib.wait_recv()
    for copy in pool_fwd:
        copy.wait_recv()

    raw = jnp.dot(dna_projt[0], dna_pooled[0], preferred_element_type=F32)
    for s in range(1, 4):
        raw = raw + jnp.dot(dna_projt[s], dna_pooled[s], preferred_element_type=F32)
    inverse = lax.rsqrt(jnp.sum(raw * raw, axis=0, keepdims=True) + EPS)
    unit = raw * inverse
    dna_inv[...] = inverse
    dna_unit[...] = unit
    unit_low = unit.astype(BF16)
    dna_rowst[...] = unit_low
    dna_rows[...] = unit_low.T

    scale = scale_ref[0]
    bias = bias_ref[0]
    row_acc[...] = jnp.zeros_like(row_acc)
    m_acc[...] = jnp.zeros_like(m_out)
    first_col = block * COLS

    def pair_tile(i, carry):
        lanes = pl.ds(pl.multiple_of(i * CHUNK, 128), CHUNK)
        rows_m = meth_rows[:, lanes]
        dots = jnp.dot(dna_rows[...], rows_m, preferred_element_type=F32)
        prob = 1.0 / (1.0 + jnp.exp(-(scale * dots + bias)))
        lane = lax.broadcasted_iota(jnp.int32, (ROWS, 128), 1) + (first_col + i * CHUNK)
        parts = []
        for g in range(CHUNK // 128):
            part = prob[:, g * 128 : (g + 1) * 128]
            hit = pair_wide[...] - g * 128 == lane
            parts.append(jnp.where(hit, part - 1.0, part).astype(BF16))
        tile = jnp.concatenate(parts, axis=1)
        row_acc[...] += lax.dot_general(rows_m, tile, NT, preferred_element_type=F32)
        up = scale * jnp.dot(dna_rowst[...], tile, preferred_element_type=F32)
        unit_m = meth_unit[:, lanes]
        inner = jnp.sum(unit_m * up, axis=0, keepdims=True)
        back = (meth_inv[:, lanes] * (up - unit_m * inner)).astype(BF16)
        m_acc[...] += lax.dot_general(
            meth_pooled[:, lanes], back, NT, preferred_element_type=F32
        )
        return carry

    lax.fori_loop(0, COLS // CHUNK, pair_tile, 0)

    other = 1 - core
    m_swap = post(m_acc.at[pl.ds(pl.multiple_of(other * M_HALF, 8), M_HALF)], m_sib, sibling)
    m_swap.start()

    up = scale * row_acc[...]
    inner = jnp.sum(dna_unit[...] * up, axis=0, keepdims=True)
    back_all[...] = (dna_inv[...] * (up - dna_unit[...] * inner)).astype(BF16)
    back_swap = post(back_all.at[pl.ds(pl.multiple_of(other * 256, 16), 256)], back_sib, sibling)
    back_swap.start()

    swap = core == 1

    def pick(one, two):
        return tuple(jnp.where(swap, q, p) for p, q in zip(one, two))

    axis_a = [pick(p, q) for p, q in zip(ring, along_y)]
    axis_b = [pick(q, p) for p, q in zip(ring, along_y)]
    at_a = jnp.where(swap, y, x)
    at_b = jnp.where(swap, x, y)

    m_swap.wait_recv()
    for a in range(4):
        rows = pl.ds(pl.multiple_of(core * M_HALF + a * 96, 8), 96)
        m_first[a] = m_acc[rows, :] + m_sib[a * 96 : (a + 1) * 96, :]
    m_a = [post(m_first.at[lax.rem(at_a + o, 4)], m_first_in.at[o - 1], axis_a[o]) for o in (1, 2, 3)]
    for copy in m_a:
        copy.start()

    back_swap.wait_recv()
    for a in range(4):
        rows = pl.ds(pl.multiple_of(core * 256 + a * 64, 16), 64)
        both = back_all[rows, :].astype(F32) + back_sib[a * 64 : (a + 1) * 64, :].astype(F32)
        back_half[a] = both.astype(BF16)
    back_x = [post(back_half.at[lax.rem(x + o, 4)], back_in.at[o - 1], ring[o]) for o in (1, 2, 3)]
    for copy in back_x:
        copy.start()
    for copy in back_x:
        copy.wait_recv()
    back = back_half[x].astype(F32)
    for o in range(3):
        back = back + back_in[o].astype(F32)
    back = back.astype(BF16)
    for s in range(4):
        part = lax.dot_general(back, dna_pooled[s], NT, preferred_element_type=F32)
        for a in range(4):
            d_first[a, :, s * D_SLICE : (s + 1) * D_SLICE] = part[a * 16 : (a + 1) * 16, :]
    d_y = [post(d_first.at[lax.rem(y + o, 4)], d_first_in.at[o - 1], along_y[o]) for o in (1, 2, 3)]
    for copy in d_y:
        copy.start()

    for copy in m_a:
        copy.wait_recv()
    for b in range(4):
        part = m_first[at_a, b * 24 : (b + 1) * 24, :]
        for o in range(3):
            part = part + m_first_in[o, b * 24 : (b + 1) * 24, :]
        m_second[b] = part
    m_b = [post(m_second.at[lax.rem(at_b + o, 4)], m_second_in.at[o - 1], axis_b[o]) for o in (1, 2, 3)]
    for copy in m_b:
        copy.start()

    for copy in d_y:
        copy.wait_recv()
    d_sum = d_first[y]
    for o in range(3):
        d_sum = d_sum + d_first_in[o]
    for s in range(8):
        lanes = slice(s * 128, (s + 1) * 128)
        third[s, 8:16, 0:128] = d_sum[0:8, lanes]
        third[s, 8:16, 128:256] = d_sum[8:16, lanes]
    for copy in m_b:
        copy.wait_recv()
    m_sum = m_second[at_b]
    for o in range(3):
        m_sum = m_sum + m_second_in[o]
    for s in range(6):
        third[s, 0:8, :] = m_sum[s // 2 * 8 : s // 2 * 8 + 8, s % 2 * 256 : s % 2 * 256 + 256]
    third[6, 0:8, :] = jnp.zeros((8, 256), F32)
    third[7, 0:8, :] = jnp.zeros((8, 256), F32)

    z_sum = [post(third.at[lax.rem(z + o, 8)], third_in.at[o - 1], along_z[o]) for o in range(1, 8)]
    for copy in z_sum:
        copy.start()
    for copy in z_sum:
        copy.wait_recv()
    total = third[z]
    for o in range(7):
        total = total + third_in[o]
    third_all[z] = total
    z_back = [post(third_all.at[z], third_all.at[z], along_z[o]) for o in range(1, 8)]
    for copy in z_back:
        copy.start()
    for copy in z_back:
        copy.wait_recv()

    for s in range(8):
        lanes = slice(s * 128, (s + 1) * 128)
        d_slab[y, 0:8, lanes] = third_all[s, 8:16, 0:128]
        d_slab[y, 8:16, lanes] = third_all[s, 8:16, 128:256]
    d_back = [post(d_slab.at[y], d_slab.at[y], along_y[o]) for o in (1, 2, 3)]
    for copy in d_back:
        copy.start()
    sub = core * M_HALF + at_a * 96 + at_b * 24
    for s in range(6):
        rows = pl.ds(pl.multiple_of(sub + s // 2 * 8, 8), 8)
        m_all[rows, s % 2 * 256 : s % 2 * 256 + 256] = third_all[s, 0:8, :]
    piece = m_all.at[pl.ds(pl.multiple_of(sub, 8), 24)]
    m_back_b = [post(piece, piece, axis_b[o]) for o in (1, 2, 3)]
    for copy in m_back_b:
        copy.start()
    for copy in m_back_b:
        copy.wait_recv()
    piece = m_all.at[pl.ds(pl.multiple_of(core * M_HALF + at_a * 96, 8), 96)]
    m_back_a = [post(piece, piece, axis_a[o]) for o in (1, 2, 3)]
    for copy in m_back_a:
        copy.start()
    for copy in d_back:
        copy.wait_recv()

    eighth = core * 4 + x

    def slice_for(device):
        return d_slab.at[:, :, pl.ds(pl.multiple_of(device[1] * D_SLICE, 128), D_SLICE)]

    d_ring = [post(slice_for(device), d_fin.at[eighth], device) for device in ring[1:] + cross[1:] + [sibling]]
    for copy in d_ring:
        copy.start()
    own_lanes = pl.ds(pl.multiple_of(mp * D_SLICE, 128), D_SLICE)
    d_fin[eighth] = d_slab[:, :, own_lanes]
    for copy in m_back_a:
        copy.wait_recv()
    half = m_all.at[pl.ds(pl.multiple_of(core * M_HALF, 8), M_HALF)]
    m_last = post(half, half, sibling)
    m_last.start()
    for copy in d_ring:
        copy.wait_recv()
    for s in range(4):
        pair = jnp.concatenate([d_fin[2 * s].reshape(64, D_SLICE), d_fin[2 * s + 1].reshape(64, D_SLICE)], axis=0)
        d_out[:, s * 128 : (s + 1) * 128] = pair.T
    m_last.wait_recv()
    m_out[...] = m_all[...]

    for s in range(8):

        @pl.when(jnp.logical_not(is_me(targets[s])))
        def _():
            ids_copy(s).wait_send()

    for copy in taken:
        copy.wait_send()


def step_call(*args):
    vmem = pl.BlockSpec(memory_space=pltpu.VMEM)
    smem = pl.BlockSpec(memory_space=pltpu.SMEM)
    hbm = pl.BlockSpec(memory_space=pl.ANY)
    dma = pltpu.SemaphoreType.DMA
    f32 = lambda *shape: pltpu.VMEM(shape, F32)
    bf16 = lambda *shape: pltpu.VMEM(shape, BF16)
    i32 = lambda *shape: pltpu.VMEM(shape, jnp.int32)
    return pl.pallas_call(
        step_kernel,
        out_shape=(
            jax.ShapeDtypeStruct((D_SLICE, E), F32),
            jax.ShapeDtypeStruct((D_METH, E), F32),
        ),
        in_specs=[vmem, vmem, vmem, hbm, hbm, vmem, hbm, smem, smem],
        out_specs=(vmem, vmem),
        scratch_shapes=[
            bf16(VOCAB_DNA, D_SLICE),
            bf16(VOCAB_METH, D_METH),
            bf16(D_METH, E),
            i32(PAIR_DEV, 16),
            bf16(PAIR_DEV, VOCAB_DNA),
            i32(16, COLS),
            i32(2, 3, 128),
            i32(ROWS, 128),
            bf16(4, D_SLICE, ROWS),
            bf16(4, E, D_SLICE),
            bf16(D_METH, VOCAB_METH),
            bf16(E, D_METH),
            bf16(VOCAB_METH, COLS),
            bf16(D_METH, COLS),
            f32(E, COLS),
            bf16(E, COLS),
            f32(1, COLS),
            f32(E, ROWS),
            f32(1, ROWS),
            bf16(E, ROWS),
            bf16(ROWS, E),
            f32(E, ROWS),
            f32(D_METH, E),
            f32(M_HALF, E),
            f32(4, 96, E),
            f32(3, 96, E),
            f32(4, 24, E),
            f32(3, 24, E),
            bf16(E, ROWS),
            bf16(256, ROWS),
            bf16(4, 64, ROWS),
            bf16(3, 64, ROWS),
            f32(4, 16, 4 * D_SLICE),
            f32(3, 16, 4 * D_SLICE),
            f32(8, 16, 256),
            f32(7, 16, 256),
            f32(8, 16, 256),
            f32(D_METH, E),
            f32(4, 16, 4 * D_SLICE),
            f32(8, 4, 16, D_SLICE),
            dma((8,)),
            dma((8,)),
            dma((N_COPIES,)),
            dma((N_COPIES,)),
            dma((4,)),
        ],
        compiler_params=pltpu.CompilerParams(
            collective_id=0, has_side_effects=True, vmem_limit_bytes=56 * 1024 * 1024
        ),
        cost_estimate=pl.CostEstimate(flops=19 * 10**9, bytes_accessed=8 * 10**6, transcendentals=5 * 10**6),
        name="contrastive_step",
    )(*args)


def per_device(
    dna_ids,
    meth_ids,
    pair_index,
    dna_table,
    meth_table,
    dna_proj,
    meth_proj,
    logit_scale,
    logit_bias,
):
    return step_call(
        dna_ids.T,
        meth_ids.T,
        pair_index.reshape(3, 128),
        dna_table,
        meth_table,
        dna_proj,
        meth_proj,
        logit_scale,
        logit_bias,
    )


def solution(mesh):
    placed = (
        P("blk", None),
        P("blk", None),
        P("blk"),
        P(None, "mp"),
        P(),
        P("mp", None),
        P(),
        P(),
        P(),
    )
    return jax.shard_map(
        per_device, mesh=mesh, in_specs=placed, out_specs=(P("mp", None), P()), check_vma=False
    )
```

time: 1830 us -> 107 us (0.06)
  the two profiles are of different devices: /device:TPU:8 before, /device:TPU:1 now
where the time goes in v1:
time: 107 us
  Pallas kernels  100 us (93%)
  local copies, waits for them, and re-layouts  4.54 us (4%)
  between operations  1.93 us (2%)
    pallas_call x1, Pallas kernels, step_call(): pl.pallas_call(step_kernel, out_shape=(jax.ShapeDtypeStruct((D_SLICE, E),...  100 us
    unnamed x2, local copies, waits for them, and re-layouts  4.54 us

profile of v1, /device:TPU:1, one launch (start us, length us, event | category | flops | bytes accessed | tf_op | source)
XLA Modules:
  0.0 106.8 jit_solution(15186281855425244039)
XLA Ops:
  1.9 100.4 %contrastive_step.1 = (f32[256,512]{1,0:T(8,128)}, f32[768,512]{1,0:T(8,128)}) custom-call(s32[16,384]{1,0:T(8,128)} %bitcast.3, s32[16,384]{1,0:T(8,128)} %bitcast.4, s32[3,128]{1,0:T(4,128)} %bitcast.5, bf16[4096,256]{1,0:T(8,128)(2,1)} %dna_table_hbm.1, bf16[512,768]{1,0:T(8,128)(2,1)} %meth_table_hbm.1, bf16[256,512]{1,0:T(8,128)(2,1)} %dna_proj.1, ...), custom_call_target="tpu_custom_call" | custom-call | flops 19000000512 | bytes 8000000 | tf_op jit(solution)/shard_map/contrastive_step/pallas_call | solution.py:497
  102.3 1.9 %copy.15 = f32[256,512]{1,0:T(8,128)} copy(f32[256,512]{1,0:T(8,128)} %get-tuple-element.4) | data formatting | bytes 1048576
  104.2 2.7 %copy.16 = f32[768,512]{1,0:T(8,128)} copy(f32[768,512]{1,0:T(8,128)} %get-tuple-element.5) | data formatting | bytes 3145728

commit v2 on v1

--- a/solution.py
+++ b/solution.py
@@ -18,7 +18,9 @@
 D_METH = 768
 VOCAB_DNA = 4096
 VOCAB_METH = 512
-CHUNK = 512
+CHUNK = 768
+PART = 256
+LOG2E = 1.4426950408889634
 M_HALF = 384
 N_COPIES = 64
 
@@ -78,7 +80,6 @@
     dna_projt,
     meth_tablet,
     meth_projt,
-    meth_counts,
     meth_pooled,
     meth_unit,
     meth_rows,
@@ -88,6 +89,7 @@
     dna_rowst,
     dna_rows,
     row_acc,
+    tiles,
     m_acc,
     m_sib,
     m_first,
@@ -222,14 +224,21 @@
         return dna_pooled.at[lax.rem(x_of, 2) * 2 + core_of, :, lanes]
 
     own = pool_block(x, core)
-    pool_far = [post(own, own, ring[o]) for o in (1, 2, 3)]
+    def rows_of(part, h):
+        return part.at[h * 128 : (h + 1) * 128]
+
+    from_left = pool_block(lax.rem(x + 3, 4), core)
+    from_right = pool_block(lax.rem(x + 1, 4), core)
+    from_across = pool_block(lax.rem(x + 2, 4), core)
+    pool_right = post(own, own, ring[1])
+    pool_left = post(own, own, ring[3])
     pool_sib = post(own, own, sibling)
-    for copy in pool_far:
-        copy.start()
+    pool_right.start()
+    pool_left.start()
     pool_sib.start()
-
-    landed = [pool_block(lax.rem(x + 4 - o, 4), core) for o in (1, 2, 3)]
-    pool_fwd = [post(part, part, sibling) for part in landed]
+    relay_right = post(rows_of(from_left, 0), rows_of(from_left, 0), ring[1])
+    relay_left = post(rows_of(from_right, 1), rows_of(from_right, 1), ring[3])
+    pool_fwd = [post(part, part, sibling) for part in (from_left, from_right, from_across)]
 
     fetch[1].wait()
     fetch[2].wait()
@@ -241,45 +250,47 @@
         def _():
             ids_arrival(s).wait_recv()
 
-    def count_meth(i, carry):
-        lanes = pl.ds(pl.multiple_of(i * 128, 128), 128)
-        ids = ids_all[:, lanes]
+    def count_meth(ids):
         place_of = jnp.bitwise_and(ids, 127)
         amount = jnp.left_shift(1, jnp.right_shift(ids, 7) * 8)
         row = lax.broadcasted_iota(jnp.int32, (128, 128), 0)
         total = jnp.zeros((128, 128), jnp.int32)
         for t in range(16):
             total = total + jnp.where(row == place_of[t : t + 1, :], amount[t : t + 1, :], 0)
-        for f in range(4):
-            field = jnp.bitwise_and(jnp.right_shift(total, 8 * f), 255)
-            meth_counts[f * 128 : (f + 1) * 128, lanes] = field.astype(F32).astype(BF16)
-        return carry
-
-    lax.fori_loop(0, COLS // 128, count_meth, 0)
+        fields = [jnp.bitwise_and(jnp.right_shift(total, 8 * f), 255) for f in range(4)]
+        return jnp.concatenate([field.astype(F32).astype(BF16) for field in fields], axis=0)
 
     def embed_meth(i, carry):
-        lanes = pl.ds(pl.multiple_of(i * CHUNK, 128), CHUNK)
-        pooled_m = jnp.dot(meth_tablet[...], meth_counts[:, lanes], preferred_element_type=F32)
-        pooled_m = (pooled_m * 0.0625).astype(BF16)
-        meth_pooled[:, lanes] = pooled_m
-        raw = jnp.dot(meth_projt[...], pooled_m, preferred_element_type=F32)
-        inverse = lax.rsqrt(jnp.sum(raw * raw, axis=0, keepdims=True) + EPS)
-        unit = raw * inverse
-        meth_inv[:, lanes] = inverse
-        meth_unit[:, lanes] = unit
-        meth_rows[:, lanes] = unit.astype(BF16)
+        for p in range(CHUNK // PART):
+            first = pl.multiple_of(i * CHUNK + p * PART, 128)
+            lanes = pl.ds(first, PART)
+            ids = [ids_all[:, pl.ds(pl.multiple_of(first + 128 * g, 128), 128)] for g in range(PART // 128)]
+            tokens = jnp.concatenate([count_meth(part) for part in ids], axis=1)
+            pooled_m = jnp.dot(meth_tablet[...], tokens, preferred_element_type=F32)
+            pooled_m = (pooled_m * 0.0625).astype(BF16)
+            meth_pooled[:, lanes] = pooled_m
+            raw = jnp.dot(meth_projt[...], pooled_m, preferred_element_type=F32)
+            inverse = lax.rsqrt(jnp.sum(raw * raw, axis=0, keepdims=True) + EPS)
+            unit = raw * inverse
+            meth_inv[:, lanes] = inverse
+            meth_unit[:, lanes] = unit
+            meth_rows[:, lanes] = unit.astype(BF16)
         return carry
 
     half = COLS // CHUNK // 2
     lax.fori_loop(0, half, embed_meth, 0)
+    pool_right.wait_recv()
+    relay_right.start()
+    pool_left.wait_recv()
+    relay_left.start()
+    pool_fwd[0].start()
+    pool_fwd[1].start()
     proj_far.wait_recv()
     proj_fwd.start()
-    for o in (1, 3):
-        pool_far[o - 1].wait_recv()
-        pool_fwd[o - 1].start()
     lax.fori_loop(half, 2 * half, embed_meth, 0)
-    pool_far[1].wait_recv()
-    pool_fwd[1].start()
+    relay_right.wait_recv()
+    relay_left.wait_recv()
+    pool_fwd[2].start()
     proj_sib.wait_recv()
     proj_fwd.wait_recv()
     pair_copy.wait_recv()
@@ -307,61 +318,55 @@
     scale = scale_ref[0]
     bias = bias_ref[0]
     row_acc[...] = jnp.zeros_like(row_acc)
-    m_acc[...] = jnp.zeros_like(m_out)
+    m_acc[...] = jnp.zeros_like(m_acc)
+    slope, offset = scale * -LOG2E, bias * -LOG2E
     first_col = block * COLS
 
     def pair_tile(i, carry):
-        lanes = pl.ds(pl.multiple_of(i * CHUNK, 128), CHUNK)
-        rows_m = meth_rows[:, lanes]
-        dots = jnp.dot(dna_rows[...], rows_m, preferred_element_type=F32)
-        prob = 1.0 / (1.0 + jnp.exp(-(scale * dots + bias)))
-        lane = lax.broadcasted_iota(jnp.int32, (ROWS, 128), 1) + (first_col + i * CHUNK)
+        first = pl.multiple_of(i * CHUNK, 128)
+        partner = pair_wide[...] - (first_col + first)
         parts = []
-        for g in range(CHUNK // 128):
-            part = prob[:, g * 128 : (g + 1) * 128]
-            hit = pair_wide[...] - g * 128 == lane
-            parts.append(jnp.where(hit, part - 1.0, part).astype(BF16))
+        for p in range(CHUNK // PART):
+            rows_m = meth_rows[:, pl.ds(pl.multiple_of(first + p * PART, 128), PART)]
+            dots = jnp.dot(dna_rows[...], rows_m, preferred_element_type=F32)
+            lower = 1.0 + jnp.exp2(slope * dots + offset)
+            prob = pl.reciprocal(lower, approx=True)
+            prob = prob * (2.0 - lower * prob)
+            for g in range(PART // 128):
+                part = prob[:, g * 128 : (g + 1) * 128]
+                lane = lax.broadcasted_iota(jnp.int32, (ROWS, 128), 1) + (p * PART + g * 128)
+                parts.append(jnp.where(partner == lane, part - 1.0, part).astype(BF16))
         tile = jnp.concatenate(parts, axis=1)
-        row_acc[...] += lax.dot_general(rows_m, tile, NT, preferred_element_type=F32)
-        up = scale * jnp.dot(dna_rowst[...], tile, preferred_element_type=F32)
-        unit_m = meth_unit[:, lanes]
-        inner = jnp.sum(unit_m * up, axis=0, keepdims=True)
-        back = (meth_inv[:, lanes] * (up - unit_m * inner)).astype(BF16)
-        m_acc[...] += lax.dot_general(
-            meth_pooled[:, lanes], back, NT, preferred_element_type=F32
-        )
+        lanes = pl.ds(first, CHUNK)
+        tiles[:, lanes] = tile
+        row_acc[...] += lax.dot_general(meth_rows[:, lanes], tile, NT, preferred_element_type=F32)
         return carry
 
     lax.fori_loop(0, COLS // CHUNK, pair_tile, 0)
 
     other = 1 - core
-    m_swap = post(m_acc.at[pl.ds(pl.multiple_of(other * M_HALF, 8), M_HALF)], m_sib, sibling)
-    m_swap.start()
-
     up = scale * row_acc[...]
     inner = jnp.sum(dna_unit[...] * up, axis=0, keepdims=True)
     back_all[...] = (dna_inv[...] * (up - dna_unit[...] * inner)).astype(BF16)
     back_swap = post(back_all.at[pl.ds(pl.multiple_of(other * 256, 16), 256)], back_sib, sibling)
     back_swap.start()
 
-    swap = core == 1
-
-    def pick(one, two):
-        return tuple(jnp.where(swap, q, p) for p, q in zip(one, two))
-
-    axis_a = [pick(p, q) for p, q in zip(ring, along_y)]
-    axis_b = [pick(q, p) for p, q in zip(ring, along_y)]
-    at_a = jnp.where(swap, y, x)
-    at_b = jnp.where(swap, x, y)
-
-    m_swap.wait_recv()
-    for a in range(4):
-        rows = pl.ds(pl.multiple_of(core * M_HALF + a * 96, 8), 96)
-        m_first[a] = m_acc[rows, :] + m_sib[a * 96 : (a + 1) * 96, :]
-    m_a = [post(m_first.at[lax.rem(at_a + o, 4)], m_first_in.at[o - 1], axis_a[o]) for o in (1, 2, 3)]
-    for copy in m_a:
-        copy.start()
-
+    def col_tile(i, carry):
+        first = pl.multiple_of(i * CHUNK, 128)
+        parts = []
+        for p in range(CHUNK // PART):
+            lanes = pl.ds(pl.multiple_of(first + p * PART, 128), PART)
+            up = scale * jnp.dot(dna_rowst[...], tiles[:, lanes], preferred_element_type=F32)
+            unit_m = meth_unit[:, lanes]
+            inner = jnp.sum(unit_m * up, axis=0, keepdims=True)
+            parts.append((meth_inv[:, lanes] * (up - unit_m * inner)).astype(BF16))
+        back = jnp.concatenate(parts, axis=1)
+        m_acc[...] += lax.dot_general(
+            meth_pooled[:, pl.ds(first, CHUNK)], back, NT, preferred_element_type=F32
+        )
+        return carry
+
+    lax.fori_loop(0, half, col_tile, 0)
     back_swap.wait_recv()
     for a in range(4):
         rows = pl.ds(pl.multiple_of(core * 256 + a * 64, 16), 64)
@@ -370,6 +375,35 @@
     back_x = [post(back_half.at[lax.rem(x + o, 4)], back_in.at[o - 1], ring[o]) for o in (1, 2, 3)]
     for copy in back_x:
         copy.start()
+    lax.fori_loop(half, 2 * half, col_tile, 0)
+
+    m_swap = post(m_acc.at[pl.ds(pl.multiple_of(other * M_HALF, 8), M_HALF)], m_sib, sibling)
+    m_swap.start()
+
+    swap = core == 1
+
+    def pick(one, two):
+        return tuple(jnp.where(swap, q, p) for p, q in zip(one, two))
+
+    axis_a = [pick(p, q) for p, q in zip(ring, along_y)]
+    axis_b = [pick(q, p) for p, q in zip(ring, along_y)]
+    at_a = jnp.where(swap, y, x)
+    at_b = jnp.where(swap, x, y)
+
+    m_swap.wait_recv()
+
+    def halve(i, carry):
+        a, b = lax.div(i, 4), lax.rem(i, 4)
+        row = jnp.where(swap, a * 96 + b * 24, b * 96 + a * 24)
+        mine = m_acc[pl.ds(pl.multiple_of(core * M_HALF + row, 8), 24), :]
+        m_first[a, b] = mine + m_sib[pl.ds(pl.multiple_of(row, 8), 24), :]
+        return carry
+
+    lax.fori_loop(0, 16, halve, 0)
+    m_a = [post(m_first.at[lax.rem(at_a + o, 4)], m_first_in.at[o - 1], axis_a[o]) for o in (1, 2, 3)]
+    for copy in m_a:
+        copy.start()
+
     for copy in back_x:
         copy.wait_recv()
     back = back_half[x].astype(F32)
@@ -387,9 +421,9 @@
     for copy in m_a:
         copy.wait_recv()
     for b in range(4):
-        part = m_first[at_a, b * 24 : (b + 1) * 24, :]
+        part = m_first[at_a, b]
         for o in range(3):
-            part = part + m_first_in[o, b * 24 : (b + 1) * 24, :]
+            part = part + m_first_in[o, b]
         m_second[b] = part
     m_b = [post(m_second.at[lax.rem(at_b + o, 4)], m_second_in.at[o - 1], axis_b[o]) for o in (1, 2, 3)]
     for copy in m_b:
@@ -436,23 +470,33 @@
     d_back = [post(d_slab.at[y], d_slab.at[y], along_y[o]) for o in (1, 2, 3)]
     for copy in d_back:
         copy.start()
-    sub = core * M_HALF + at_a * 96 + at_b * 24
+    sub = core * M_HALF + y * 96 + x * 24
     for s in range(6):
         rows = pl.ds(pl.multiple_of(sub + s // 2 * 8, 8), 8)
         m_all[rows, s % 2 * 256 : s % 2 * 256 + 256] = third_all[s, 0:8, :]
     piece = m_all.at[pl.ds(pl.multiple_of(sub, 8), 24)]
-    m_back_b = [post(piece, piece, axis_b[o]) for o in (1, 2, 3)]
-    for copy in m_back_b:
-        copy.start()
-    for copy in m_back_b:
-        copy.wait_recv()
-    piece = m_all.at[pl.ds(pl.multiple_of(core * M_HALF + at_a * 96, 8), 96)]
-    m_back_a = [post(piece, piece, axis_a[o]) for o in (1, 2, 3)]
-    for copy in m_back_a:
-        copy.start()
+    m_back_x = [post(piece, piece, ring[o]) for o in (1, 2, 3)]
+    for copy in m_back_x:
+        copy.start()
+
+    def band(y_of, low, rows):
+        first = core * M_HALF + lax.rem(y_of, 4) * 96 + low
+        return m_all.at[pl.ds(pl.multiple_of(first, 8), rows)]
+
+    def to(part, device):
+        copy = post(part, part, device)
+        copy.start()
+        return copy
+
+    for copy in m_back_x:
+        copy.wait_recv()
+    own_band = band(y, 0, 96)
+    up_copy = to(own_band, along_y[1])
+    down_copy = to(own_band, along_y[3])
+    m_last = [to(own_band, sibling)]
+
     for copy in d_back:
         copy.wait_recv()
-
     eighth = core * 4 + x
 
     def slice_for(device):
@@ -463,17 +507,24 @@
         copy.start()
     own_lanes = pl.ds(pl.multiple_of(mp * D_SLICE, 128), D_SLICE)
     d_fin[eighth] = d_slab[:, :, own_lanes]
-    for copy in m_back_a:
-        copy.wait_recv()
-    half = m_all.at[pl.ds(pl.multiple_of(core * M_HALF, 8), M_HALF)]
-    m_last = post(half, half, sibling)
-    m_last.start()
+
+    up_copy.wait_recv()
+    relay_up = to(band(y + 3, 0, 48), along_y[1])
+    m_last.append(to(band(y + 3, 0, 96), sibling))
+    down_copy.wait_recv()
+    relay_down = to(band(y + 1, 48, 48), along_y[3])
+    m_last.append(to(band(y + 1, 0, 96), sibling))
+
     for copy in d_ring:
         copy.wait_recv()
     for s in range(4):
         pair = jnp.concatenate([d_fin[2 * s].reshape(64, D_SLICE), d_fin[2 * s + 1].reshape(64, D_SLICE)], axis=0)
         d_out[:, s * 128 : (s + 1) * 128] = pair.T
-    m_last.wait_recv()
+    relay_up.wait_recv()
+    relay_down.wait_recv()
+    m_last.append(to(band(y + 2, 0, 96), sibling))
+    for copy in m_last:
+        copy.wait_recv()
     m_out[...] = m_all[...]
 
     for s in range(8):
@@ -515,7 +566,6 @@
             bf16(4, E, D_SLICE),
             bf16(D_METH, VOCAB_METH),
             bf16(E, D_METH),
-            bf16(VOCAB_METH, COLS),
             bf16(D_METH, COLS),
             f32(E, COLS),
             bf16(E, COLS),
@@ -525,10 +575,11 @@
             bf16(E, ROWS),
             bf16(ROWS, E),
             f32(E, ROWS),
+            bf16(ROWS, COLS),
             f32(D_METH, E),
             f32(M_HALF, E),
-            f32(4, 96, E),
-            f32(3, 96, E),
+            f32(4, 4, 24, E),
+            f32(3, 4, 24, E),
             f32(4, 24, E),
             f32(3, 24, E),
             bf16(E, ROWS),

time: 107 us -> 101 us (0.944)
  Pallas kernels: 100 us -> 94.4 us
    pallas_call x1, Pallas kernels: 100 us -> 94.4 us  [step_call(): pl.pallas_call(step_kernel, out_shape=(jax.ShapeDtypeStruct((D_SLICE, E),...]
where the time goes in v2:
time: 101 us
  Pallas kernels  94.4 us (93%)
  local copies, waits for them, and re-layouts  4.54 us (4%)
  between operations  1.93 us (2%)
    pallas_call x1, Pallas kernels, step_call(): pl.pallas_call(step_kernel, out_shape=(jax.ShapeDtypeStruct((D_SLICE, E),...  94.4 us
    unnamed x2, local copies, waits for them, and re-layouts  4.54 us

profile of v2, /device:TPU:1, one launch (start us, length us, event | category | flops | bytes accessed | tf_op | source)
XLA Modules:
  0.0 100.9 jit_solution(7950982420426759658)
XLA Ops:
  1.9 94.4 %contrastive_step.1 = (f32[256,512]{1,0:T(8,128)}, f32[768,512]{1,0:T(8,128)}) custom-call(s32[16,384]{1,0:T(8,128)} %bitcast.3, s32[16,384]{1,0:T(8,128)} %bitcast.4, s32[3,128]{1,0:T(4,128)} %bitcast.5, bf16[4096,256]{1,0:T(8,128)(2,1)} %dna_table_hbm.1, bf16[512,768]{1,0:T(8,128)(2,1)} %meth_table_hbm.1, bf16[256,512]{1,0:T(8,128)(2,1)} %dna_proj.1, ...), custom_call_target="tpu_custom_call" | custom-call | flops 19000000512 | bytes 8000000 | tf_op jit(solution)/shard_map/contrastive_step/pallas_call | solution.py:548
  96.3 1.9 %copy.15 = f32[256,512]{1,0:T(8,128)} copy(f32[256,512]{1,0:T(8,128)} %get-tuple-element.4) | data formatting | bytes 1048576
  98.2 2.7 %copy.16 = f32[768,512]{1,0:T(8,128)} copy(f32[768,512]{1,0:T(8,128)} %get-tuple-element.5) | data formatting | bytes 3145728

commit v3 on v2

--- a/solution.py
+++ b/solution.py
@@ -90,6 +90,7 @@
     dna_rows,
     row_acc,
     tiles,
+    meth_back,
     m_acc,
     m_sib,
     m_first,
@@ -187,13 +188,17 @@
     pair_copy.start()
     pair_all[x_hi] = pairs[...]
 
-    dna_projt[mp] = dna_proj[...].T
+    dna_projt[:, pl.ds(pl.multiple_of(mp * D_SLICE, 128), D_SLICE)] = dna_proj[...].T
     toward = 1 + 2 * core
     far = device_at(z, y, lax.rem(x + toward, 4), core)
     other_mp = lax.rem(mp + 2, 4)
-    proj_far = post(dna_projt.at[mp], dna_projt.at[mp], far)
-    proj_sib = post(dna_projt.at[mp], dna_projt.at[mp], sibling)
-    proj_fwd = post(dna_projt.at[other_mp], dna_projt.at[other_mp], sibling)
+
+    def quarter(of):
+        return dna_projt.at[:, pl.ds(pl.multiple_of(of * D_SLICE, 128), D_SLICE)]
+
+    proj_far = post(quarter(mp), quarter(mp), far)
+    proj_sib = post(quarter(mp), quarter(mp), sibling)
+    proj_fwd = post(quarter(other_mp), quarter(other_mp), sibling)
     proj_far.start()
     proj_sib.start()
 
@@ -217,16 +222,14 @@
     fetch[0].wait()
     pooled = jnp.dot(counts[...], dna_table[...], preferred_element_type=F32) * 0.0625
     own_lanes = pl.ds(pl.multiple_of(x_hi * PAIR_DEV, 128), PAIR_DEV)
-    dna_pooled[mp, :, own_lanes] = pooled.T.astype(BF16)
-
-    def pool_block(x_of, core_of):
+    dna_pooled[pl.ds(pl.multiple_of(mp * D_SLICE, 16), D_SLICE), own_lanes] = pooled.T.astype(BF16)
+
+    def pool_block(x_of, core_of, low=0, count=D_SLICE):
+        first = (lax.rem(x_of, 2) * 2 + core_of) * D_SLICE + low
         lanes = pl.ds(pl.multiple_of(lax.div(x_of, 2) * PAIR_DEV, 128), PAIR_DEV)
-        return dna_pooled.at[lax.rem(x_of, 2) * 2 + core_of, :, lanes]
+        return dna_pooled.at[pl.ds(pl.multiple_of(first, 16), count), lanes]
 
     own = pool_block(x, core)
-    def rows_of(part, h):
-        return part.at[h * 128 : (h + 1) * 128]
-
     from_left = pool_block(lax.rem(x + 3, 4), core)
     from_right = pool_block(lax.rem(x + 1, 4), core)
     from_across = pool_block(lax.rem(x + 2, 4), core)
@@ -236,8 +239,10 @@
     pool_right.start()
     pool_left.start()
     pool_sib.start()
-    relay_right = post(rows_of(from_left, 0), rows_of(from_left, 0), ring[1])
-    relay_left = post(rows_of(from_right, 1), rows_of(from_right, 1), ring[3])
+    half_left = pool_block(lax.rem(x + 3, 4), core, 0, 128)
+    half_right = pool_block(lax.rem(x + 1, 4), core, 128, 128)
+    relay_right = post(half_left, half_left, ring[1])
+    relay_left = post(half_right, half_right, ring[3])
     pool_fwd = [post(part, part, sibling) for part in (from_left, from_right, from_across)]
 
     fetch[1].wait()
@@ -304,9 +309,7 @@
     for copy in pool_fwd:
         copy.wait_recv()
 
-    raw = jnp.dot(dna_projt[0], dna_pooled[0], preferred_element_type=F32)
-    for s in range(1, 4):
-        raw = raw + jnp.dot(dna_projt[s], dna_pooled[s], preferred_element_type=F32)
+    raw = jnp.dot(dna_projt[...], dna_pooled[...], preferred_element_type=F32)
     inverse = lax.rsqrt(jnp.sum(raw * raw, axis=0, keepdims=True) + EPS)
     unit = raw * inverse
     dna_inv[...] = inverse
@@ -317,8 +320,6 @@
 
     scale = scale_ref[0]
     bias = bias_ref[0]
-    row_acc[...] = jnp.zeros_like(row_acc)
-    m_acc[...] = jnp.zeros_like(m_acc)
     slope, offset = scale * -LOG2E, bias * -LOG2E
     first_col = block * COLS
 
@@ -337,12 +338,17 @@
                 lane = lax.broadcasted_iota(jnp.int32, (ROWS, 128), 1) + (p * PART + g * 128)
                 parts.append(jnp.where(partner == lane, part - 1.0, part).astype(BF16))
         tile = jnp.concatenate(parts, axis=1)
-        lanes = pl.ds(first, CHUNK)
-        tiles[:, lanes] = tile
-        row_acc[...] += lax.dot_general(meth_rows[:, lanes], tile, NT, preferred_element_type=F32)
+        tiles[:, pl.ds(first, CHUNK)] = tile
         return carry
 
     lax.fori_loop(0, COLS // CHUNK, pair_tile, 0)
+
+    def row_sums(i, carry):
+        rows = pl.ds(pl.multiple_of(i * PART, 128), PART)
+        row_acc[:, rows] = lax.dot_general(meth_rows[...], tiles[rows, :], NT, preferred_element_type=F32)
+        return carry
+
+    lax.fori_loop(0, ROWS // PART, row_sums, 0)
 
     other = 1 - core
     up = scale * row_acc[...]
@@ -353,17 +359,12 @@
 
     def col_tile(i, carry):
         first = pl.multiple_of(i * CHUNK, 128)
-        parts = []
         for p in range(CHUNK // PART):
             lanes = pl.ds(pl.multiple_of(first + p * PART, 128), PART)
             up = scale * jnp.dot(dna_rowst[...], tiles[:, lanes], preferred_element_type=F32)
             unit_m = meth_unit[:, lanes]
             inner = jnp.sum(unit_m * up, axis=0, keepdims=True)
-            parts.append((meth_inv[:, lanes] * (up - unit_m * inner)).astype(BF16))
-        back = jnp.concatenate(parts, axis=1)
-        m_acc[...] += lax.dot_general(
-            meth_pooled[:, pl.ds(first, CHUNK)], back, NT, preferred_element_type=F32
-        )
+            meth_back[:, lanes] = (meth_inv[:, lanes] * (up - unit_m * inner)).astype(BF16)
         return carry
 
     lax.fori_loop(0, half, col_tile, 0)
@@ -377,6 +378,13 @@
         copy.start()
     lax.fori_loop(half, 2 * half, col_tile, 0)
 
+    def head_tile(i, carry):
+        wide = pl.ds(pl.multiple_of(i * PART, 128), PART)
+        m_acc[:, wide] = lax.dot_general(meth_pooled[...], meth_back[wide, :], NT, preferred_element_type=F32)
+        return carry
+
+    lax.fori_loop(0, E // PART, head_tile, 0)
+
     m_swap = post(m_acc.at[pl.ds(pl.multiple_of(other * M_HALF, 8), M_HALF)], m_sib, sibling)
     m_swap.start()
 
@@ -411,7 +419,8 @@
         back = back + back_in[o].astype(F32)
     back = back.astype(BF16)
     for s in range(4):
-        part = lax.dot_general(back, dna_pooled[s], NT, preferred_element_type=F32)
+        features = dna_pooled[s * D_SLICE : (s + 1) * D_SLICE, :]
+        part = lax.dot_general(back, features, NT, preferred_element_type=F32)
         for a in range(4):
             d_first[a, :, s * D_SLICE : (s + 1) * D_SLICE] = part[a * 16 : (a + 1) * 16, :]
     d_y = [post(d_first.at[lax.rem(y + o, 4)], d_first_in.at[o - 1], along_y[o]) for o in (1, 2, 3)]
@@ -517,9 +526,7 @@
 
     for copy in d_ring:
         copy.wait_recv()
-    for s in range(4):
-        pair = jnp.concatenate([d_fin[2 * s].reshape(64, D_SLICE), d_fin[2 * s + 1].reshape(64, D_SLICE)], axis=0)
-        d_out[:, s * 128 : (s + 1) * 128] = pair.T
+    d_out[...] = d_fin[...].reshape(E, D_SLICE)
     relay_up.wait_recv()
     relay_down.wait_recv()
     m_last.append(to(band(y + 2, 0, 96), sibling))
@@ -548,7 +555,7 @@
     return pl.pallas_call(
         step_kernel,
         out_shape=(
-            jax.ShapeDtypeStruct((D_SLICE, E), F32),
+            jax.ShapeDtypeStruct((E, D_SLICE), F32),
             jax.ShapeDtypeStruct((D_METH, E), F32),
         ),
         in_specs=[vmem, vmem, vmem, hbm, hbm, vmem, hbm, smem, smem],
@@ -562,8 +569,8 @@
             i32(16, COLS),
             i32(2, 3, 128),
             i32(ROWS, 128),
-            bf16(4, D_SLICE, ROWS),
-            bf16(4, E, D_SLICE),
+            bf16(4 * D_SLICE, ROWS),
+            bf16(E, 4 * D_SLICE),
             bf16(D_METH, VOCAB_METH),
             bf16(E, D_METH),
             bf16(D_METH, COLS),
@@ -576,6 +583,7 @@
             bf16(ROWS, E),
             f32(E, ROWS),
             bf16(ROWS, COLS),
+            bf16(E, COLS),
             f32(D_METH, E),
             f32(M_HALF, E),
             f32(4, 4, 24, E),
@@ -608,6 +616,27 @@
     )(*args)
 
 
+def hand_over_kernel(d_in, m_in, d_out, m_out):
+    for s in range(E // 128):
+        d_out[:, s * 128 : (s + 1) * 128] = d_in[s * 128 : (s + 1) * 128, :].T
+    m_out[...] = m_in[...]
+
+
+def hand_over(d_part, m_part):
+    vmem = pl.BlockSpec(memory_space=pltpu.VMEM)
+    return pl.pallas_call(
+        hand_over_kernel,
+        out_shape=(
+            jax.ShapeDtypeStruct((D_SLICE, E), F32),
+            jax.ShapeDtypeStruct((D_METH, E), F32),
+        ),
+        in_specs=[vmem, vmem],
+        out_specs=(vmem, vmem),
+        compiler_params=pltpu.CompilerParams(vmem_limit_bytes=8 * 1024 * 1024),
+        name="hand_over",
+    )(d_part, m_part)
+
+
 def per_device(
     dna_ids,
     meth_ids,
@@ -619,7 +648,7 @@
     logit_scale,
     logit_bias,
 ):
-    return step_call(
+    d_part, m_part = step_call(
         dna_ids.T,
         meth_ids.T,
         pair_index.reshape(3, 128),
@@ -630,6 +659,7 @@
         logit_scale,
         logit_bias,
     )
+    return hand_over(d_part, m_part)
 
 
 def solution(mesh):

time: 101 us -> 102 us (level)
  Pallas kernels: 94.4 us -> 97 us
  local copies, waits for them, and re-layouts: 4.54 us -> 2.44 us
    pallas_call x1 -> x2, Pallas kernels: 94.4 us -> 97 us  [the longest x1 95.4 us: step_call(): pl.pallas_call(step_kernel, out_shape=(jax.ShapeDtypeStruct((E, D_SLICE),...]
    unnamed x2 -> x4, local copies, waits for them, and re-layouts: 4.54 us -> 2.44 us
where the time goes in v3:
time: 102 us; the launch traced here: 101 us
  Pallas kernels  97 us (95%)
  local copies, waits for them, and re-layouts  2.44 us (2%)
  between operations  1.94 us (2%)
    pallas_call x1, Pallas kernels, step_call(): pl.pallas_call(step_kernel, out_shape=(jax.ShapeDtypeStruct((E, D_SLICE),...  95.4 us
    unnamed x4, local copies, waits for them, and re-layouts  2.44 us

profile of v3, /device:TPU:1, one launch (start us, length us, event | category | flops | bytes accessed | tf_op | source)
XLA Modules:
  0.0 101.4 jit_solution(15544578244144497121)
XLA Ops:
  1.9 95.4 %contrastive_step.1 = (f32[512,256]{1,0:T(8,128)}, f32[768,512]{1,0:T(8,128)}) custom-call(s32[16,384]{1,0:T(8,128)} %bitcast.3, s32[16,384]{1,0:T(8,128)} %bitcast.4, s32[3,128]{1,0:T(4,128)} %bitcast.5, bf16[4096,256]{1,0:T(8,128)(2,1)} %dna_table_hbm.1, bf16[512,768]{1,0:T(8,128)(2,1)} %meth_table_hbm.1, bf16[256,512]{1,0:T(8,128)(2,1)} %dna_proj.1, ...), custom_call_target="tpu_custom_call" | custom-call | flops 19000000512 | bytes 8000000 | tf_op jit(solution)/shard_map/contrastive_step/pallas_call | solution.py:555
  97.4 0.0 copy-start
  97.4 1.4 %copy-done = f32[768,512]{1,0:T(8,128)S(1)} copy-done((f32[768,512]{1,0:T(8,128)S(1)}, f32[768,512]{1,0:T(8,128)}, u32[]{:S(2)}) %copy-start) | copy-done | bytes 1572888
  98.8 0.0 copy-start.1
  98.8 1.0 %copy-done.1 = f32[512,256]{1,0:T(8,128)S(1)} copy-done((f32[512,256]{1,0:T(8,128)S(1)}, f32[512,256]{1,0:T(8,128)}, u32[]{:S(2)}) %copy-start.1) | copy-done | bytes 524312
  99.8 1.6 %hand_over.1 = (f32[256,512]{1,0:T(8,128)}, f32[768,512]{1,0:T(8,128)}) custom-call(f32[512,256]{1,0:T(8,128)S(1)} %copy-done.1, f32[768,512]{1,0:T(8,128)S(1)} %copy-done), custom_call_target="tpu_custom_call" | custom-call | tf_op jit(solution)/shard_map/hand_over/pallas_call | solution.py:627
Async XLA Ops:
  97.4 1.4 %copy-start = (f32[768,512]{1,0:T(8,128)S(1)}, f32[768,512]{1,0:T(8,128)}, u32[]{:S(2)}) copy-start(f32[768,512]{1,0:T(8,128)} %get-tuple-element.5.m_in) | copy-start | bytes 4718596
  98.8 1.0 %copy-start.1 = (f32[512,256]{1,0:T(8,128)S(1)}, f32[512,256]{1,0:T(8,128)}, u32[]{:S(2)}) copy-start(f32[512,256]{1,0:T(8,128)} %get-tuple-element.4.d_in) | copy-start | bytes 1572868

commit v4 on v3

--- a/solution.py
+++ b/solution.py
@@ -18,8 +18,8 @@
 D_METH = 768
 VOCAB_DNA = 4096
 VOCAB_METH = 512
-CHUNK = 768
-PART = 256
+CHUNK = 1536
+PART = 512
 LOG2E = 1.4426950408889634
 M_HALF = 384
 N_COPIES = 64
@@ -343,12 +343,7 @@
 
     lax.fori_loop(0, COLS // CHUNK, pair_tile, 0)
 
-    def row_sums(i, carry):
-        rows = pl.ds(pl.multiple_of(i * PART, 128), PART)
-        row_acc[:, rows] = lax.dot_general(meth_rows[...], tiles[rows, :], NT, preferred_element_type=F32)
-        return carry
-
-    lax.fori_loop(0, ROWS // PART, row_sums, 0)
+    row_acc[...] = lax.dot_general(meth_rows[...], tiles[...], NT, preferred_element_type=F32)
 
     other = 1 - core
     up = scale * row_acc[...]
@@ -378,12 +373,7 @@
         copy.start()
     lax.fori_loop(half, 2 * half, col_tile, 0)
 
-    def head_tile(i, carry):
-        wide = pl.ds(pl.multiple_of(i * PART, 128), PART)
-        m_acc[:, wide] = lax.dot_general(meth_pooled[...], meth_back[wide, :], NT, preferred_element_type=F32)
-        return carry
-
-    lax.fori_loop(0, E // PART, head_tile, 0)
+    m_acc[...] = lax.dot_general(meth_pooled[...], meth_back[...], NT, preferred_element_type=F32)
 
     m_swap = post(m_acc.at[pl.ds(pl.multiple_of(other * M_HALF, 8), M_HALF)], m_sib, sibling)
     m_swap.start()

time: 102 us -> 101 us (level)
  no operation moved by 1% of the time
where the time goes in v4:
time: 101 us
  Pallas kernels  96.2 us (95%)
  local copies, waits for them, and re-layouts  2.44 us (2%)
  between operations  1.94 us (2%)
    pallas_call x1, Pallas kernels, step_call(): pl.pallas_call(step_kernel, out_shape=(jax.ShapeDtypeStruct((E, D_SLICE),...  94.6 us
    unnamed x4, local copies, waits for them, and re-layouts  2.44 us

profile of v4, /device:TPU:1, one launch (start us, length us, event | category | flops | bytes accessed | tf_op | source)
XLA Modules:
  0.0 100.5 jit_solution(18366984065425822471)
XLA Ops:
  1.9 94.6 %contrastive_step.1 = (f32[512,256]{1,0:T(8,128)}, f32[768,512]{1,0:T(8,128)}) custom-call(s32[16,384]{1,0:T(8,128)} %bitcast.3, s32[16,384]{1,0:T(8,128)} %bitcast.4, s32[3,128]{1,0:T(4,128)} %bitcast.5, bf16[4096,256]{1,0:T(8,128)(2,1)} %dna_table_hbm.1, bf16[512,768]{1,0:T(8,128)(2,1)} %meth_table_hbm.1, bf16[256,512]{1,0:T(8,128)(2,1)} %dna_proj.1, ...), custom_call_target="tpu_custom_call" | custom-call | flops 19000000512 | bytes 8000000 | tf_op jit(solution)/shard_map/contrastive_step/pallas_call | solution.py:545
  96.5 0.0 copy-start
  96.5 1.4 %copy-done = f32[768,512]{1,0:T(8,128)S(1)} copy-done((f32[768,512]{1,0:T(8,128)S(1)}, f32[768,512]{1,0:T(8,128)}, u32[]{:S(2)}) %copy-start) | copy-done | bytes 1572888
  97.9 0.0 copy-start.1
  97.9 1.0 %copy-done.1 = f32[512,256]{1,0:T(8,128)S(1)} copy-done((f32[512,256]{1,0:T(8,128)S(1)}, f32[512,256]{1,0:T(8,128)}, u32[]{:S(2)}) %copy-start.1) | copy-done | bytes 524312
  99.0 1.6 %hand_over.1 = (f32[256,512]{1,0:T(8,128)}, f32[768,512]{1,0:T(8,128)}) custom-call(f32[512,256]{1,0:T(8,128)S(1)} %copy-done.1, f32[768,512]{1,0:T(8,128)S(1)} %copy-done), custom_call_target="tpu_custom_call" | custom-call | tf_op jit(solution)/shard_map/hand_over/pallas_call | solution.py:617
Async XLA Ops:
  96.5 1.4 %copy-start = (f32[768,512]{1,0:T(8,128)S(1)}, f32[768,512]{1,0:T(8,128)}, u32[]{:S(2)}) copy-start(f32[768,512]{1,0:T(8,128)} %get-tuple-element.5.m_in) | copy-start | bytes 4718596
  97.9 1.0 %copy-start.1 = (f32[512,256]{1,0:T(8,128)S(1)}, f32[512,256]{1,0:T(8,128)}, u32[]{:S(2)}) copy-start(f32[512,256]{1,0:T(8,128)} %get-tuple-element.4.d_in) | copy-start | bytes 1572868

commit v5 on v4

--- a/solution.py
+++ b/solution.py
@@ -56,23 +56,61 @@
     )
 
 
+def pool_kernel(dna_ids, dna_table, dna_proj, pooled_out, projt_out, dna_tokens, counts):
+    projt_out[...] = dna_proj[...].T
+    dna_tokens[...] = dna_ids[...].T
+
+    def count_dna(i, carry):
+        rows = pl.ds(pl.multiple_of(i * 16, 16), 16)
+        ids = dna_tokens[rows, :]
+        place_of = jnp.bitwise_and(ids, VOCAB_DNA // 4 - 1)
+        amount = jnp.left_shift(1, jnp.right_shift(ids, 10) * 8)
+        lane = lax.broadcasted_iota(jnp.int32, (16, VOCAB_DNA // 4), 1)
+        total = jnp.zeros((16, VOCAB_DNA // 4), jnp.int32)
+        for t in range(16):
+            total = total + jnp.where(lane == place_of[:, t : t + 1], amount[:, t : t + 1], 0)
+        for f in range(4):
+            field = jnp.bitwise_and(jnp.right_shift(total, 8 * f), 255)
+            counts[rows, f * 1024 : (f + 1) * 1024] = field.astype(F32).astype(BF16)
+        return carry
+
+    lax.fori_loop(0, PAIR_DEV // 16, count_dna, 0)
+    pooled = jnp.dot(counts[...], dna_table[...], preferred_element_type=F32) * 0.0625
+    pooled_out[...] = pooled.T.astype(BF16)
+
+
+def pool_call(*args):
+    vmem = pl.BlockSpec(memory_space=pltpu.VMEM)
+    return pl.pallas_call(
+        pool_kernel,
+        out_shape=(
+            jax.ShapeDtypeStruct((D_SLICE, PAIR_DEV), BF16),
+            jax.ShapeDtypeStruct((E, D_SLICE), BF16),
+        ),
+        in_specs=[vmem] * 3,
+        out_specs=(vmem, vmem),
+        scratch_shapes=[
+            pltpu.VMEM((PAIR_DEV, 16), jnp.int32),
+            pltpu.VMEM((PAIR_DEV, VOCAB_DNA), BF16),
+        ],
+        compiler_params=pltpu.CompilerParams(vmem_limit_bytes=16 * 1024 * 1024),
+        name="pool_dna",
+    )(*args)
+
+
 def step_kernel(
-    dna_ids,
+    dna_part,
+    dna_projt_part,
     meth_ids,
     pairs,
-    dna_table_hbm,
     meth_table_hbm,
-    dna_proj,
     meth_proj_hbm,
     scale_ref,
     bias_ref,
-    d_out,
-    m_out,
-    dna_table,
+    d_first,
+    m_acc,
     meth_table,
     meth_proj,
-    dna_tokens,
-    counts,
     ids_all,
     pair_all,
     pair_wide,
@@ -91,24 +129,10 @@
     row_acc,
     tiles,
     meth_back,
-    m_acc,
-    m_sib,
-    m_first,
-    m_first_in,
-    m_second,
-    m_second_in,
     back_all,
     back_sib,
     back_half,
     back_in,
-    d_first,
-    d_first_in,
-    third,
-    third_in,
-    third_all,
-    m_all,
-    d_slab,
-    d_fin,
     ids_send,
     ids_recv,
     send_sems,
@@ -119,9 +143,6 @@
     x_hi = lax.div(x, 2)
     sibling = device_at(z, y, x, 1 - core)
     ring = [device_at(z, y, lax.rem(x + o, 4), core) for o in range(4)]
-    cross = [device_at(z, y, lax.rem(x + o, 4), 1 - core) for o in range(4)]
-    along_y = [device_at(z, lax.rem(y + o, 4), x, core) for o in range(4)]
-    along_z = [device_at(lax.rem(z + o, 8), y, x, core) for o in range(8)]
     slot = lax.rem(blk, 8)
     block = x_hi * 4 + mp
     taken = []
@@ -135,7 +156,7 @@
     fetch = [
         pltpu.make_async_copy(src, dst, local_sems.at[1 + n])
         for n, (src, dst) in enumerate(
-            ((dna_table_hbm, dna_table), (meth_table_hbm, meth_table), (meth_proj_hbm, meth_proj))
+            ((meth_table_hbm, meth_table), (meth_proj_hbm, meth_proj))
         )
     ]
     for copy in fetch:
@@ -155,13 +176,9 @@
 
     for o in (1, 2, 3):
         signal(ring[o])
-        signal(cross[o])
-        signal(along_y[o])
-    for o in range(1, 8):
-        signal(along_z[o])
     signal(sibling)
     to_self = jnp.logical_and(mp == y, block == z).astype(jnp.int32)
-    pl.semaphore_wait(pltpu.get_barrier_semaphore(), 25 - to_self)
+    pl.semaphore_wait(pltpu.get_barrier_semaphore(), 12 - to_self)
 
     def ids_copy(s):
         lanes = pl.ds(pl.multiple_of(slot * PAIR_DEV, 128), PAIR_DEV)
@@ -188,7 +205,7 @@
     pair_copy.start()
     pair_all[x_hi] = pairs[...]
 
-    dna_projt[:, pl.ds(pl.multiple_of(mp * D_SLICE, 128), D_SLICE)] = dna_proj[...].T
+    dna_projt[:, pl.ds(pl.multiple_of(mp * D_SLICE, 128), D_SLICE)] = dna_projt_part[...]
     toward = 1 + 2 * core
     far = device_at(z, y, lax.rem(x + toward, 4), core)
     other_mp = lax.rem(mp + 2, 4)
@@ -202,27 +219,8 @@
     proj_far.start()
     proj_sib.start()
 
-    dna_tokens[...] = dna_ids[...].T
-
-    def count_dna(i, carry):
-        rows = pl.ds(pl.multiple_of(i * 16, 16), 16)
-        ids = dna_tokens[rows, :]
-        place_of = jnp.bitwise_and(ids, VOCAB_DNA // 4 - 1)
-        amount = jnp.left_shift(1, jnp.right_shift(ids, 10) * 8)
-        lane = lax.broadcasted_iota(jnp.int32, (16, VOCAB_DNA // 4), 1)
-        total = jnp.zeros((16, VOCAB_DNA // 4), jnp.int32)
-        for t in range(16):
-            total = total + jnp.where(lane == place_of[:, t : t + 1], amount[:, t : t + 1], 0)
-        for f in range(4):
-            field = jnp.bitwise_and(jnp.right_shift(total, 8 * f), 255)
-            counts[rows, f * 1024 : (f + 1) * 1024] = field.astype(F32).astype(BF16)
-        return carry
-
-    lax.fori_loop(0, PAIR_DEV // 16, count_dna, 0)
-    fetch[0].wait()
-    pooled = jnp.dot(counts[...], dna_table[...], preferred_element_type=F32) * 0.0625
     own_lanes = pl.ds(pl.multiple_of(x_hi * PAIR_DEV, 128), PAIR_DEV)
-    dna_pooled[pl.ds(pl.multiple_of(mp * D_SLICE, 16), D_SLICE), own_lanes] = pooled.T.astype(BF16)
+    dna_pooled[pl.ds(pl.multiple_of(mp * D_SLICE, 16), D_SLICE), own_lanes] = dna_part[...]
 
     def pool_block(x_of, core_of, low=0, count=D_SLICE):
         first = (lax.rem(x_of, 2) * 2 + core_of) * D_SLICE + low
@@ -245,8 +243,8 @@
     relay_left = post(half_right, half_right, ring[3])
     pool_fwd = [post(part, part, sibling) for part in (from_left, from_right, from_across)]
 
+    fetch[0].wait()
     fetch[1].wait()
-    fetch[2].wait()
     meth_tablet[...] = meth_table[...].T
     meth_projt[...] = meth_proj[...].T
     for s in range(8):
@@ -375,33 +373,6 @@
 
     m_acc[...] = lax.dot_general(meth_pooled[...], meth_back[...], NT, preferred_element_type=F32)
 
-    m_swap = post(m_acc.at[pl.ds(pl.multiple_of(other * M_HALF, 8), M_HALF)], m_sib, sibling)
-    m_swap.start()
-
-    swap = core == 1
-
-    def pick(one, two):
-        return tuple(jnp.where(swap, q, p) for p, q in zip(one, two))
-
-    axis_a = [pick(p, q) for p, q in zip(ring, along_y)]
-    axis_b = [pick(q, p) for p, q in zip(ring, along_y)]
-    at_a = jnp.where(swap, y, x)
-    at_b = jnp.where(swap, x, y)
-
-    m_swap.wait_recv()
-
-    def halve(i, carry):
-        a, b = lax.div(i, 4), lax.rem(i, 4)
-        row = jnp.where(swap, a * 96 + b * 24, b * 96 + a * 24)
-        mine = m_acc[pl.ds(pl.multiple_of(core * M_HALF + row, 8), 24), :]
-        m_first[a, b] = mine + m_sib[pl.ds(pl.multiple_of(row, 8), 24), :]
-        return carry
-
-    lax.fori_loop(0, 16, halve, 0)
-    m_a = [post(m_first.at[lax.rem(at_a + o, 4)], m_first_in.at[o - 1], axis_a[o]) for o in (1, 2, 3)]
-    for copy in m_a:
-        copy.start()
-
     for copy in back_x:
         copy.wait_recv()
     back = back_half[x].astype(F32)
@@ -413,8 +384,88 @@
         part = lax.dot_general(back, features, NT, preferred_element_type=F32)
         for a in range(4):
             d_first[a, :, s * D_SLICE : (s + 1) * D_SLICE] = part[a * 16 : (a + 1) * 16, :]
+    for s in range(8):
+
+        @pl.when(jnp.logical_not(is_me(targets[s])))
+        def _():
+            ids_copy(s).wait_send()
+
+    for copy in taken:
+        copy.wait_send()
+
+
+def sum_kernel(
+    d_first,
+    m_acc,
+    d_out,
+    m_all,
+    m_sib,
+    m_first,
+    m_first_in,
+    m_second,
+    m_second_in,
+    d_first_in,
+    third,
+    third_in,
+    third_all,
+    d_slab,
+    d_fin,
+    send_sems,
+    recv_sems,
+):
+    blk, mp, z, y, x, core = place()
+    sibling = device_at(z, y, x, 1 - core)
+    ring = [device_at(z, y, lax.rem(x + o, 4), core) for o in range(4)]
+    cross = [device_at(z, y, lax.rem(x + o, 4), 1 - core) for o in range(4)]
+    along_y = [device_at(z, lax.rem(y + o, 4), x, core) for o in range(4)]
+    along_z = [device_at(lax.rem(z + o, 8), y, x, core) for o in range(8)]
+    other = 1 - core
+    taken = []
+
+    def post(src, dst, device):
+        n = len(taken)
+        copy = send(src, dst, send_sems.at[n], recv_sems.at[n], device)
+        taken.append(copy)
+        return copy
+
+    for o in (1, 2, 3):
+        signal(ring[o])
+        signal(cross[o])
+        signal(along_y[o])
+    for o in range(1, 8):
+        signal(along_z[o])
+    signal(sibling)
+    pl.semaphore_wait(pltpu.get_barrier_semaphore(), 17)
+
+    m_swap = post(m_acc.at[pl.ds(pl.multiple_of(other * M_HALF, 8), M_HALF)], m_sib, sibling)
+    m_swap.start()
     d_y = [post(d_first.at[lax.rem(y + o, 4)], d_first_in.at[o - 1], along_y[o]) for o in (1, 2, 3)]
     for copy in d_y:
+        copy.start()
+
+
+    swap = core == 1
+
+    def pick(one, two):
+        return tuple(jnp.where(swap, q, p) for p, q in zip(one, two))
+
+    axis_a = [pick(p, q) for p, q in zip(ring, along_y)]
+    axis_b = [pick(q, p) for p, q in zip(ring, along_y)]
+    at_a = jnp.where(swap, y, x)
+    at_b = jnp.where(swap, x, y)
+
+    m_swap.wait_recv()
+
+    def halve(i, carry):
+        a, b = lax.div(i, 4), lax.rem(i, 4)
+        row = jnp.where(swap, a * 96 + b * 24, b * 96 + a * 24)
+        mine = m_acc[pl.ds(pl.multiple_of(core * M_HALF + row, 8), 24), :]
+        m_first[a, b] = mine + m_sib[pl.ds(pl.multiple_of(row, 8), 24), :]
+        return carry
+
+    lax.fori_loop(0, 16, halve, 0)
+    m_a = [post(m_first.at[lax.rem(at_a + o, 4)], m_first_in.at[o - 1], axis_a[o]) for o in (1, 2, 3)]
+    for copy in m_a:
         copy.start()
 
     for copy in m_a:
@@ -522,16 +573,44 @@
     m_last.append(to(band(y + 2, 0, 96), sibling))
     for copy in m_last:
         copy.wait_recv()
-    m_out[...] = m_all[...]
-
-    for s in range(8):
-
-        @pl.when(jnp.logical_not(is_me(targets[s])))
-        def _():
-            ids_copy(s).wait_send()
 
     for copy in taken:
         copy.wait_send()
+
+
+def sum_call(*args):
+    vmem = pl.BlockSpec(memory_space=pltpu.VMEM)
+    dma = pltpu.SemaphoreType.DMA
+    f32 = lambda *shape: pltpu.VMEM(shape, F32)
+    return pl.pallas_call(
+        sum_kernel,
+        out_shape=(
+            jax.ShapeDtypeStruct((E, D_SLICE), F32),
+            jax.ShapeDtypeStruct((D_METH, E), F32),
+        ),
+        in_specs=[vmem, vmem],
+        out_specs=(vmem, vmem),
+        scratch_shapes=[
+            f32(M_HALF, E),
+            f32(4, 4, 24, E),
+            f32(3, 4, 24, E),
+            f32(4, 24, E),
+            f32(3, 24, E),
+            f32(3, 16, 4 * D_SLICE),
+            f32(8, 16, 256),
+            f32(7, 16, 256),
+            f32(8, 16, 256),
+            f32(4, 16, 4 * D_SLICE),
+            f32(8, 4, 16, D_SLICE),
+            dma((N_COPIES,)),
+            dma((N_COPIES,)),
+        ],
+        compiler_params=pltpu.CompilerParams(
+            collective_id=1, has_side_effects=True, vmem_limit_bytes=20 * 1024 * 1024
+        ),
+        cost_estimate=pl.CostEstimate(flops=10**7, bytes_accessed=8 * 10**6, transcendentals=0),
+        name="sum_heads",
+    )(*args)
 
 
 def step_call(*args):
@@ -545,17 +624,14 @@
     return pl.pallas_call(
         step_kernel,
         out_shape=(
-            jax.ShapeDtypeStruct((E, D_SLICE), F32),
+            jax.ShapeDtypeStruct((4, 16, 4 * D_SLICE), F32),
             jax.ShapeDtypeStruct((D_METH, E), F32),
         ),
-        in_specs=[vmem, vmem, vmem, hbm, hbm, vmem, hbm, smem, smem],
+        in_specs=[vmem, vmem, vmem, vmem, hbm, hbm, smem, smem],
         out_specs=(vmem, vmem),
         scratch_shapes=[
-            bf16(VOCAB_DNA, D_SLICE),
             bf16(VOCAB_METH, D_METH),
             bf16(D_METH, E),
-            i32(PAIR_DEV, 16),
-            bf16(PAIR_DEV, VOCAB_DNA),
             i32(16, COLS),
             i32(2, 3, 128),
             i32(ROWS, 128),
@@ -574,24 +650,10 @@
             f32(E, ROWS),
             bf16(ROWS, COLS),
             bf16(E, COLS),
-            f32(D_METH, E),
-            f32(M_HALF, E),
-            f32(4, 4, 24, E),
-            f32(3, 4, 24, E),
-            f32(4, 24, E),
-            f32(3, 24, E),
             bf16(E, ROWS),
             bf16(256, ROWS),
             bf16(4, 64, ROWS),
             bf16(3, 64, ROWS),
-            f32(4, 16, 4 * D_SLICE),
-            f32(3, 16, 4 * D_SLICE),
-            f32(8, 16, 256),
-            f32(7, 16, 256),
-            f32(8, 16, 256),
-            f32(D_METH, E),
-            f32(4, 16, 4 * D_SLICE),
-            f32(8, 4, 16, D_SLICE),
             dma((8,)),
             dma((8,)),
             dma((N_COPIES,)),
@@ -599,10 +661,10 @@
             dma((4,)),
         ],
         compiler_params=pltpu.CompilerParams(
-            collective_id=0, has_side_effects=True, vmem_limit_bytes=56 * 1024 * 1024
+            collective_id=0, has_side_effects=True, vmem_limit_bytes=52 * 1024 * 1024
         ),
-        cost_estimate=pl.CostEstimate(flops=19 * 10**9, bytes_accessed=8 * 10**6, transcendentals=5 * 10**6),
-        name="contrastive_step",
+        cost_estimate=pl.CostEstimate(flops=17 * 10**9, bytes_accessed=4 * 10**6, transcendentals=5 * 10**6),
+        name="pair_tiles",
     )(*args)
 
 
@@ -638,18 +700,18 @@
     logit_scale,
     logit_bias,
 ):
+    dna_part, projt_part = pool_call(dna_ids.T, dna_table, dna_proj)
     d_part, m_part = step_call(
-        dna_ids.T,
+        dna_part,
+        projt_part,
         meth_ids.T,
         pair_index.reshape(3, 128),
-        dna_table,
         meth_table,
-        dna_proj,
         meth_proj,
         logit_scale,
         logit_bias,
     )
-    return hand_over(d_part, m_part)
+    return hand_over(*sum_call(d_part, m_part))
 
 
 def solution(mesh):

time: 101 us -> 115 us (1.14)
  Pallas kernels: 96.2 us -> 108 us
  local copies, waits for them, and re-layouts: 2.44 us -> 4.68 us
    pallas_call x1 -> x3, Pallas kernels: 94.6 us -> 106 us  [the longest x1 53.2 us: step_call(): pl.pallas_call(step_kernel, out_shape=(jax.ShapeDtypeStruct((4, 16, 4 * D...]
    unnamed x4 -> x14, local copies, waits for them, and re-layouts: 2.44 us -> 4.68 us
where the time goes in v5:
time: 115 us; the launch traced here: 114 us
  Pallas kernels  108 us (94%)
  local copies, waits for them, and re-layouts  4.68 us (4%)
  between operations  2.01 us (2%)
    pallas_call x1, Pallas kernels, step_call(): pl.pallas_call(step_kernel, out_shape=(jax.ShapeDtypeStruct((4, 16, 4 * D...  53.2 us
    pallas_call x1, Pallas kernels, sum_call(): pl.pallas_call(sum_kernel, out_shape=(jax.ShapeDtypeStruct((E, D_SLICE),...  46.9 us
    pallas_call x1, Pallas kernels, pool_call(): pl.pallas_call(pool_kernel, out_shape=(jax.ShapeDtypeStruct((D_SLICE, PAI...  6.06 us
    unnamed x14, local copies, waits for them, and re-layouts  4.68 us

profile of v5, /device:TPU:1, one launch (start us, length us, event | category | flops | bytes accessed | tf_op | source)
XLA Modules:
  0.0 114.4 jit_solution(1888630703831703001)
XLA Ops:
  0.6 0.0 copy-start.6
  1.9 0.0 copy-start
  2.0 1.6 %copy-done = bf16[4096,256]{1,0:T(8,128)(2,1)S(1)} copy-done((bf16[4096,256]{1,0:T(8,128)(2,1)S(1)}, bf16[4096,256]{1,0:T(8,128)(2,1)}, u32[]{:S(2)}) %copy-start) | copy-done | bytes 2097176
  3.5 0.0 copy-start.2
  3.5 0.9 copy-done.2
  4.5 0.0 copy-start.3
  4.5 0.7 copy-done.3
  5.2 0.0 copy-start.4
  5.2 0.0 copy-start.5
  5.2 6.1 %pool_dna.1 = (bf16[256,384]{1,0:T(8,128)(2,1)S(1)}, bf16[512,256]{1,0:T(8,128)(2,1)S(1)}) custom-call(s32[16,384]{1,0:T(8,128)S(1)} %bitcast.3, bf16[4096,256]{1,0:T(8,128)(2,1)S(1)} %copy-done, bf16[256,512]{1,0:T(8,128)(2,1)S(1)} %copy-done.2), custom_call_target="tpu_custom_call" | custom-call | tf_op jit(solution)/shard_map/pool_dna/pallas_call | solution.py:84
  11.3 0.0 copy-done.6
  11.3 0.0 copy-done.4
  11.3 0.0 copy-done.5
  11.3 53.2 %pair_tiles.1 = (f32[4,16,1024]{2,1,0:T(8,128)S(1)}, f32[768,512]{1,0:T(8,128)}) custom-call(bf16[256,384]{1,0:T(8,128)(2,1)S(1)} %get-tuple-element.8.dna_part, bf16[512,256]{1,0:T(8,128)(2,1)S(1)} %get-tuple-element.9.dna_projt_part, s32[16,384]{1,0:T(8,128)S(1)} %bitcast.4, s32[3,128]{1,0:T(4,128)S(1)} %bitcast.5, bf16[512,768]{1,0:T(8,128)(2,1)S(1)} %copy-done.4, ...), custom_call_target="tpu_custom_call" | custom-call | flops 16999999488 | bytes 4000000 | tf_op jit(solution)/shard_map/pair_tiles/pallas_call | solution.py:624
  64.6 0.0 copy-start.1
  64.6 1.4 %copy-done.1 = f32[768,512]{1,0:T(8,128)S(1)} copy-done((f32[768,512]{1,0:T(8,128)S(1)}, f32[768,512]{1,0:T(8,128)}, u32[]{:S(2)}) %copy-start.1) | copy-done | bytes 1572888
  66.0 46.9 %sum_heads.1 = (f32[512,256]{1,0:T(8,128)S(1)}, f32[768,512]{1,0:T(8,128)S(1)}) custom-call(f32[4,16,1024]{2,1,0:T(8,128)S(1)} %get-tuple-element.10.d_first, f32[768,512]{1,0:T(8,128)S(1)} %copy-done.1), custom_call_target="tpu_custom_call" | custom-call | flops 10000000 | bytes 8000000 | tf_op jit(solution)/shard_map/sum_heads/pallas_call | solution.py:585
  112.9 1.6 %hand_over.1 = (f32[256,512]{1,0:T(8,128)}, f32[768,512]{1,0:T(8,128)}) custom-call(f32[512,256]{1,0:T(8,128)S(1)} %get-tuple-element.12.d_in, f32[768,512]{1,0:T(8,128)S(1)} %get-tuple-element.13.m_in), custom_call_target="tpu_custom_call" | custom-call | tf_op jit(solution)/shard_map/hand_over/pallas_call | solution.py:679
Async XLA Ops:
  0.6 10.7 %copy-start.6 = (s32[384]{0:T(512)S(1)}, s32[384]{0:T(512)}, u32[]{:S(2)}) copy-start(s32[384]{0:T(512)} %param.11) | copy-start | bytes 4612
  1.9 1.6 %copy-start = (bf16[4096,256]{1,0:T(8,128)(2,1)S(1)}, bf16[4096,256]{1,0:T(8,128)(2,1)}, u32[]{:S(2)}) copy-start(bf16[4096,256]{1,0:T(8,128)(2,1)} %dna_table.1) | copy-start | bytes 6291460
  3.5 0.9 copy-start.2
  4.5 0.7 copy-start.3
  5.2 6.1 %copy-start.4 = (bf16[512,768]{1,0:T(8,128)(2,1)S(1)}, bf16[512,768]{1,0:T(8,128)(2,1)}, u32[]{:S(2)}) copy-start(bf16[512,768]{1,0:T(8,128)(2,1)} %meth_table_hbm.1) | copy-start | bytes 2359300
  5.2 6.1 %copy-start.5 = (s32[384,16]{0,1:T(8,128)S(1)}, s32[384,16]{0,1:T(8,128)}, u32[]{:S(2)}) copy-start(s32[384,16]{0,1:T(8,128)} %param.10) | copy-start | bytes 73732
  64.6 1.4 %copy-start.1 = (f32[768,512]{1,0:T(8,128)S(1)}, f32[768,512]{1,0:T(8,128)}, u32[]{:S(2)}) copy-start(f32[768,512]{1,0:T(8,128)} %get-tuple-element.11.m_acc) | copy-start | bytes 4718596

commit v6 on v4

--- a/solution.py
+++ b/solution.py
@@ -21,8 +21,8 @@
 CHUNK = 1536
 PART = 512
 LOG2E = 1.4426950408889634
-M_HALF = 384
-N_COPIES = 64
+E_HALF = 256
+N_COPIES = 80
 
 NT = (((1,), (1,)), ((), ()))
 
@@ -57,22 +57,25 @@
 
 
 def step_kernel(
-    dna_ids,
-    meth_ids,
-    pairs,
+    dna_ids_hbm,
+    meth_ids_hbm,
+    pairs_hbm,
     dna_table_hbm,
     meth_table_hbm,
-    dna_proj,
+    dna_proj_hbm,
     meth_proj_hbm,
     scale_ref,
     bias_ref,
     d_out,
     m_out,
+    dna_ids,
+    meth_ids,
+    pairs,
+    dna_proj,
     dna_table,
     meth_table,
     meth_proj,
     dna_tokens,
-    counts,
     ids_all,
     pair_all,
     pair_wide,
@@ -90,30 +93,33 @@
     dna_rows,
     row_acc,
     tiles,
-    meth_back,
-    m_acc,
+    m_give,
+    m_keep,
     m_sib,
-    m_first,
     m_first_in,
     m_second,
     m_second_in,
+    m_third,
+    m_third_in,
+    m_z_all,
     back_all,
     back_sib,
     back_half,
     back_in,
     d_first,
     d_first_in,
-    third,
-    third_in,
-    third_all,
+    d_third,
+    d_third_in,
+    d_all,
+    d_slab,
     m_all,
-    d_slab,
     d_fin,
     ids_send,
     ids_recv,
     send_sems,
     recv_sems,
     local_sems,
+    write_sems,
 ):
     blk, mp, z, y, x, core = place()
     x_hi = lax.div(x, 2)
@@ -135,11 +141,19 @@
     fetch = [
         pltpu.make_async_copy(src, dst, local_sems.at[1 + n])
         for n, (src, dst) in enumerate(
-            ((dna_table_hbm, dna_table), (meth_table_hbm, meth_table), (meth_proj_hbm, meth_proj))
+            (
+                (dna_table_hbm, dna_table),
+                (meth_table_hbm, meth_table),
+                (meth_proj_hbm, meth_proj),
+                (dna_ids_hbm, dna_ids),
+                (meth_ids_hbm, meth_ids),
+                (pairs_hbm, pairs),
+                (dna_proj_hbm, dna_proj),
+            )
         )
     ]
-    for copy in fetch:
-        copy.start()
+    for n in (4, 5, 6, 3, 0, 1, 2):
+        fetch[n].start()
 
     targets = [device_at(s, mp, lax.div(z, 2), lax.rem(z, 2)) for s in range(8)]
     sources = [device_at(block, s // 2, (s % 2) * 2 + lax.div(y, 2), lax.rem(y, 2)) for s in range(8)]
@@ -160,6 +174,8 @@
     for o in range(1, 8):
         signal(along_z[o])
     signal(sibling)
+    for n in (3, 4, 5, 6):
+        fetch[n].wait()
     to_self = jnp.logical_and(mp == y, block == z).astype(jnp.int32)
     pl.semaphore_wait(pltpu.get_barrier_semaphore(), 25 - to_self)
 
@@ -215,12 +231,20 @@
             total = total + jnp.where(lane == place_of[:, t : t + 1], amount[:, t : t + 1], 0)
         for f in range(4):
             field = jnp.bitwise_and(jnp.right_shift(total, 8 * f), 255)
-            counts[rows, f * 1024 : (f + 1) * 1024] = field.astype(F32).astype(BF16)
+            field = field.astype(F32).astype(BF16)
+            if f < 3:
+                tiles[rows, f * 1024 : (f + 1) * 1024] = field
+            else:
+                tiles[pl.ds(pl.multiple_of(PAIR_DEV + i * 16, 16), 16), 0:1024] = field
         return carry
 
     lax.fori_loop(0, PAIR_DEV // 16, count_dna, 0)
     fetch[0].wait()
-    pooled = jnp.dot(counts[...], dna_table[...], preferred_element_type=F32) * 0.0625
+    pooled = jnp.dot(tiles[0:PAIR_DEV, :], dna_table[0:COLS, :], preferred_element_type=F32)
+    pooled = pooled + jnp.dot(
+        tiles[PAIR_DEV:ROWS, 0 : VOCAB_DNA - COLS], dna_table[COLS:VOCAB_DNA, :], preferred_element_type=F32
+    )
+    pooled = pooled * 0.0625
     own_lanes = pl.ds(pl.multiple_of(x_hi * PAIR_DEV, 128), PAIR_DEV)
     dna_pooled[pl.ds(pl.multiple_of(mp * D_SLICE, 16), D_SLICE), own_lanes] = pooled.T.astype(BF16)
 
@@ -359,7 +383,7 @@
             up = scale * jnp.dot(dna_rowst[...], tiles[:, lanes], preferred_element_type=F32)
             unit_m = meth_unit[:, lanes]
             inner = jnp.sum(unit_m * up, axis=0, keepdims=True)
-            meth_back[:, lanes] = (meth_inv[:, lanes] * (up - unit_m * inner)).astype(BF16)
+            meth_rows[:, lanes] = (meth_inv[:, lanes] * (up - unit_m * inner)).astype(BF16)
         return carry
 
     lax.fori_loop(0, half, col_tile, 0)
@@ -372,35 +396,6 @@
     for copy in back_x:
         copy.start()
     lax.fori_loop(half, 2 * half, col_tile, 0)
-
-    m_acc[...] = lax.dot_general(meth_pooled[...], meth_back[...], NT, preferred_element_type=F32)
-
-    m_swap = post(m_acc.at[pl.ds(pl.multiple_of(other * M_HALF, 8), M_HALF)], m_sib, sibling)
-    m_swap.start()
-
-    swap = core == 1
-
-    def pick(one, two):
-        return tuple(jnp.where(swap, q, p) for p, q in zip(one, two))
-
-    axis_a = [pick(p, q) for p, q in zip(ring, along_y)]
-    axis_b = [pick(q, p) for p, q in zip(ring, along_y)]
-    at_a = jnp.where(swap, y, x)
-    at_b = jnp.where(swap, x, y)
-
-    m_swap.wait_recv()
-
-    def halve(i, carry):
-        a, b = lax.div(i, 4), lax.rem(i, 4)
-        row = jnp.where(swap, a * 96 + b * 24, b * 96 + a * 24)
-        mine = m_acc[pl.ds(pl.multiple_of(core * M_HALF + row, 8), 24), :]
-        m_first[a, b] = mine + m_sib[pl.ds(pl.multiple_of(row, 8), 24), :]
-        return carry
-
-    lax.fori_loop(0, 16, halve, 0)
-    m_a = [post(m_first.at[lax.rem(at_a + o, 4)], m_first_in.at[o - 1], axis_a[o]) for o in (1, 2, 3)]
-    for copy in m_a:
-        copy.start()
 
     for copy in back_x:
         copy.wait_recv()
@@ -417,16 +412,14 @@
     for copy in d_y:
         copy.start()
 
-    for copy in m_a:
-        copy.wait_recv()
-    for b in range(4):
-        part = m_first[at_a, b]
-        for o in range(3):
-            part = part + m_first_in[o, b]
-        m_second[b] = part
-    m_b = [post(m_second.at[lax.rem(at_b + o, 4)], m_second_in.at[o - 1], axis_b[o]) for o in (1, 2, 3)]
-    for copy in m_b:
-        copy.start()
+    def half_head(which):
+        rows = pl.ds(pl.multiple_of(which * E_HALF, 16), E_HALF)
+        return lax.dot_general(meth_rows[rows, :], meth_pooled[...], NT, preferred_element_type=F32)
+
+    m_give[...] = half_head(other)
+    m_swap = post(m_give, m_sib, sibling)
+    m_swap.start()
+    m_keep[...] = half_head(core)
 
     for copy in d_y:
         copy.wait_recv()
@@ -434,95 +427,146 @@
     for o in range(3):
         d_sum = d_sum + d_first_in[o]
     for s in range(8):
-        lanes = slice(s * 128, (s + 1) * 128)
-        third[s, 8:16, 0:128] = d_sum[0:8, lanes]
-        third[s, 8:16, 128:256] = d_sum[8:16, lanes]
+        d_third[s] = d_sum[:, s * 128 : (s + 1) * 128]
+    d_z = [post(d_third.at[lax.rem(z + o, 8)], d_third_in.at[o - 1], along_z[o]) for o in range(1, 8)]
+    for copy in d_z:
+        copy.start()
+
+    swap = core == 1
+
+    def pick(one, two):
+        return tuple(jnp.where(swap, q, p) for p, q in zip(one, two))
+
+    axis_a = [pick(p, q) for p, q in zip(ring, along_y)]
+    axis_b = [pick(q, p) for p, q in zip(ring, along_y)]
+    at_a = jnp.where(swap, y, x)
+    at_b = jnp.where(swap, x, y)
+
+    def band(of, rows=64):
+        return pl.ds(pl.multiple_of(of * rows, 16), rows)
+
+    m_swap.wait_recv()
+    m_keep[...] = m_keep[...] + m_sib[...]
+    m_a = [post(m_keep.at[band(lax.rem(at_a + o, 4))], m_first_in.at[o - 1], axis_a[o]) for o in (1, 2, 3)]
+    for copy in m_a:
+        copy.start()
+
+    for copy in d_z:
+        copy.wait_recv()
+    total = d_third[z]
+    for o in range(7):
+        total = total + d_third_in[o]
+    d_all[z] = total
+    d_z_back = [post(d_all.at[z], d_all.at[z], along_z[o]) for o in range(1, 8)]
+    for copy in d_z_back:
+        copy.start()
+
+    for copy in m_a:
+        copy.wait_recv()
+    part = m_keep[band(at_a), :]
+    for o in range(3):
+        part = part + m_first_in[o]
+    for b in range(4):
+        m_second[b] = part[b * 16 : (b + 1) * 16, :]
+    m_b = [post(m_second.at[lax.rem(at_b + o, 4)], m_second_in.at[o - 1], axis_b[o]) for o in (1, 2, 3)]
+    for copy in m_b:
+        copy.start()
+
+    for copy in d_z_back:
+        copy.wait_recv()
+    for s in range(8):
+        d_slab[y, :, s * 128 : (s + 1) * 128] = d_all[s]
+    d_back = [post(d_slab.at[y], d_slab.at[y], along_y[o]) for o in (1, 2, 3)]
+    for copy in d_back:
+        copy.start()
+
     for copy in m_b:
         copy.wait_recv()
     m_sum = m_second[at_b]
     for o in range(3):
         m_sum = m_sum + m_second_in[o]
     for s in range(6):
-        third[s, 0:8, :] = m_sum[s // 2 * 8 : s // 2 * 8 + 8, s % 2 * 256 : s % 2 * 256 + 256]
-    third[6, 0:8, :] = jnp.zeros((8, 256), F32)
-    third[7, 0:8, :] = jnp.zeros((8, 256), F32)
-
-    z_sum = [post(third.at[lax.rem(z + o, 8)], third_in.at[o - 1], along_z[o]) for o in range(1, 8)]
-    for copy in z_sum:
-        copy.start()
-    for copy in z_sum:
-        copy.wait_recv()
-    total = third[z]
+        m_third[s] = m_sum[:, s * 128 : (s + 1) * 128]
+    m_third[6] = jnp.zeros((16, 128), F32)
+    m_third[7] = jnp.zeros((16, 128), F32)
+    m_z = [post(m_third.at[lax.rem(z + o, 8)], m_third_in.at[o - 1], along_z[o]) for o in range(1, 8)]
+    for copy in m_z:
+        copy.start()
+
+    for copy in d_back:
+        copy.wait_recv()
+    eighth = core * 4 + x
+
+    def slice_for(device):
+        return d_slab.at[:, :, pl.ds(pl.multiple_of(device[1] * D_SLICE, 128), D_SLICE)]
+
+    d_ring = [post(slice_for(device), d_fin.at[eighth], device) for device in ring[1:] + cross[1:] + [sibling]]
+    for copy in d_ring:
+        copy.start()
+    d_fin[eighth] = d_slab[:, :, pl.ds(pl.multiple_of(mp * D_SLICE, 128), D_SLICE)]
+
+    for copy in m_z:
+        copy.wait_recv()
+    total = m_third[z]
     for o in range(7):
-        total = total + third_in[o]
-    third_all[z] = total
-    z_back = [post(third_all.at[z], third_all.at[z], along_z[o]) for o in range(1, 8)]
-    for copy in z_back:
-        copy.start()
-    for copy in z_back:
-        copy.wait_recv()
-
-    for s in range(8):
-        lanes = slice(s * 128, (s + 1) * 128)
-        d_slab[y, 0:8, lanes] = third_all[s, 8:16, 0:128]
-        d_slab[y, 8:16, lanes] = third_all[s, 8:16, 128:256]
-    d_back = [post(d_slab.at[y], d_slab.at[y], along_y[o]) for o in (1, 2, 3)]
-    for copy in d_back:
-        copy.start()
-    sub = core * M_HALF + y * 96 + x * 24
-    for s in range(6):
-        rows = pl.ds(pl.multiple_of(sub + s // 2 * 8, 8), 8)
-        m_all[rows, s % 2 * 256 : s % 2 * 256 + 256] = third_all[s, 0:8, :]
-    piece = m_all.at[pl.ds(pl.multiple_of(sub, 8), 24)]
-    m_back_x = [post(piece, piece, ring[o]) for o in (1, 2, 3)]
-    for copy in m_back_x:
-        copy.start()
-
-    def band(y_of, low, rows):
-        first = core * M_HALF + lax.rem(y_of, 4) * 96 + low
-        return m_all.at[pl.ds(pl.multiple_of(first, 8), rows)]
+        total = total + m_third_in[o]
+    m_z_all[z] = total
+    m_z_back = [post(m_z_all.at[z], m_z_all.at[z], along_z[o]) for o in range(1, 8)]
+    for copy in m_z_back:
+        copy.start()
+    for copy in m_z_back:
+        copy.wait_recv()
+
+    def rows_at(a, low, rows):
+        return m_all.at[pl.ds(pl.multiple_of(core * E_HALF + lax.rem(a, 4) * 64 + low, 16), rows)]
 
     def to(part, device):
         copy = post(part, part, device)
         copy.start()
         return copy
 
-    for copy in m_back_x:
-        copy.wait_recv()
-    own_band = band(y, 0, 96)
-    up_copy = to(own_band, along_y[1])
-    down_copy = to(own_band, along_y[3])
+    sub = pl.ds(pl.multiple_of(core * E_HALF + at_a * 64 + at_b * 16, 16), 16)
+    for s in range(6):
+        m_all[sub, s * 128 : (s + 1) * 128] = m_z_all[s]
+    m_back_b = [to(m_all.at[sub], axis_b[o]) for o in (1, 2, 3)]
+    for copy in m_back_b:
+        copy.wait_recv()
+    own_band = rows_at(at_a, 0, 64)
+    up_copy = to(own_band, axis_a[1])
+    down_copy = to(own_band, axis_a[3])
     m_last = [to(own_band, sibling)]
-
-    for copy in d_back:
-        copy.wait_recv()
-    eighth = core * 4 + x
-
-    def slice_for(device):
-        return d_slab.at[:, :, pl.ds(pl.multiple_of(device[1] * D_SLICE, 128), D_SLICE)]
-
-    d_ring = [post(slice_for(device), d_fin.at[eighth], device) for device in ring[1:] + cross[1:] + [sibling]]
+    up_copy.wait_recv()
+    relay_up = to(rows_at(at_a + 3, 0, 32), axis_a[1])
+    m_last.append(to(rows_at(at_a + 3, 0, 64), sibling))
+    down_copy.wait_recv()
+    relay_down = to(rows_at(at_a + 1, 32, 32), axis_a[3])
+    m_last.append(to(rows_at(at_a + 1, 0, 64), sibling))
+    written = []
+
+    def write(src, dst):
+        copy = pltpu.make_async_copy(src, dst, write_sems.at[len(written)])
+        copy.start()
+        written.append(copy)
+
+    def write_band(of, half):
+        rows = pl.ds(pl.multiple_of(half * E_HALF + lax.rem(of, 4) * 64, 16), 64)
+        write(m_all.at[rows], m_out.at[rows])
+
+    for o in (0, 3, 1):
+        write_band(at_a + o, core)
     for copy in d_ring:
-        copy.start()
-    own_lanes = pl.ds(pl.multiple_of(mp * D_SLICE, 128), D_SLICE)
-    d_fin[eighth] = d_slab[:, :, own_lanes]
-
-    up_copy.wait_recv()
-    relay_up = to(band(y + 3, 0, 48), along_y[1])
-    m_last.append(to(band(y + 3, 0, 96), sibling))
-    down_copy.wait_recv()
-    relay_down = to(band(y + 1, 48, 48), along_y[3])
-    m_last.append(to(band(y + 1, 0, 96), sibling))
-
-    for copy in d_ring:
-        copy.wait_recv()
-    d_out[...] = d_fin[...].reshape(E, D_SLICE)
+        copy.wait_recv()
+    write(d_fin, d_out)
     relay_up.wait_recv()
     relay_down.wait_recv()
-    m_last.append(to(band(y + 2, 0, 96), sibling))
-    for copy in m_last:
-        copy.wait_recv()
-    m_out[...] = m_all[...]
+    m_last.append(to(rows_at(at_a + 2, 0, 64), sibling))
+    write_band(at_a + 2, core)
+    sib_a = jnp.where(swap, x, y)
+    for copy, o in zip(m_last, (0, 3, 1, 2)):
+        copy.wait_recv()
+        write_band(sib_a + o, other)
+    for copy in written:
+        copy.wait()
 
     for s in range(8):
 
@@ -537,7 +581,7 @@
 def step_call(*args):
     vmem = pl.BlockSpec(memory_space=pltpu.VMEM)
     smem = pl.BlockSpec(memory_space=pltpu.SMEM)
-    hbm = pl.BlockSpec(memory_space=pl.ANY)
+    hbm = pl.BlockSpec(memory_space=pltpu.HBM)
     dma = pltpu.SemaphoreType.DMA
     f32 = lambda *shape: pltpu.VMEM(shape, F32)
     bf16 = lambda *shape: pltpu.VMEM(shape, BF16)
@@ -545,17 +589,20 @@
     return pl.pallas_call(
         step_kernel,
         out_shape=(
-            jax.ShapeDtypeStruct((E, D_SLICE), F32),
-            jax.ShapeDtypeStruct((D_METH, E), F32),
+            jax.ShapeDtypeStruct((8, 4, 16, D_SLICE), F32),
+            jax.ShapeDtypeStruct((E, D_METH), F32),
         ),
-        in_specs=[vmem, vmem, vmem, hbm, hbm, vmem, hbm, smem, smem],
-        out_specs=(vmem, vmem),
+        in_specs=[hbm] * 7 + [smem] * 2,
+        out_specs=(hbm, hbm),
         scratch_shapes=[
+            i32(16, PAIR_DEV),
+            i32(16, PAIR_DEV),
+            i32(3, 128),
+            bf16(D_SLICE, E),
             bf16(VOCAB_DNA, D_SLICE),
             bf16(VOCAB_METH, D_METH),
             bf16(D_METH, E),
             i32(PAIR_DEV, 16),
-            bf16(PAIR_DEV, VOCAB_DNA),
             i32(16, COLS),
             i32(2, 3, 128),
             i32(ROWS, 128),
@@ -573,30 +620,33 @@
             bf16(ROWS, E),
             f32(E, ROWS),
             bf16(ROWS, COLS),
-            bf16(E, COLS),
-            f32(D_METH, E),
-            f32(M_HALF, E),
-            f32(4, 4, 24, E),
-            f32(3, 4, 24, E),
-            f32(4, 24, E),
-            f32(3, 24, E),
+            f32(E_HALF, D_METH),
+            f32(E_HALF, D_METH),
+            f32(E_HALF, D_METH),
+            f32(3, 64, D_METH),
+            f32(4, 16, D_METH),
+            f32(3, 16, D_METH),
+            f32(8, 16, 128),
+            f32(7, 16, 128),
+            f32(8, 16, 128),
             bf16(E, ROWS),
             bf16(256, ROWS),
             bf16(4, 64, ROWS),
             bf16(3, 64, ROWS),
             f32(4, 16, 4 * D_SLICE),
             f32(3, 16, 4 * D_SLICE),
-            f32(8, 16, 256),
-            f32(7, 16, 256),
-            f32(8, 16, 256),
-            f32(D_METH, E),
+            f32(8, 16, 128),
+            f32(7, 16, 128),
+            f32(8, 16, 128),
             f32(4, 16, 4 * D_SLICE),
+            f32(E, D_METH),
             f32(8, 4, 16, D_SLICE),
             dma((8,)),
             dma((8,)),
             dma((N_COPIES,)),
             dma((N_COPIES,)),
-            dma((4,)),
+            dma((8,)),
+            dma((9,)),
         ],
         compiler_params=pltpu.CompilerParams(
             collective_id=0, has_side_effects=True, vmem_limit_bytes=56 * 1024 * 1024
@@ -606,23 +656,47 @@
     )(*args)
 
 
-def hand_over_kernel(d_in, m_in, d_out, m_out):
-    for s in range(E // 128):
-        d_out[:, s * 128 : (s + 1) * 128] = d_in[s * 128 : (s + 1) * 128, :].T
-    m_out[...] = m_in[...]
+def hand_over_kernel(d_in, m_in, d_out, m_out, d_here, m_here, d_turned, m_turned, in_sems, out_sems):
+    bands = [slice(s * 128, (s + 1) * 128) for s in range(E // 128)]
+    pairs = [(m_in, m_here, m_turned, m_out), (d_in, d_here, d_turned, d_out)]
+    parts = [(rows, pair) for pair in pairs for rows in bands]
+    fetch = [
+        pltpu.make_async_copy(src.at[rows], here.at[rows], in_sems.at[n])
+        for n, (rows, (src, here, turned, dst)) in enumerate(parts)
+    ]
+    store = [
+        pltpu.make_async_copy(turned.at[:, rows], dst.at[:, rows], out_sems.at[n])
+        for n, (rows, (src, here, turned, dst)) in enumerate(parts)
+    ]
+    for copy in fetch:
+        copy.start()
+    for n, (rows, (src, here, turned, dst)) in enumerate(parts):
+        fetch[n].wait()
+        turned[:, rows] = here[rows, :].T
+        store[n].start()
+    for copy in store:
+        copy.wait()
 
 
 def hand_over(d_part, m_part):
-    vmem = pl.BlockSpec(memory_space=pltpu.VMEM)
+    hbm = pl.BlockSpec(memory_space=pltpu.HBM)
     return pl.pallas_call(
         hand_over_kernel,
         out_shape=(
             jax.ShapeDtypeStruct((D_SLICE, E), F32),
             jax.ShapeDtypeStruct((D_METH, E), F32),
         ),
-        in_specs=[vmem, vmem],
-        out_specs=(vmem, vmem),
-        compiler_params=pltpu.CompilerParams(vmem_limit_bytes=8 * 1024 * 1024),
+        in_specs=[hbm, hbm],
+        out_specs=(hbm, hbm),
+        scratch_shapes=[
+            pltpu.VMEM((E, D_SLICE), F32),
+            pltpu.VMEM((E, D_METH), F32),
+            pltpu.VMEM((D_SLICE, E), F32),
+            pltpu.VMEM((D_METH, E), F32),
+            pltpu.SemaphoreType.DMA((8,)),
+            pltpu.SemaphoreType.DMA((8,)),
+        ],
+        compiler_params=pltpu.CompilerParams(vmem_limit_bytes=56 * 1024 * 1024),
         name="hand_over",
     )(d_part, m_part)
 
@@ -649,7 +723,7 @@
         logit_scale,
         logit_bias,
     )
-    return hand_over(d_part, m_part)
+    return hand_over(d_part.reshape(E, D_SLICE), m_part)
 
 
 def solution(mesh):

time: 101 us -> 105 us (1.040)
  Pallas kernels: 96.2 us -> 103 us
  local copies, waits for them, and re-layouts: 2.44 us -> 0 us
    pallas_call x1, Pallas kernels: 94.6 us -> 99.9 us  [step_call(): pl.pallas_call(step_kernel, out_shape=(jax.ShapeDtypeStruct((8, 4, 16, D_...]
    unnamed x4 -> x0, local copies, waits for them, and re-layouts: 2.44 us -> none
    pallas_call x1, Pallas kernels: 1.55 us -> 2.88 us  [hand_over(): pl.pallas_call(hand_over_kernel, out_shape=(jax.ShapeDtypeStruct((D_SLICE...]
where the time goes in v6:
time: 105 us
  Pallas kernels  103 us (98%)
  between operations  2.09 us (2%)
    pallas_call x1, Pallas kernels, step_call(): pl.pallas_call(step_kernel, out_shape=(jax.ShapeDtypeStruct((8, 4, 16, D_...  99.9 us
    pallas_call x1, Pallas kernels, hand_over(): pl.pallas_call(hand_over_kernel, out_shape=(jax.ShapeDtypeStruct((D_SLICE...  2.88 us

profile of v6, /device:TPU:1, one launch (start us, length us, event | category | flops | bytes accessed | tf_op | source)
XLA Modules:
  0.0 104.8 jit_solution(1097208874791538251)
XLA Ops:
  1.9 99.9 %contrastive_step.1 = (f32[8,4,16,256]{3,2,1,0:T(8,128)}, f32[512,768]{1,0:T(8,128)}) custom-call(s32[16,384]{1,0:T(8,128)} %bitcast.5, s32[16,384]{1,0:T(8,128)} %bitcast.6, s32[3,128]{1,0:T(4,128)} %bitcast.7, bf16[4096,256]{1,0:T(8,128)(2,1)} %dna_table_hbm.1, bf16[512,768]{1,0:T(8,128)(2,1)} %meth_table_hbm.1, bf16[256,512]{1,0:T(8,128)(2,1)} %dna_proj_hbm.1, ...), custom_call_target="tpu_custom_call" | custom-call | flops 19000000512 | bytes 8000000 | tf_op jit(solution)/shard_map/contrastive_step/pallas_call | solution.py:589
  101.8 2.9 %hand_over.1 = (f32[256,512]{1,0:T(8,128)}, f32[768,512]{1,0:T(8,128)}) custom-call(f32[512,256]{1,0:T(8,128)} %bitcast.4, f32[512,768]{1,0:T(8,128)} %get-tuple-element.5.m_in), custom_call_target="tpu_custom_call" | custom-call | tf_op jit(solution)/shard_map/hand_over/pallas_call | solution.py:683

commit v7 on v6

--- a/solution.py
+++ b/solution.py
@@ -94,6 +94,7 @@
     row_acc,
     tiles,
     m_give,
+    m_low,
     m_keep,
     m_sib,
     m_first_in,
@@ -107,6 +108,7 @@
     back_half,
     back_in,
     d_first,
+    d_first_low,
     d_first_in,
     d_third,
     d_third_in,
@@ -408,15 +410,16 @@
         part = lax.dot_general(back, features, NT, preferred_element_type=F32)
         for a in range(4):
             d_first[a, :, s * D_SLICE : (s + 1) * D_SLICE] = part[a * 16 : (a + 1) * 16, :]
-    d_y = [post(d_first.at[lax.rem(y + o, 4)], d_first_in.at[o - 1], along_y[o]) for o in (1, 2, 3)]
+            d_first_low[a, :, s * D_SLICE : (s + 1) * D_SLICE] = part[a * 16 : (a + 1) * 16, :].astype(BF16)
+    d_y = [post(d_first_low.at[lax.rem(y + o, 4)], d_first_in.at[o - 1], along_y[o]) for o in (1, 2, 3)]
     for copy in d_y:
         copy.start()
 
     def half_head(which):
         rows = pl.ds(pl.multiple_of(which * E_HALF, 16), E_HALF)
-        return lax.dot_general(meth_rows[rows, :], meth_pooled[...], NT, preferred_element_type=F32)
-
-    m_give[...] = half_head(other)
+        return lax.dot_general(meth_pooled[...], meth_rows[rows, :], NT, preferred_element_type=F32)
+
+    m_give[...] = half_head(other).astype(BF16)
     m_swap = post(m_give, m_sib, sibling)
     m_swap.start()
     m_keep[...] = half_head(core)
@@ -425,7 +428,7 @@
         copy.wait_recv()
     d_sum = d_first[y]
     for o in range(3):
-        d_sum = d_sum + d_first_in[o]
+        d_sum = d_sum + d_first_in[o].astype(F32)
     for s in range(8):
         d_third[s] = d_sum[:, s * 128 : (s + 1) * 128]
     d_z = [post(d_third.at[lax.rem(z + o, 8)], d_third_in.at[o - 1], along_z[o]) for o in range(1, 8)]
@@ -442,12 +445,14 @@
     at_a = jnp.where(swap, y, x)
     at_b = jnp.where(swap, x, y)
 
-    def band(of, rows=64):
+    def band(of, rows=192):
         return pl.ds(pl.multiple_of(of * rows, 16), rows)
 
     m_swap.wait_recv()
-    m_keep[...] = m_keep[...] + m_sib[...]
-    m_a = [post(m_keep.at[band(lax.rem(at_a + o, 4))], m_first_in.at[o - 1], axis_a[o]) for o in (1, 2, 3)]
+    both = m_keep[...] + m_sib[...].astype(F32)
+    m_keep[...] = both
+    m_low[...] = both.astype(BF16)
+    m_a = [post(m_low.at[band(lax.rem(at_a + o, 4))], m_first_in.at[o - 1], axis_a[o]) for o in (1, 2, 3)]
     for copy in m_a:
         copy.start()
 
@@ -465,9 +470,9 @@
         copy.wait_recv()
     part = m_keep[band(at_a), :]
     for o in range(3):
-        part = part + m_first_in[o]
+        part = part + m_first_in[o].astype(F32)
     for b in range(4):
-        m_second[b] = part[b * 16 : (b + 1) * 16, :]
+        m_second[b] = part[b * 48 : (b + 1) * 48, :]
     m_b = [post(m_second.at[lax.rem(at_b + o, 4)], m_second_in.at[o - 1], axis_b[o]) for o in (1, 2, 3)]
     for copy in m_b:
         copy.start()
@@ -486,7 +491,7 @@
     for o in range(3):
         m_sum = m_sum + m_second_in[o]
     for s in range(6):
-        m_third[s] = m_sum[:, s * 128 : (s + 1) * 128]
+        m_third[s] = m_sum[s // 2 * 16 : s // 2 * 16 + 16, s % 2 * 128 : s % 2 * 128 + 128]
     m_third[6] = jnp.zeros((16, 128), F32)
     m_third[7] = jnp.zeros((16, 128), F32)
     m_z = [post(m_third.at[lax.rem(z + o, 8)], m_third_in.at[o - 1], along_z[o]) for o in range(1, 8)]
@@ -518,29 +523,31 @@
         copy.wait_recv()
 
     def rows_at(a, low, rows):
-        return m_all.at[pl.ds(pl.multiple_of(core * E_HALF + lax.rem(a, 4) * 64 + low, 16), rows)]
+        return m_all.at[core, pl.ds(pl.multiple_of(lax.rem(a, 4) * 192 + low, 16), rows)]
 
     def to(part, device):
         copy = post(part, part, device)
         copy.start()
         return copy
 
-    sub = pl.ds(pl.multiple_of(core * E_HALF + at_a * 64 + at_b * 16, 16), 16)
+    sub = at_a * 192 + at_b * 48
     for s in range(6):
-        m_all[sub, s * 128 : (s + 1) * 128] = m_z_all[s]
-    m_back_b = [to(m_all.at[sub], axis_b[o]) for o in (1, 2, 3)]
+        rows = pl.ds(pl.multiple_of(sub + s // 2 * 16, 16), 16)
+        m_all[core, rows, s % 2 * 128 : s % 2 * 128 + 128] = m_z_all[s]
+    own_block = m_all.at[core, pl.ds(pl.multiple_of(sub, 16), 48)]
+    m_back_b = [to(own_block, axis_b[o]) for o in (1, 2, 3)]
     for copy in m_back_b:
         copy.wait_recv()
-    own_band = rows_at(at_a, 0, 64)
+    own_band = rows_at(at_a, 0, 192)
     up_copy = to(own_band, axis_a[1])
     down_copy = to(own_band, axis_a[3])
     m_last = [to(own_band, sibling)]
     up_copy.wait_recv()
-    relay_up = to(rows_at(at_a + 3, 0, 32), axis_a[1])
-    m_last.append(to(rows_at(at_a + 3, 0, 64), sibling))
+    relay_up = to(rows_at(at_a + 3, 0, 96), axis_a[1])
+    m_last.append(to(rows_at(at_a + 3, 0, 192), sibling))
     down_copy.wait_recv()
-    relay_down = to(rows_at(at_a + 1, 32, 32), axis_a[3])
-    m_last.append(to(rows_at(at_a + 1, 0, 64), sibling))
+    relay_down = to(rows_at(at_a + 1, 96, 96), axis_a[3])
+    m_last.append(to(rows_at(at_a + 1, 0, 192), sibling))
     written = []
 
     def write(src, dst):
@@ -549,8 +556,8 @@
         written.append(copy)
 
     def write_band(of, half):
-        rows = pl.ds(pl.multiple_of(half * E_HALF + lax.rem(of, 4) * 64, 16), 64)
-        write(m_all.at[rows], m_out.at[rows])
+        rows = pl.ds(pl.multiple_of(lax.rem(of, 4) * 192, 16), 192)
+        write(m_all.at[half, rows], m_out.at[half, rows])
 
     for o in (0, 3, 1):
         write_band(at_a + o, core)
@@ -559,7 +566,7 @@
     write(d_fin, d_out)
     relay_up.wait_recv()
     relay_down.wait_recv()
-    m_last.append(to(rows_at(at_a + 2, 0, 64), sibling))
+    m_last.append(to(rows_at(at_a + 2, 0, 192), sibling))
     write_band(at_a + 2, core)
     sib_a = jnp.where(swap, x, y)
     for copy, o in zip(m_last, (0, 3, 1, 2)):
@@ -590,7 +597,7 @@
         step_kernel,
         out_shape=(
             jax.ShapeDtypeStruct((8, 4, 16, D_SLICE), F32),
-            jax.ShapeDtypeStruct((E, D_METH), F32),
+            jax.ShapeDtypeStruct((2, D_METH, E_HALF), F32),
         ),
         in_specs=[hbm] * 7 + [smem] * 2,
         out_specs=(hbm, hbm),
@@ -620,12 +627,13 @@
             bf16(ROWS, E),
             f32(E, ROWS),
             bf16(ROWS, COLS),
-            f32(E_HALF, D_METH),
-            f32(E_HALF, D_METH),
-            f32(E_HALF, D_METH),
-            f32(3, 64, D_METH),
-            f32(4, 16, D_METH),
-            f32(3, 16, D_METH),
+            bf16(D_METH, E_HALF),
+            bf16(D_METH, E_HALF),
+            f32(D_METH, E_HALF),
+            bf16(D_METH, E_HALF),
+            bf16(3, 192, E_HALF),
+            f32(4, 48, E_HALF),
+            f32(3, 48, E_HALF),
             f32(8, 16, 128),
             f32(7, 16, 128),
             f32(8, 16, 128),
@@ -634,12 +642,13 @@
             bf16(4, 64, ROWS),
             bf16(3, 64, ROWS),
             f32(4, 16, 4 * D_SLICE),
-            f32(3, 16, 4 * D_SLICE),
+            bf16(4, 16, 4 * D_SLICE),
+            bf16(3, 16, 4 * D_SLICE),
             f32(8, 16, 128),
             f32(7, 16, 128),
             f32(8, 16, 128),
             f32(4, 16, 4 * D_SLICE),
-            f32(E, D_METH),
+            f32(2, D_METH, E_HALF),
             f32(8, 4, 16, D_SLICE),
             dma((8,)),
             dma((8,)),
@@ -656,23 +665,22 @@
     )(*args)
 
 
-def hand_over_kernel(d_in, m_in, d_out, m_out, d_here, m_here, d_turned, m_turned, in_sems, out_sems):
-    bands = [slice(s * 128, (s + 1) * 128) for s in range(E // 128)]
-    pairs = [(m_in, m_here, m_turned, m_out), (d_in, d_here, d_turned, d_out)]
-    parts = [(rows, pair) for pair in pairs for rows in bands]
-    fetch = [
-        pltpu.make_async_copy(src.at[rows], here.at[rows], in_sems.at[n])
-        for n, (rows, (src, here, turned, dst)) in enumerate(parts)
-    ]
-    store = [
-        pltpu.make_async_copy(turned.at[:, rows], dst.at[:, rows], out_sems.at[n])
-        for n, (rows, (src, here, turned, dst)) in enumerate(parts)
-    ]
+def hand_over_kernel(d_in, m_in, d_out, m_out, d_here, m_here, d_turned, in_sems, out_sems):
+    m_parts = [(half, pl.ds(first, 192)) for half in range(2) for first in range(0, D_METH, 192)]
+    d_parts = [slice(s * 128, (s + 1) * 128) for s in range(E // 128)]
+    fetch = [(m_in.at[h, rows], m_here.at[h, rows]) for h, rows in m_parts]
+    store = [(m_here.at[h, rows], m_out.at[rows, pl.ds(h * E_HALF, E_HALF)]) for h, rows in m_parts]
+    fetch += [(d_in.at[rows], d_here.at[rows]) for rows in d_parts]
+    store += [(d_turned.at[:, rows], d_out.at[:, rows]) for rows in d_parts]
+    fetch = [pltpu.make_async_copy(*pair, in_sems.at[n]) for n, pair in enumerate(fetch)]
+    store = [pltpu.make_async_copy(*pair, out_sems.at[n]) for n, pair in enumerate(store)]
     for copy in fetch:
         copy.start()
-    for n, (rows, (src, here, turned, dst)) in enumerate(parts):
+    for n in range(len(store)):
         fetch[n].wait()
-        turned[:, rows] = here[rows, :].T
+        if n >= len(m_parts):
+            rows = d_parts[n - len(m_parts)]
+            d_turned[:, rows] = d_here[rows, :].T
         store[n].start()
     for copy in store:
         copy.wait()
@@ -690,11 +698,10 @@
         out_specs=(hbm, hbm),
         scratch_shapes=[
             pltpu.VMEM((E, D_SLICE), F32),
-            pltpu.VMEM((E, D_METH), F32),
+            pltpu.VMEM((2, D_METH, E_HALF), F32),
             pltpu.VMEM((D_SLICE, E), F32),
-            pltpu.VMEM((D_METH, E), F32),
-            pltpu.SemaphoreType.DMA((8,)),
-            pltpu.SemaphoreType.DMA((8,)),
+            pltpu.SemaphoreType.DMA((12,)),
+            pltpu.SemaphoreType.DMA((12,)),
         ],
         compiler_params=pltpu.CompilerParams(vmem_limit_bytes=56 * 1024 * 1024),
         name="hand_over",

time: 105 us -> 102 us (0.971)
  Pallas kernels: 103 us -> 100 us
    pallas_call x1, Pallas kernels: 99.9 us -> 97.3 us  [step_call(): pl.pallas_call(step_kernel, out_shape=(jax.ShapeDtypeStruct((8, 4, 16, D_...]
where the time goes in v7:
time: 102 us
  Pallas kernels  100 us (98%)
  between operations  2.09 us (2%)
    pallas_call x1, Pallas kernels, step_call(): pl.pallas_call(step_kernel, out_shape=(jax.ShapeDtypeStruct((8, 4, 16, D_...  97.3 us
    pallas_call x1, Pallas kernels, hand_over(): pl.pallas_call(hand_over_kernel, out_shape=(jax.ShapeDtypeStruct((D_SLICE...  2.76 us

profile of v7, /device:TPU:1, one launch (start us, length us, event | category | flops | bytes accessed | tf_op | source)
XLA Modules:
  0.0 102.2 jit_solution(244832637428196513)
XLA Ops:
  1.9 97.3 %contrastive_step.1 = (f32[8,4,16,256]{3,2,1,0:T(8,128)}, f32[2,768,256]{2,1,0:T(8,128)}) custom-call(s32[16,384]{1,0:T(8,128)} %bitcast.5, s32[16,384]{1,0:T(8,128)} %bitcast.6, s32[3,128]{1,0:T(4,128)} %bitcast.7, bf16[4096,256]{1,0:T(8,128)(2,1)} %dna_table_hbm.1, bf16[512,768]{1,0:T(8,128)(2,1)} %meth_table_hbm.1, bf16[256,512]{1,0:T(8,128)(2,1)} %dna_proj_hbm.1, ...), custom_call_target="tpu_custom_call" | custom-call | flops 19000000512 | bytes 8000000 | tf_op jit(solution)/shard_map/contrastive_step/pallas_call | solution.py:596
  99.3 2.8 %hand_over.1 = (f32[256,512]{1,0:T(8,128)}, f32[768,512]{1,0:T(8,128)}) custom-call(f32[512,256]{1,0:T(8,128)} %bitcast.4, f32[2,768,256]{2,1,0:T(8,128)} %get-tuple-element.5.m_in), custom_call_target="tpu_custom_call" | custom-call | tf_op jit(solution)/shard_map/hand_over/pallas_call | solution.py:691

commit v8 on v7

--- a/solution.py
+++ b/solution.py
@@ -18,8 +18,8 @@
 D_METH = 768
 VOCAB_DNA = 4096
 VOCAB_METH = 512
-CHUNK = 1536
-PART = 512
+CHUNK = 768
+PART = 256
 LOG2E = 1.4426950408889634
 E_HALF = 256
 N_COPIES = 80
@@ -94,15 +94,16 @@
     row_acc,
     tiles,
     m_give,
+    m_sib,
+    m_keep,
+    m_first,
     m_low,
-    m_keep,
-    m_sib,
     m_first_in,
     m_second,
     m_second_in,
-    m_third,
-    m_third_in,
-    m_z_all,
+    third,
+    third_in,
+    third_all,
     back_all,
     back_sib,
     back_half,
@@ -110,9 +111,6 @@
     d_first,
     d_first_low,
     d_first_in,
-    d_third,
-    d_third_in,
-    d_all,
     d_slab,
     m_all,
     d_fin,
@@ -130,8 +128,9 @@
     cross = [device_at(z, y, lax.rem(x + o, 4), 1 - core) for o in range(4)]
     along_y = [device_at(z, lax.rem(y + o, 4), x, core) for o in range(4)]
     along_z = [device_at(lax.rem(z + o, 8), y, x, core) for o in range(8)]
-    slot = lax.rem(blk, 8)
-    block = x_hi * 4 + mp
+    ring_place = x_hi * 4 + mp
+    nearest = lax.rem(lax.div(ring_place + 1, 2), 4)
+
     taken = []
 
     def post(src, dst, device):
@@ -157,8 +156,19 @@
     for n in (4, 5, 6, 3, 0, 1, 2):
         fetch[n].start()
 
-    targets = [device_at(s, mp, lax.div(z, 2), lax.rem(z, 2)) for s in range(8)]
-    sources = [device_at(block, s // 2, (s % 2) * 2 + lax.div(y, 2), lax.rem(y, 2)) for s in range(8)]
+    def at_ring_place(z_of, y_of, place_of):
+        return device_at(lax.rem(z_of, 8), lax.rem(y_of, 4), lax.div(place_of, 2), lax.rem(place_of, 2))
+
+    def group(dy):
+        dz = lax.rem(ring_place + 8 - 2 * dy, 8)
+        return lax.rem(z + dz, 8), lax.rem(y + dy, 4)
+
+    def source(dy, half):
+        z_of, y_of = group(dy)
+        return ((z_of * 4 + y_of) * 2 + half, dy)
+
+    targets = [at_ring_place(z + 8 - s, y + 4 - mp, lax.rem(s + 2 * mp, 8)) for s in range(8)]
+    sources = [source(s // 2, s % 2) for s in range(8)]
 
     def is_me(device):
         return jnp.logical_and(device[0] == blk, device[1] == mp)
@@ -178,48 +188,6 @@
     signal(sibling)
     for n in (3, 4, 5, 6):
         fetch[n].wait()
-    to_self = jnp.logical_and(mp == y, block == z).astype(jnp.int32)
-    pl.semaphore_wait(pltpu.get_barrier_semaphore(), 25 - to_self)
-
-    def ids_copy(s):
-        lanes = pl.ds(pl.multiple_of(slot * PAIR_DEV, 128), PAIR_DEV)
-        return send(meth_ids, ids_all.at[:, lanes], ids_send.at[s], ids_recv.at[slot], targets[s])
-
-    def ids_arrival(s):
-        lanes = pl.ds(s * PAIR_DEV, PAIR_DEV)
-        return send(meth_ids, ids_all.at[:, lanes], ids_send.at[s], ids_recv.at[s], sources[s])
-
-    for s in range(8):
-
-        @pl.when(jnp.logical_not(is_me(targets[s])))
-        def _():
-            ids_copy(s).start()
-
-        @pl.when(is_me(targets[s]))
-        def _():
-            lanes = pl.ds(pl.multiple_of(slot * PAIR_DEV, 128), PAIR_DEV)
-            local = pltpu.make_async_copy(meth_ids, ids_all.at[:, lanes], local_sems.at[0])
-            local.start()
-            local.wait()
-
-    pair_copy = post(pairs, pair_all.at[x_hi], ring[2])
-    pair_copy.start()
-    pair_all[x_hi] = pairs[...]
-
-    dna_projt[:, pl.ds(pl.multiple_of(mp * D_SLICE, 128), D_SLICE)] = dna_proj[...].T
-    toward = 1 + 2 * core
-    far = device_at(z, y, lax.rem(x + toward, 4), core)
-    other_mp = lax.rem(mp + 2, 4)
-
-    def quarter(of):
-        return dna_projt.at[:, pl.ds(pl.multiple_of(of * D_SLICE, 128), D_SLICE)]
-
-    proj_far = post(quarter(mp), quarter(mp), far)
-    proj_sib = post(quarter(mp), quarter(mp), sibling)
-    proj_fwd = post(quarter(other_mp), quarter(other_mp), sibling)
-    proj_far.start()
-    proj_sib.start()
-
     dna_tokens[...] = dna_ids[...].T
 
     def count_dna(i, carry):
@@ -241,6 +209,45 @@
         return carry
 
     lax.fori_loop(0, PAIR_DEV // 16, count_dna, 0)
+    to_self = jnp.logical_and(mp == 0, x_hi == 0).astype(jnp.int32)
+    pl.semaphore_wait(pltpu.get_barrier_semaphore(), 25 - to_self)
+
+    slot = mp * 2 + x_hi
+    slot_lanes = pl.ds(pl.multiple_of(slot * PAIR_DEV, 128), PAIR_DEV)
+
+    def ids_copy(s):
+        return send(meth_ids, ids_all.at[:, slot_lanes], ids_send.at[s], ids_recv.at[slot], targets[s])
+
+    for s in range(8):
+
+        @pl.when(jnp.logical_not(is_me(targets[s])))
+        def _():
+            ids_copy(s).start()
+
+        @pl.when(is_me(targets[s]))
+        def _():
+            local = pltpu.make_async_copy(meth_ids, ids_all.at[:, slot_lanes], local_sems.at[0])
+            local.start()
+            local.wait()
+
+    pair_copy = post(pairs, pair_all.at[x_hi], ring[2])
+    pair_copy.start()
+    pair_all[x_hi] = pairs[...]
+
+    dna_projt[:, pl.ds(pl.multiple_of(mp * D_SLICE, 128), D_SLICE)] = dna_proj[...].T
+    toward = 1 + 2 * core
+    far = device_at(z, y, lax.rem(x + toward, 4), core)
+    other_mp = lax.rem(mp + 2, 4)
+
+    def quarter(of):
+        return dna_projt.at[:, pl.ds(pl.multiple_of(of * D_SLICE, 128), D_SLICE)]
+
+    proj_far = post(quarter(mp), quarter(mp), far)
+    proj_sib = post(quarter(mp), quarter(mp), sibling)
+    proj_fwd = post(quarter(other_mp), quarter(other_mp), sibling)
+    proj_far.start()
+    proj_sib.start()
+
     fetch[0].wait()
     pooled = jnp.dot(tiles[0:PAIR_DEV, :], dna_table[0:COLS, :], preferred_element_type=F32)
     pooled = pooled + jnp.dot(
@@ -275,12 +282,6 @@
     fetch[2].wait()
     meth_tablet[...] = meth_table[...].T
     meth_projt[...] = meth_proj[...].T
-    for s in range(8):
-
-        @pl.when(jnp.logical_not(is_me(sources[s])))
-        def _():
-            ids_arrival(s).wait_recv()
-
     def count_meth(ids):
         place_of = jnp.bitwise_and(ids, 127)
         amount = jnp.left_shift(1, jnp.right_shift(ids, 7) * 8)
@@ -292,8 +293,19 @@
         return jnp.concatenate([field.astype(F32).astype(BF16) for field in fields], axis=0)
 
     def embed_meth(i, carry):
+        dy = lax.rem(nearest + i + lax.div(i, 2) * (5 - 2 * i), 4)
+        for half in range(2):
+            lanes = pl.ds(pl.multiple_of((dy * 2 + half) * PAIR_DEV, 128), PAIR_DEV)
+            arrival = send(
+                meth_ids, ids_all.at[:, lanes], ids_send.at[0], ids_recv.at[dy * 2 + half], source(dy, half)
+            )
+
+            @pl.when(jnp.logical_not(is_me(source(dy, half))))
+            def _():
+                arrival.wait_recv()
+
         for p in range(CHUNK // PART):
-            first = pl.multiple_of(i * CHUNK + p * PART, 128)
+            first = pl.multiple_of(dy * CHUNK + p * PART, 128)
             lanes = pl.ds(first, PART)
             ids = [ids_all[:, pl.ds(pl.multiple_of(first + 128 * g, 128), 128)] for g in range(PART // 128)]
             tokens = jnp.concatenate([count_meth(part) for part in ids], axis=1)
@@ -347,11 +359,10 @@
     scale = scale_ref[0]
     bias = bias_ref[0]
     slope, offset = scale * -LOG2E, bias * -LOG2E
-    first_col = block * COLS
-
     def pair_tile(i, carry):
         first = pl.multiple_of(i * CHUNK, 128)
-        partner = pair_wide[...] - (first_col + first)
+        z_of, y_of = group(i)
+        partner = pair_wide[...] - (z_of * 4 + y_of) * ROWS
         parts = []
         for p in range(CHUNK // PART):
             rows_m = meth_rows[:, pl.ds(pl.multiple_of(first + p * PART, 128), PART)]
@@ -424,79 +435,99 @@
     m_swap.start()
     m_keep[...] = half_head(core)
 
+    swap = core == 1
+
+    def pick(one, two):
+        return tuple(jnp.where(swap, q, p) for p, q in zip(one, two))
+
+    axis_a = [pick(p, q) for p, q in zip(ring, along_y)]
+    axis_b = [pick(q, p) for p, q in zip(ring, along_y)]
+    at_a = jnp.where(swap, y, x)
+    at_b = jnp.where(swap, x, y)
+    m_swap.wait_recv()
+
+    def halve(i, carry):
+        a, b = lax.div(i, 4), lax.rem(i, 4)
+        rows = pl.ds(pl.multiple_of(jnp.where(swap, a * 192 + b * 48, b * 192 + a * 48), 16), 48)
+        both = m_keep[rows, :] + m_sib[rows, :].astype(F32)
+        m_first[a, b] = both
+        m_low[a, b] = both.astype(BF16)
+        return carry
+
+    lax.fori_loop(0, 16, halve, 0)
+    m_a = [post(m_low.at[lax.rem(at_a + o, 4)], m_first_in.at[o - 1], axis_a[o]) for o in (1, 2, 3)]
+    for copy in m_a:
+        copy.start()
+
     for copy in d_y:
         copy.wait_recv()
     d_sum = d_first[y]
     for o in range(3):
         d_sum = d_sum + d_first_in[o].astype(F32)
     for s in range(8):
-        d_third[s] = d_sum[:, s * 128 : (s + 1) * 128]
-    d_z = [post(d_third.at[lax.rem(z + o, 8)], d_third_in.at[o - 1], along_z[o]) for o in range(1, 8)]
-    for copy in d_z:
-        copy.start()
-
-    swap = core == 1
-
-    def pick(one, two):
-        return tuple(jnp.where(swap, q, p) for p, q in zip(one, two))
-
-    axis_a = [pick(p, q) for p, q in zip(ring, along_y)]
-    axis_b = [pick(q, p) for p, q in zip(ring, along_y)]
-    at_a = jnp.where(swap, y, x)
-    at_b = jnp.where(swap, x, y)
-
-    def band(of, rows=192):
-        return pl.ds(pl.multiple_of(of * rows, 16), rows)
-
-    m_swap.wait_recv()
-    both = m_keep[...] + m_sib[...].astype(F32)
-    m_keep[...] = both
-    m_low[...] = both.astype(BF16)
-    m_a = [post(m_low.at[band(lax.rem(at_a + o, 4))], m_first_in.at[o - 1], axis_a[o]) for o in (1, 2, 3)]
+        third[s, 1] = d_sum[:, s * 128 : (s + 1) * 128]
+
     for copy in m_a:
-        copy.start()
-
-    for copy in d_z:
-        copy.wait_recv()
-    total = d_third[z]
-    for o in range(7):
-        total = total + d_third_in[o]
-    d_all[z] = total
-    d_z_back = [post(d_all.at[z], d_all.at[z], along_z[o]) for o in range(1, 8)]
-    for copy in d_z_back:
-        copy.start()
-
-    for copy in m_a:
-        copy.wait_recv()
-    part = m_keep[band(at_a), :]
-    for o in range(3):
-        part = part + m_first_in[o].astype(F32)
+        copy.wait_recv()
     for b in range(4):
-        m_second[b] = part[b * 48 : (b + 1) * 48, :]
+        part = m_first[at_a, b]
+        for o in range(3):
+            part = part + m_first_in[o, b].astype(F32)
+        m_second[b] = part
     m_b = [post(m_second.at[lax.rem(at_b + o, 4)], m_second_in.at[o - 1], axis_b[o]) for o in (1, 2, 3)]
     for copy in m_b:
         copy.start()
-
-    for copy in d_z_back:
-        copy.wait_recv()
-    for s in range(8):
-        d_slab[y, :, s * 128 : (s + 1) * 128] = d_all[s]
-    d_back = [post(d_slab.at[y], d_slab.at[y], along_y[o]) for o in (1, 2, 3)]
-    for copy in d_back:
-        copy.start()
-
     for copy in m_b:
         copy.wait_recv()
     m_sum = m_second[at_b]
     for o in range(3):
         m_sum = m_sum + m_second_in[o]
     for s in range(6):
-        m_third[s] = m_sum[s // 2 * 16 : s // 2 * 16 + 16, s % 2 * 128 : s % 2 * 128 + 128]
-    m_third[6] = jnp.zeros((16, 128), F32)
-    m_third[7] = jnp.zeros((16, 128), F32)
-    m_z = [post(m_third.at[lax.rem(z + o, 8)], m_third_in.at[o - 1], along_z[o]) for o in range(1, 8)]
-    for copy in m_z:
-        copy.start()
+        third[s, 0] = m_sum[s // 2 * 16 : s // 2 * 16 + 16, s % 2 * 128 : s % 2 * 128 + 128]
+    third[6, 0] = jnp.zeros((16, 128), F32)
+    third[7, 0] = jnp.zeros((16, 128), F32)
+
+    z_sum = [post(third.at[lax.rem(z + o, 8)], third_in.at[o - 1], along_z[o]) for o in range(1, 8)]
+    for copy in z_sum:
+        copy.start()
+    for copy in z_sum:
+        copy.wait_recv()
+    total = third[z]
+    for o in range(7):
+        total = total + third_in[o]
+    third_all[z] = total
+    z_back = [post(third_all.at[z], third_all.at[z], along_z[o]) for o in range(1, 8)]
+    for copy in z_back:
+        copy.start()
+    for copy in z_back:
+        copy.wait_recv()
+
+    for s in range(8):
+        d_slab[y, :, s * 128 : (s + 1) * 128] = third_all[s, 1]
+    d_back = [post(d_slab.at[y], d_slab.at[y], along_y[o]) for o in (1, 2, 3)]
+    for copy in d_back:
+        copy.start()
+
+    def rows_at(y_of, low, rows):
+        return m_all.at[core, pl.ds(pl.multiple_of(lax.rem(y_of, 4) * 192 + low, 16), rows)]
+
+    def to(part, device):
+        copy = post(part, part, device)
+        copy.start()
+        return copy
+
+    sub = y * 192 + x * 48
+    for s in range(6):
+        rows = pl.ds(pl.multiple_of(sub + s // 2 * 16, 16), 16)
+        m_all[core, rows, s % 2 * 128 : s % 2 * 128 + 128] = third_all[s, 0]
+    own_block = m_all.at[core, pl.ds(pl.multiple_of(sub, 16), 48)]
+    m_back_x = [to(own_block, ring[o]) for o in (1, 2, 3)]
+    for copy in m_back_x:
+        copy.wait_recv()
+    own_band = rows_at(y, 0, 192)
+    up_copy = to(own_band, along_y[1])
+    down_copy = to(own_band, along_y[3])
+    m_last = [to(own_band, sibling)]
 
     for copy in d_back:
         copy.wait_recv()
@@ -510,44 +541,6 @@
         copy.start()
     d_fin[eighth] = d_slab[:, :, pl.ds(pl.multiple_of(mp * D_SLICE, 128), D_SLICE)]
 
-    for copy in m_z:
-        copy.wait_recv()
-    total = m_third[z]
-    for o in range(7):
-        total = total + m_third_in[o]
-    m_z_all[z] = total
-    m_z_back = [post(m_z_all.at[z], m_z_all.at[z], along_z[o]) for o in range(1, 8)]
-    for copy in m_z_back:
-        copy.start()
-    for copy in m_z_back:
-        copy.wait_recv()
-
-    def rows_at(a, low, rows):
-        return m_all.at[core, pl.ds(pl.multiple_of(lax.rem(a, 4) * 192 + low, 16), rows)]
-
-    def to(part, device):
-        copy = post(part, part, device)
-        copy.start()
-        return copy
-
-    sub = at_a * 192 + at_b * 48
-    for s in range(6):
-        rows = pl.ds(pl.multiple_of(sub + s // 2 * 16, 16), 16)
-        m_all[core, rows, s % 2 * 128 : s % 2 * 128 + 128] = m_z_all[s]
-    own_block = m_all.at[core, pl.ds(pl.multiple_of(sub, 16), 48)]
-    m_back_b = [to(own_block, axis_b[o]) for o in (1, 2, 3)]
-    for copy in m_back_b:
-        copy.wait_recv()
-    own_band = rows_at(at_a, 0, 192)
-    up_copy = to(own_band, axis_a[1])
-    down_copy = to(own_band, axis_a[3])
-    m_last = [to(own_band, sibling)]
-    up_copy.wait_recv()
-    relay_up = to(rows_at(at_a + 3, 0, 96), axis_a[1])
-    m_last.append(to(rows_at(at_a + 3, 0, 192), sibling))
-    down_copy.wait_recv()
-    relay_down = to(rows_at(at_a + 1, 96, 96), axis_a[3])
-    m_last.append(to(rows_at(at_a + 1, 0, 192), sibling))
     written = []
 
     def write(src, dst):
@@ -555,23 +548,29 @@
         copy.start()
         written.append(copy)
 
-    def write_band(of, half):
-        rows = pl.ds(pl.multiple_of(lax.rem(of, 4) * 192, 16), 192)
+    def write_band(y_of, half):
+        rows = pl.ds(pl.multiple_of(lax.rem(y_of, 4) * 192, 16), 192)
         write(m_all.at[half, rows], m_out.at[half, rows])
 
-    for o in (0, 3, 1):
-        write_band(at_a + o, core)
+    write_band(y, core)
+    up_copy.wait_recv()
+    relay_up = to(rows_at(y + 3, 0, 96), along_y[1])
+    m_last.append(to(rows_at(y + 3, 0, 192), sibling))
+    down_copy.wait_recv()
+    relay_down = to(rows_at(y + 1, 96, 96), along_y[3])
+    m_last.append(to(rows_at(y + 1, 0, 192), sibling))
+    write_band(y + 3, core)
+    write_band(y + 1, core)
     for copy in d_ring:
         copy.wait_recv()
     write(d_fin, d_out)
     relay_up.wait_recv()
     relay_down.wait_recv()
-    m_last.append(to(rows_at(at_a + 2, 0, 192), sibling))
-    write_band(at_a + 2, core)
-    sib_a = jnp.where(swap, x, y)
+    m_last.append(to(rows_at(y + 2, 0, 192), sibling))
+    write_band(y + 2, core)
     for copy, o in zip(m_last, (0, 3, 1, 2)):
         copy.wait_recv()
-        write_band(sib_a + o, other)
+        write_band(y + o, other)
     for copy in written:
         copy.wait()
 
@@ -630,13 +629,14 @@
             bf16(D_METH, E_HALF),
             bf16(D_METH, E_HALF),
             f32(D_METH, E_HALF),
-            bf16(D_METH, E_HALF),
-            bf16(3, 192, E_HALF),
+            f32(4, 4, 48, E_HALF),
+            bf16(4, 4, 48, E_HALF),
+            bf16(3, 4, 48, E_HALF),
             f32(4, 48, E_HALF),
             f32(3, 48, E_HALF),
-            f32(8, 16, 128),
-            f32(7, 16, 128),
-            f32(8, 16, 128),
+            f32(8, 2, 16, 128),
+            f32(7, 2, 16, 128),
+            f32(8, 2, 16, 128),
             bf16(E, ROWS),
             bf16(256, ROWS),
             bf16(4, 64, ROWS),
@@ -644,9 +644,6 @@
             f32(4, 16, 4 * D_SLICE),
             bf16(4, 16, 4 * D_SLICE),
             bf16(3, 16, 4 * D_SLICE),
-            f32(8, 16, 128),
-            f32(7, 16, 128),
-            f32(8, 16, 128),
             f32(4, 16, 4 * D_SLICE),
             f32(2, D_METH, E_HALF),
             f32(8, 4, 16, D_SLICE),

time: 102 us -> 101 us (level)
  Pallas kernels: 100 us -> 98.9 us
    pallas_call x1, Pallas kernels: 97.3 us -> 96.1 us  [step_call(): pl.pallas_call(step_kernel, out_shape=(jax.ShapeDtypeStruct((8, 4, 16, D_...]
where the time goes in v8:
time: 101 us
  Pallas kernels  98.9 us (98%)
  between operations  2.09 us (2%)
    pallas_call x1, Pallas kernels, step_call(): pl.pallas_call(step_kernel, out_shape=(jax.ShapeDtypeStruct((8, 4, 16, D_...  96.1 us
    pallas_call x1, Pallas kernels, hand_over(): pl.pallas_call(hand_over_kernel, out_shape=(jax.ShapeDtypeStruct((D_SLICE...  2.76 us

profile of v8, /device:TPU:1, one launch (start us, length us, event | category | flops | bytes accessed | tf_op | source)
XLA Modules:
  0.0 101.0 jit_solution(4216446381572576395)
XLA Ops:
  1.9 96.1 %contrastive_step.1 = (f32[8,4,16,256]{3,2,1,0:T(8,128)}, f32[2,768,256]{2,1,0:T(8,128)}) custom-call(s32[16,384]{1,0:T(8,128)} %bitcast.5, s32[16,384]{1,0:T(8,128)} %bitcast.6, s32[3,128]{1,0:T(4,128)} %bitcast.7, bf16[4096,256]{1,0:T(8,128)(2,1)} %dna_table_hbm.1, bf16[512,768]{1,0:T(8,128)(2,1)} %meth_table_hbm.1, bf16[256,512]{1,0:T(8,128)(2,1)} %dna_proj_hbm.1, ...), custom_call_target="tpu_custom_call" | custom-call | flops 19000000512 | bytes 8000000 | tf_op jit(solution)/shard_map/contrastive_step/pallas_call | solution.py:595
  98.0 2.8 %hand_over.1 = (f32[256,512]{1,0:T(8,128)}, f32[768,512]{1,0:T(8,128)}) custom-call(f32[512,256]{1,0:T(8,128)} %bitcast.4, f32[2,768,256]{2,1,0:T(8,128)} %get-tuple-element.5.m_in), custom_call_target="tpu_custom_call" | custom-call | tf_op jit(solution)/shard_map/hand_over/pallas_call | solution.py:688

commit v9 on v8

--- a/solution.py
+++ b/solution.py
@@ -18,8 +18,10 @@
 D_METH = 768
 VOCAB_DNA = 4096
 VOCAB_METH = 512
-CHUNK = 768
-PART = 256
+CHUNK = 1536
+PART = 512
+EMBED = 256
+NIBBLES = 0x0F0F0F0F
 LOG2E = 1.4426950408889634
 E_HALF = 256
 N_COPIES = 80
@@ -54,6 +56,27 @@
         device_id=device,
         device_id_type=MESH,
     )
+
+
+def token_counts(ids, bits, axis):
+    place_of = jnp.bitwise_and(ids, 2**bits - 1)
+    amount = jnp.left_shift(1, jnp.right_shift(ids, bits) * 4)
+    shape = (ids.shape[0], 2**bits) if axis else (2**bits, ids.shape[1])
+    spot = lax.broadcasted_iota(jnp.int32, shape, axis)
+    even = odd = None
+    for first in (0, 8):
+        total = jnp.zeros(shape, jnp.int32)
+        for t in range(first, first + 8):
+            take = (slice(None), slice(t, t + 1)) if axis else (slice(t, t + 1), slice(None))
+            total = total + jnp.where(spot == place_of[take], amount[take], 0)
+        low = jnp.bitwise_and(total, NIBBLES)
+        high = jnp.bitwise_and(jnp.right_shift(total, 4), NIBBLES)
+        even, odd = (low, high) if even is None else (even + low, odd + high)
+    fields = []
+    for f in range(8):
+        field = jnp.bitwise_and(jnp.right_shift(odd if f % 2 else even, f // 2 * 8), 255)
+        fields.append(field.astype(F32).astype(BF16))
+    return fields
 
 
 def step_kernel(
@@ -93,10 +116,7 @@
     dna_rows,
     row_acc,
     tiles,
-    m_give,
-    m_sib,
     m_keep,
-    m_first,
     m_low,
     m_first_in,
     m_second,
@@ -127,6 +147,7 @@
     ring = [device_at(z, y, lax.rem(x + o, 4), core) for o in range(4)]
     cross = [device_at(z, y, lax.rem(x + o, 4), 1 - core) for o in range(4)]
     along_y = [device_at(z, lax.rem(y + o, 4), x, core) for o in range(4)]
+    cross_y = [device_at(z, lax.rem(y + o, 4), x, 1 - core) for o in range(4)]
     along_z = [device_at(lax.rem(z + o, 8), y, x, core) for o in range(8)]
     ring_place = x_hi * 4 + mp
     nearest = lax.rem(lax.div(ring_place + 1, 2), 4)
@@ -183,6 +204,7 @@
         signal(ring[o])
         signal(cross[o])
         signal(along_y[o])
+        signal(cross_y[o])
     for o in range(1, 8):
         signal(along_z[o])
     signal(sibling)
@@ -192,25 +214,18 @@
 
     def count_dna(i, carry):
         rows = pl.ds(pl.multiple_of(i * 16, 16), 16)
-        ids = dna_tokens[rows, :]
-        place_of = jnp.bitwise_and(ids, VOCAB_DNA // 4 - 1)
-        amount = jnp.left_shift(1, jnp.right_shift(ids, 10) * 8)
-        lane = lax.broadcasted_iota(jnp.int32, (16, VOCAB_DNA // 4), 1)
-        total = jnp.zeros((16, VOCAB_DNA // 4), jnp.int32)
-        for t in range(16):
-            total = total + jnp.where(lane == place_of[:, t : t + 1], amount[:, t : t + 1], 0)
-        for f in range(4):
-            field = jnp.bitwise_and(jnp.right_shift(total, 8 * f), 255)
-            field = field.astype(F32).astype(BF16)
-            if f < 3:
-                tiles[rows, f * 1024 : (f + 1) * 1024] = field
+        fields = token_counts(dna_tokens[rows, :], 9, 1)
+        for f, field in enumerate(fields):
+            if f < 6:
+                tiles[rows, f * 512 : (f + 1) * 512] = field
             else:
-                tiles[pl.ds(pl.multiple_of(PAIR_DEV + i * 16, 16), 16), 0:1024] = field
+                low = pl.ds(pl.multiple_of(PAIR_DEV + i * 16, 16), 16)
+                tiles[low, (f - 6) * 512 : (f - 5) * 512] = field
         return carry
 
     lax.fori_loop(0, PAIR_DEV // 16, count_dna, 0)
     to_self = jnp.logical_and(mp == 0, x_hi == 0).astype(jnp.int32)
-    pl.semaphore_wait(pltpu.get_barrier_semaphore(), 25 - to_self)
+    pl.semaphore_wait(pltpu.get_barrier_semaphore(), 28 - to_self)
 
     slot = mp * 2 + x_hi
     slot_lanes = pl.ds(pl.multiple_of(slot * PAIR_DEV, 128), PAIR_DEV)
@@ -282,16 +297,6 @@
     fetch[2].wait()
     meth_tablet[...] = meth_table[...].T
     meth_projt[...] = meth_proj[...].T
-    def count_meth(ids):
-        place_of = jnp.bitwise_and(ids, 127)
-        amount = jnp.left_shift(1, jnp.right_shift(ids, 7) * 8)
-        row = lax.broadcasted_iota(jnp.int32, (128, 128), 0)
-        total = jnp.zeros((128, 128), jnp.int32)
-        for t in range(16):
-            total = total + jnp.where(row == place_of[t : t + 1, :], amount[t : t + 1, :], 0)
-        fields = [jnp.bitwise_and(jnp.right_shift(total, 8 * f), 255) for f in range(4)]
-        return jnp.concatenate([field.astype(F32).astype(BF16) for field in fields], axis=0)
-
     def embed_meth(i, carry):
         dy = lax.rem(nearest + i + lax.div(i, 2) * (5 - 2 * i), 4)
         for half in range(2):
@@ -304,11 +309,13 @@
             def _():
                 arrival.wait_recv()
 
-        for p in range(CHUNK // PART):
-            first = pl.multiple_of(dy * CHUNK + p * PART, 128)
-            lanes = pl.ds(first, PART)
-            ids = [ids_all[:, pl.ds(pl.multiple_of(first + 128 * g, 128), 128)] for g in range(PART // 128)]
-            tokens = jnp.concatenate([count_meth(part) for part in ids], axis=1)
+        for p in range(ROWS // EMBED):
+            first = pl.multiple_of(dy * ROWS + p * EMBED, 128)
+            lanes = pl.ds(first, EMBED)
+            ids = [ids_all[:, pl.ds(pl.multiple_of(first + 128 * g, 128), 128)] for g in range(EMBED // 128)]
+            tokens = jnp.concatenate(
+                [jnp.concatenate(token_counts(part, 6, 0), axis=0) for part in ids], axis=1
+            )
             pooled_m = jnp.dot(meth_tablet[...], tokens, preferred_element_type=F32)
             pooled_m = (pooled_m * 0.0625).astype(BF16)
             meth_pooled[:, lanes] = pooled_m
@@ -320,8 +327,7 @@
             meth_rows[:, lanes] = unit.astype(BF16)
         return carry
 
-    half = COLS // CHUNK // 2
-    lax.fori_loop(0, half, embed_meth, 0)
+    lax.fori_loop(0, 2, embed_meth, 0)
     pool_right.wait_recv()
     relay_right.start()
     pool_left.wait_recv()
@@ -330,7 +336,7 @@
     pool_fwd[1].start()
     proj_far.wait_recv()
     proj_fwd.start()
-    lax.fori_loop(half, 2 * half, embed_meth, 0)
+    lax.fori_loop(2, 4, embed_meth, 0)
     relay_right.wait_recv()
     relay_left.wait_recv()
     pool_fwd[2].start()
@@ -361,8 +367,10 @@
     slope, offset = scale * -LOG2E, bias * -LOG2E
     def pair_tile(i, carry):
         first = pl.multiple_of(i * CHUNK, 128)
-        z_of, y_of = group(i)
-        partner = pair_wide[...] - (z_of * 4 + y_of) * ROWS
+        partners = []
+        for j in range(CHUNK // ROWS):
+            z_of, y_of = group(i * (CHUNK // ROWS) + j)
+            partners.append(pair_wide[...] - (z_of * 4 + y_of) * ROWS)
         parts = []
         for p in range(CHUNK // PART):
             rows_m = meth_rows[:, pl.ds(pl.multiple_of(first + p * PART, 128), PART)]
@@ -372,8 +380,9 @@
             prob = prob * (2.0 - lower * prob)
             for g in range(PART // 128):
                 part = prob[:, g * 128 : (g + 1) * 128]
-                lane = lax.broadcasted_iota(jnp.int32, (ROWS, 128), 1) + (p * PART + g * 128)
-                parts.append(jnp.where(partner == lane, part - 1.0, part).astype(BF16))
+                j, low = divmod(p * PART + g * 128, ROWS)
+                lane = lax.broadcasted_iota(jnp.int32, (ROWS, 128), 1) + low
+                parts.append(jnp.where(partners[j] == lane, part - 1.0, part).astype(BF16))
         tile = jnp.concatenate(parts, axis=1)
         tiles[:, pl.ds(first, CHUNK)] = tile
         return carry
@@ -399,7 +408,7 @@
             meth_rows[:, lanes] = (meth_inv[:, lanes] * (up - unit_m * inner)).astype(BF16)
         return carry
 
-    lax.fori_loop(0, half, col_tile, 0)
+    lax.fori_loop(0, 1, col_tile, 0)
     back_swap.wait_recv()
     for a in range(4):
         rows = pl.ds(pl.multiple_of(core * 256 + a * 64, 16), 64)
@@ -408,7 +417,7 @@
     back_x = [post(back_half.at[lax.rem(x + o, 4)], back_in.at[o - 1], ring[o]) for o in (1, 2, 3)]
     for copy in back_x:
         copy.start()
-    lax.fori_loop(half, 2 * half, col_tile, 0)
+    lax.fori_loop(1, 2, col_tile, 0)
 
     for copy in back_x:
         copy.wait_recv()
@@ -426,38 +435,47 @@
     for copy in d_y:
         copy.start()
 
+    swap = core == 1
+
+    def pick(one, two):
+        return tuple(jnp.where(swap, q, p) for p, q in zip(one, two))
+
+    axis_a = [pick(p, q) for p, q in zip(ring, along_y)]
+    axis_b = [pick(q, p) for p, q in zip(ring, along_y)]
+    cross_a = [pick(q, p) for p, q in zip(cross, cross_y)]
+    at_a = jnp.where(swap, y, x)
+    at_b = jnp.where(swap, x, y)
+    at_cross = jnp.where(swap, x, y)
+
     def half_head(which):
         rows = pl.ds(pl.multiple_of(which * E_HALF, 16), E_HALF)
         return lax.dot_general(meth_pooled[...], meth_rows[rows, :], NT, preferred_element_type=F32)
 
-    m_give[...] = half_head(other).astype(BF16)
-    m_swap = post(m_give, m_sib, sibling)
-    m_swap.start()
+    def block_rows(which, a, b):
+        return pl.ds(pl.multiple_of(jnp.where(which == 1, a * 192 + b * 48, b * 192 + a * 48), 16), 48)
+
+    def pack(which):
+        def pack_block(i, carry):
+            a, b = lax.div(i, 4), lax.rem(i, 4)
+            m_low[which, a, b] = m_keep[block_rows(which, a, b), :].astype(BF16)
+            return carry
+
+        lax.fori_loop(0, 16, pack_block, 0)
+
+    m_keep[...] = half_head(other)
+    pack(other)
+    m_a = [
+        post(m_low.at[other, lax.rem(at_cross + o, 4)], m_first_in.at[3 + o], sibling if o == 0 else cross_a[o])
+        for o in range(4)
+    ]
+    for copy in m_a:
+        copy.start()
     m_keep[...] = half_head(core)
-
-    swap = core == 1
-
-    def pick(one, two):
-        return tuple(jnp.where(swap, q, p) for p, q in zip(one, two))
-
-    axis_a = [pick(p, q) for p, q in zip(ring, along_y)]
-    axis_b = [pick(q, p) for p, q in zip(ring, along_y)]
-    at_a = jnp.where(swap, y, x)
-    at_b = jnp.where(swap, x, y)
-    m_swap.wait_recv()
-
-    def halve(i, carry):
-        a, b = lax.div(i, 4), lax.rem(i, 4)
-        rows = pl.ds(pl.multiple_of(jnp.where(swap, a * 192 + b * 48, b * 192 + a * 48), 16), 48)
-        both = m_keep[rows, :] + m_sib[rows, :].astype(F32)
-        m_first[a, b] = both
-        m_low[a, b] = both.astype(BF16)
-        return carry
-
-    lax.fori_loop(0, 16, halve, 0)
-    m_a = [post(m_low.at[lax.rem(at_a + o, 4)], m_first_in.at[o - 1], axis_a[o]) for o in (1, 2, 3)]
-    for copy in m_a:
-        copy.start()
+    pack(core)
+    m_own = [post(m_low.at[core, lax.rem(at_a + o, 4)], m_first_in.at[o - 1], axis_a[o]) for o in (1, 2, 3)]
+    for copy in m_own:
+        copy.start()
+    m_a = m_a + m_own
 
     for copy in d_y:
         copy.wait_recv()
@@ -470,8 +488,8 @@
     for copy in m_a:
         copy.wait_recv()
     for b in range(4):
-        part = m_first[at_a, b]
-        for o in range(3):
+        part = m_keep[block_rows(core, at_a, b), :]
+        for o in range(7):
             part = part + m_first_in[o, b].astype(F32)
         m_second[b] = part
     m_b = [post(m_second.at[lax.rem(at_b + o, 4)], m_second_in.at[o - 1], axis_b[o]) for o in (1, 2, 3)]
@@ -626,12 +644,9 @@
             bf16(ROWS, E),
             f32(E, ROWS),
             bf16(ROWS, COLS),
-            bf16(D_METH, E_HALF),
-            bf16(D_METH, E_HALF),
             f32(D_METH, E_HALF),
-            f32(4, 4, 48, E_HALF),
-            bf16(4, 4, 48, E_HALF),
-            bf16(3, 4, 48, E_HALF),
+            bf16(2, 4, 4, 48, E_HALF),
+            bf16(7, 4, 48, E_HALF),
             f32(4, 48, E_HALF),
             f32(3, 48, E_HALF),
             f32(8, 2, 16, 128),

time: 101 us -> 102 us (level)
  no operation moved by 1% of the time
where the time goes in v9:
time: 102 us; the launch traced here: 101 us
  Pallas kernels  99.4 us (97%)
  between operations  2.09 us (2%)
    pallas_call x1, Pallas kernels, step_call(): pl.pallas_call(step_kernel, out_shape=(jax.ShapeDtypeStruct((8, 4, 16, D_...  96.6 us
    pallas_call x1, Pallas kernels, hand_over(): pl.pallas_call(hand_over_kernel, out_shape=(jax.ShapeDtypeStruct((D_SLICE...  2.76 us

profile of v9, /device:TPU:1, one launch (start us, length us, event | category | flops | bytes accessed | tf_op | source)
XLA Modules:
  0.0 101.4 jit_solution(11638407786505858259)
XLA Ops:
  1.9 96.6 %contrastive_step.1 = (f32[8,4,16,256]{3,2,1,0:T(8,128)}, f32[2,768,256]{2,1,0:T(8,128)}) custom-call(s32[16,384]{1,0:T(8,128)} %bitcast.5, s32[16,384]{1,0:T(8,128)} %bitcast.6, s32[3,128]{1,0:T(4,128)} %bitcast.7, bf16[4096,256]{1,0:T(8,128)(2,1)} %dna_table_hbm.1, bf16[512,768]{1,0:T(8,128)(2,1)} %meth_table_hbm.1, bf16[256,512]{1,0:T(8,128)(2,1)} %dna_proj_hbm.1, ...), custom_call_target="tpu_custom_call" | custom-call | flops 19000000512 | bytes 8000000 | tf_op jit(solution)/shard_map/contrastive_step/pallas_call | solution.py:613
  98.5 2.8 %hand_over.1 = (f32[256,512]{1,0:T(8,128)}, f32[768,512]{1,0:T(8,128)}) custom-call(f32[512,256]{1,0:T(8,128)} %bitcast.4, f32[2,768,256]{2,1,0:T(8,128)} %get-tuple-element.5.m_in), custom_call_target="tpu_custom_call" | custom-call | tf_op jit(solution)/shard_map/hand_over/pallas_call | solution.py:703

commit v10 on v9

--- a/solution.py
+++ b/solution.py
@@ -18,8 +18,6 @@
 D_METH = 768
 VOCAB_DNA = 4096
 VOCAB_METH = 512
-CHUNK = 1536
-PART = 512
 EMBED = 256
 NIBBLES = 0x0F0F0F0F
 LOG2E = 1.4426950408889634
@@ -116,7 +114,7 @@
     dna_rows,
     row_acc,
     tiles,
-    m_keep,
+    m_acc,
     m_low,
     m_first_in,
     m_second,
@@ -365,31 +363,42 @@
     scale = scale_ref[0]
     bias = bias_ref[0]
     slope, offset = scale * -LOG2E, bias * -LOG2E
-    def pair_tile(i, carry):
-        first = pl.multiple_of(i * CHUNK, 128)
-        partners = []
-        for j in range(CHUNK // ROWS):
-            z_of, y_of = group(i * (CHUNK // ROWS) + j)
-            partners.append(pair_wide[...] - (z_of * 4 + y_of) * ROWS)
-        parts = []
-        for p in range(CHUNK // PART):
-            rows_m = meth_rows[:, pl.ds(pl.multiple_of(first + p * PART, 128), PART)]
-            dots = jnp.dot(dna_rows[...], rows_m, preferred_element_type=F32)
-            lower = 1.0 + jnp.exp2(slope * dots + offset)
-            prob = pl.reciprocal(lower, approx=True)
-            prob = prob * (2.0 - lower * prob)
-            for g in range(PART // 128):
-                part = prob[:, g * 128 : (g + 1) * 128]
-                j, low = divmod(p * PART + g * 128, ROWS)
-                lane = lax.broadcasted_iota(jnp.int32, (ROWS, 128), 1) + low
-                parts.append(jnp.where(partners[j] == lane, part - 1.0, part).astype(BF16))
-        tile = jnp.concatenate(parts, axis=1)
-        tiles[:, pl.ds(first, CHUNK)] = tile
-        return carry
-
-    lax.fori_loop(0, COLS // CHUNK, pair_tile, 0)
-
-    row_acc[...] = lax.dot_general(meth_rows[...], tiles[...], NT, preferred_element_type=F32)
+    def lanes_of(c):
+        return slice(c * ROWS, (c + 1) * ROWS)
+
+    def probabilities(c, dots):
+        z_of, y_of = group(c)
+        partner = pair_wide[...] - (z_of * 4 + y_of) * ROWS
+        lower = 1.0 + jnp.exp2(slope * dots + offset)
+        prob = pl.reciprocal(lower, approx=True)
+        prob = prob * (2.0 - lower * prob)
+        for g in range(ROWS // 128):
+            part = prob[:, g * 128 : (g + 1) * 128]
+            lane = lax.broadcasted_iota(jnp.int32, (ROWS, 128), 1) + g * 128
+            first = c * ROWS + g * 128
+            tiles[:, first : first + 128] = jnp.where(partner == lane, part - 1.0, part).astype(BF16)
+
+    def back_of(c, col_dots):
+        up = scale * col_dots
+        unit_m = meth_unit[:, lanes_of(c)]
+        inner = jnp.sum(unit_m * up, axis=0, keepdims=True)
+        return (meth_inv[:, lanes_of(c)] * (up - unit_m * inner)).astype(BF16)
+
+    def add_head(c, back):
+        part = lax.dot_general(meth_pooled[:, lanes_of(c)], back, NT, preferred_element_type=F32)
+        m_acc[...] = part if c == 0 else m_acc[...] + part
+
+    last = COLS // ROWS - 1
+    for c in range(last + 1):
+        rows_m = meth_rows[:, lanes_of(c)]
+        dots = jnp.dot(dna_rows[...], rows_m, preferred_element_type=F32)
+        if c > 0:
+            col_dots = jnp.dot(dna_rowst[...], tiles[:, lanes_of(c - 1)], preferred_element_type=F32)
+        probabilities(c, dots)
+        if c > 0:
+            add_head(c - 1, back_of(c - 1, col_dots))
+        part = lax.dot_general(rows_m, tiles[:, lanes_of(c)], NT, preferred_element_type=F32)
+        row_acc[...] = part if c == 0 else row_acc[...] + part
 
     other = 1 - core
     up = scale * row_acc[...]
@@ -398,17 +407,9 @@
     back_swap = post(back_all.at[pl.ds(pl.multiple_of(other * 256, 16), 256)], back_sib, sibling)
     back_swap.start()
 
-    def col_tile(i, carry):
-        first = pl.multiple_of(i * CHUNK, 128)
-        for p in range(CHUNK // PART):
-            lanes = pl.ds(pl.multiple_of(first + p * PART, 128), PART)
-            up = scale * jnp.dot(dna_rowst[...], tiles[:, lanes], preferred_element_type=F32)
-            unit_m = meth_unit[:, lanes]
-            inner = jnp.sum(unit_m * up, axis=0, keepdims=True)
-            meth_rows[:, lanes] = (meth_inv[:, lanes] * (up - unit_m * inner)).astype(BF16)
-        return carry
-
-    lax.fori_loop(0, 1, col_tile, 0)
+    col_dots = jnp.dot(dna_rowst[...], tiles[:, lanes_of(last)], preferred_element_type=F32)
+    add_head(last, back_of(last, col_dots))
+
     back_swap.wait_recv()
     for a in range(4):
         rows = pl.ds(pl.multiple_of(core * 256 + a * 64, 16), 64)
@@ -417,7 +418,44 @@
     back_x = [post(back_half.at[lax.rem(x + o, 4)], back_in.at[o - 1], ring[o]) for o in (1, 2, 3)]
     for copy in back_x:
         copy.start()
-    lax.fori_loop(1, 2, col_tile, 0)
+    swap = core == 1
+
+    def pick(one, two):
+        return tuple(jnp.where(swap, q, p) for p, q in zip(one, two))
+
+    axis_a = [pick(p, q) for p, q in zip(ring, along_y)]
+    axis_b = [pick(q, p) for p, q in zip(ring, along_y)]
+    cross_a = [pick(q, p) for p, q in zip(cross, cross_y)]
+    at_a = jnp.where(swap, y, x)
+    at_b = jnp.where(swap, x, y)
+    at_cross = jnp.where(swap, x, y)
+
+    def block_rows(which, a, b):
+        return pl.ds(pl.multiple_of(jnp.where(which == 1, a * 192 + b * 48, b * 192 + a * 48), 16), 48)
+
+    def half_lanes(which):
+        return pl.ds(pl.multiple_of(which * E_HALF, 128), E_HALF)
+
+    def pack(which):
+        def pack_block(i, carry):
+            a, b = lax.div(i, 4), lax.rem(i, 4)
+            m_low[which, a, b] = m_acc[block_rows(which, a, b), half_lanes(which)].astype(BF16)
+            return carry
+
+        lax.fori_loop(0, 16, pack_block, 0)
+
+    pack(other)
+    m_a = [
+        post(m_low.at[other, lax.rem(at_cross + o, 4)], m_first_in.at[3 + o], sibling if o == 0 else cross_a[o])
+        for o in range(4)
+    ]
+    for copy in m_a:
+        copy.start()
+    pack(core)
+    m_own = [post(m_low.at[core, lax.rem(at_a + o, 4)], m_first_in.at[o - 1], axis_a[o]) for o in (1, 2, 3)]
+    for copy in m_own:
+        copy.start()
+    m_a = m_a + m_own
 
     for copy in back_x:
         copy.wait_recv()
@@ -435,48 +473,6 @@
     for copy in d_y:
         copy.start()
 
-    swap = core == 1
-
-    def pick(one, two):
-        return tuple(jnp.where(swap, q, p) for p, q in zip(one, two))
-
-    axis_a = [pick(p, q) for p, q in zip(ring, along_y)]
-    axis_b = [pick(q, p) for p, q in zip(ring, along_y)]
-    cross_a = [pick(q, p) for p, q in zip(cross, cross_y)]
-    at_a = jnp.where(swap, y, x)
-    at_b = jnp.where(swap, x, y)
-    at_cross = jnp.where(swap, x, y)
-
-    def half_head(which):
-        rows = pl.ds(pl.multiple_of(which * E_HALF, 16), E_HALF)
-        return lax.dot_general(meth_pooled[...], meth_rows[rows, :], NT, preferred_element_type=F32)
-
-    def block_rows(which, a, b):
-        return pl.ds(pl.multiple_of(jnp.where(which == 1, a * 192 + b * 48, b * 192 + a * 48), 16), 48)
-
-    def pack(which):
-        def pack_block(i, carry):
-            a, b = lax.div(i, 4), lax.rem(i, 4)
-            m_low[which, a, b] = m_keep[block_rows(which, a, b), :].astype(BF16)
-            return carry
-
-        lax.fori_loop(0, 16, pack_block, 0)
-
-    m_keep[...] = half_head(other)
-    pack(other)
-    m_a = [
-        post(m_low.at[other, lax.rem(at_cross + o, 4)], m_first_in.at[3 + o], sibling if o == 0 else cross_a[o])
-        for o in range(4)
-    ]
-    for copy in m_a:
-        copy.start()
-    m_keep[...] = half_head(core)
-    pack(core)
-    m_own = [post(m_low.at[core, lax.rem(at_a + o, 4)], m_first_in.at[o - 1], axis_a[o]) for o in (1, 2, 3)]
-    for copy in m_own:
-        copy.start()
-    m_a = m_a + m_own
-
     for copy in d_y:
         copy.wait_recv()
     d_sum = d_first[y]
@@ -488,7 +484,7 @@
     for copy in m_a:
         copy.wait_recv()
     for b in range(4):
-        part = m_keep[block_rows(core, at_a, b), :]
+        part = m_acc[block_rows(core, at_a, b), half_lanes(core)]
         for o in range(7):
             part = part + m_first_in[o, b].astype(F32)
         m_second[b] = part
@@ -644,7 +640,7 @@
             bf16(ROWS, E),
             f32(E, ROWS),
             bf16(ROWS, COLS),
-            f32(D_METH, E_HALF),
+            f32(D_METH, E),
             bf16(2, 4, 4, 48, E_HALF),
             bf16(7, 4, 48, E_HALF),
             f32(4, 48, E_HALF),

time: 102 us -> 97 us (0.951)
  Pallas kernels: 99.4 us -> 94.8 us
    pallas_call x1, Pallas kernels: 96.6 us -> 92 us  [step_call(): pl.pallas_call(step_kernel, out_shape=(jax.ShapeDtypeStruct((8, 4, 16, D_...]
where the time goes in v10:
time: 97 us; the launch traced here: 96.9 us
  Pallas kernels  94.8 us (98%)
  between operations  2.09 us (2%)
    pallas_call x1, Pallas kernels, step_call(): pl.pallas_call(step_kernel, out_shape=(jax.ShapeDtypeStruct((8, 4, 16, D_...  92 us
    pallas_call x1, Pallas kernels, hand_over(): pl.pallas_call(hand_over_kernel, out_shape=(jax.ShapeDtypeStruct((D_SLICE...  2.76 us

profile of v10, /device:TPU:1, one launch (start us, length us, event | category | flops | bytes accessed | tf_op | source)
XLA Modules:
  0.0 96.9 jit_solution(8277927371349952770)
XLA Ops:
  1.9 92.0 %contrastive_step.1 = (f32[8,4,16,256]{3,2,1,0:T(8,128)}, f32[2,768,256]{2,1,0:T(8,128)}) custom-call(s32[16,384]{1,0:T(8,128)} %bitcast.5, s32[16,384]{1,0:T(8,128)} %bitcast.6, s32[3,128]{1,0:T(4,128)} %bitcast.7, bf16[4096,256]{1,0:T(8,128)(2,1)} %dna_table_hbm.1, bf16[512,768]{1,0:T(8,128)(2,1)} %meth_table_hbm.1, bf16[256,512]{1,0:T(8,128)(2,1)} %dna_proj_hbm.1, ...), custom_call_target="tpu_custom_call" | custom-call | flops 19000000512 | bytes 8000000 | tf_op jit(solution)/shard_map/contrastive_step/pallas_call | solution.py:609
  94.0 2.8 %hand_over.1 = (f32[256,512]{1,0:T(8,128)}, f32[768,512]{1,0:T(8,128)}) custom-call(f32[512,256]{1,0:T(8,128)} %bitcast.4, f32[2,768,256]{2,1,0:T(8,128)} %get-tuple-element.5.m_in), custom_call_target="tpu_custom_call" | custom-call | tf_op jit(solution)/shard_map/hand_over/pallas_call | solution.py:699

commit v11 on v10

--- a/solution.py
+++ b/solution.py
@@ -278,7 +278,6 @@
     own = pool_block(x, core)
     from_left = pool_block(lax.rem(x + 3, 4), core)
     from_right = pool_block(lax.rem(x + 1, 4), core)
-    from_across = pool_block(lax.rem(x + 2, 4), core)
     pool_right = post(own, own, ring[1])
     pool_left = post(own, own, ring[3])
     pool_sib = post(own, own, sibling)
@@ -287,9 +286,9 @@
     pool_sib.start()
     half_left = pool_block(lax.rem(x + 3, 4), core, 0, 128)
     half_right = pool_block(lax.rem(x + 1, 4), core, 128, 128)
-    relay_right = post(half_left, half_left, ring[1])
-    relay_left = post(half_right, half_right, ring[3])
-    pool_fwd = [post(part, part, sibling) for part in (from_left, from_right, from_across)]
+    relay_right = [post(half_left, half_left, device) for device in (ring[1], cross[1])]
+    relay_left = [post(half_right, half_right, device) for device in (ring[3], cross[3])]
+    pool_fwd = [post(part, part, sibling) for part in (from_left, from_right)]
 
     fetch[1].wait()
     fetch[2].wait()
@@ -327,17 +326,18 @@
 
     lax.fori_loop(0, 2, embed_meth, 0)
     pool_right.wait_recv()
-    relay_right.start()
+    for copy in relay_right:
+        copy.start()
     pool_left.wait_recv()
-    relay_left.start()
+    for copy in relay_left:
+        copy.start()
     pool_fwd[0].start()
     pool_fwd[1].start()
     proj_far.wait_recv()
     proj_fwd.start()
     lax.fori_loop(2, 4, embed_meth, 0)
-    relay_right.wait_recv()
-    relay_left.wait_recv()
-    pool_fwd[2].start()
+    for copy in relay_right + relay_left:
+        copy.wait_recv()
     proj_sib.wait_recv()
     proj_fwd.wait_recv()
     pair_copy.wait_recv()
@@ -463,12 +463,11 @@
     for o in range(3):
         back = back + back_in[o].astype(F32)
     back = back.astype(BF16)
-    for s in range(4):
-        features = dna_pooled[s * D_SLICE : (s + 1) * D_SLICE, :]
-        part = lax.dot_general(back, features, NT, preferred_element_type=F32)
-        for a in range(4):
-            d_first[a, :, s * D_SLICE : (s + 1) * D_SLICE] = part[a * 16 : (a + 1) * 16, :]
-            d_first_low[a, :, s * D_SLICE : (s + 1) * D_SLICE] = part[a * 16 : (a + 1) * 16, :].astype(BF16)
+    wide = jnp.concatenate([back, back], axis=0)
+    part = lax.dot_general(dna_pooled[...], wide, NT, preferred_element_type=F32).T
+    for a in range(4):
+        d_first[a] = part[a * 16 : (a + 1) * 16, :]
+        d_first_low[a] = part[a * 16 : (a + 1) * 16, :].astype(BF16)
     d_y = [post(d_first_low.at[lax.rem(y + o, 4)], d_first_in.at[o - 1], along_y[o]) for o in (1, 2, 3)]
     for copy in d_y:
         copy.start()

time: 97 us -> 96.2 us (level)
  no operation moved by 1% of the time
where the time goes in v11:
time: 96.2 us; the launch traced here: 96.1 us
  Pallas kernels  94 us (98%)
  between operations  2.09 us (2%)
    pallas_call x1, Pallas kernels, step_call(): pl.pallas_call(step_kernel, out_shape=(jax.ShapeDtypeStruct((8, 4, 16, D_...  91.2 us
    pallas_call x1, Pallas kernels, hand_over(): pl.pallas_call(hand_over_kernel, out_shape=(jax.ShapeDtypeStruct((D_SLICE...  2.76 us

profile of v11, /device:TPU:1, one launch (start us, length us, event | category | flops | bytes accessed | tf_op | source)
XLA Modules:
  0.0 96.1 jit_solution(740586843769182507)
XLA Ops:
  1.9 91.2 %contrastive_step.1 = (f32[8,4,16,256]{3,2,1,0:T(8,128)}, f32[2,768,256]{2,1,0:T(8,128)}) custom-call(s32[16,384]{1,0:T(8,128)} %bitcast.5, s32[16,384]{1,0:T(8,128)} %bitcast.6, s32[3,128]{1,0:T(4,128)} %bitcast.7, bf16[4096,256]{1,0:T(8,128)(2,1)} %dna_table_hbm.1, bf16[512,768]{1,0:T(8,128)(2,1)} %meth_table_hbm.1, bf16[256,512]{1,0:T(8,128)(2,1)} %dna_proj_hbm.1, ...), custom_call_target="tpu_custom_call" | custom-call | flops 19000000512 | bytes 8000000 | tf_op jit(solution)/shard_map/contrastive_step/pallas_call | solution.py:608
  93.1 2.8 %hand_over.1 = (f32[256,512]{1,0:T(8,128)}, f32[768,512]{1,0:T(8,128)}) custom-call(f32[512,256]{1,0:T(8,128)} %bitcast.4, f32[2,768,256]{2,1,0:T(8,128)} %get-tuple-element.5.m_in), custom_call_target="tpu_custom_call" | custom-call | tf_op jit(solution)/shard_map/hand_over/pallas_call | solution.py:698

commit v12 on v11

--- a/solution.py
+++ b/solution.py
@@ -43,6 +43,14 @@
     pl.semaphore_signal(
         pltpu.get_barrier_semaphore(), inc=1, device_id=device, device_id_type=MESH
     )
+
+
+def repeat(first, last, body):
+    def step(i, carry):
+        body(i)
+        return carry
+
+    lax.fori_loop(first, last, step, 0)
 
 
 def send(src, dst, send_sem, recv_sem, device):
@@ -122,6 +130,7 @@
     third,
     third_in,
     third_all,
+    total,
     back_all,
     back_sib,
     back_half,
@@ -134,6 +143,8 @@
     d_fin,
     ids_send,
     ids_recv,
+    z_send,
+    z_recv,
     send_sems,
     recv_sems,
     local_sems,
@@ -146,7 +157,6 @@
     cross = [device_at(z, y, lax.rem(x + o, 4), 1 - core) for o in range(4)]
     along_y = [device_at(z, lax.rem(y + o, 4), x, core) for o in range(4)]
     cross_y = [device_at(z, lax.rem(y + o, 4), x, 1 - core) for o in range(4)]
-    along_z = [device_at(lax.rem(z + o, 8), y, x, core) for o in range(8)]
     ring_place = x_hi * 4 + mp
     nearest = lax.rem(lax.div(ring_place + 1, 2), 4)
 
@@ -186,25 +196,27 @@
         z_of, y_of = group(dy)
         return ((z_of * 4 + y_of) * 2 + half, dy)
 
-    targets = [at_ring_place(z + 8 - s, y + 4 - mp, lax.rem(s + 2 * mp, 8)) for s in range(8)]
-    sources = [source(s // 2, s % 2) for s in range(8)]
+    def target(s):
+        return at_ring_place(z + 8 - s, y + 4 - mp, lax.rem(s + 2 * mp, 8))
 
     def is_me(device):
         return jnp.logical_and(device[0] == blk, device[1] == mp)
 
-    for s in range(8):
-
-        @pl.when(jnp.logical_not(is_me(sources[s])))
+    def greet(s):
+        device = source(lax.div(s, 2), lax.rem(s, 2))
+
+        @pl.when(jnp.logical_not(is_me(device)))
         def _():
-            signal(sources[s])
+            signal(device)
+
+    repeat(0, 8, greet)
 
     for o in (1, 2, 3):
         signal(ring[o])
         signal(cross[o])
         signal(along_y[o])
         signal(cross_y[o])
-    for o in range(1, 8):
-        signal(along_z[o])
+    repeat(1, 8, lambda o: signal(device_at(lax.rem(z + o, 8), y, x, core)))
     signal(sibling)
     for n in (3, 4, 5, 6):
         fetch[n].wait()
@@ -229,19 +241,20 @@
     slot_lanes = pl.ds(pl.multiple_of(slot * PAIR_DEV, 128), PAIR_DEV)
 
     def ids_copy(s):
-        return send(meth_ids, ids_all.at[:, slot_lanes], ids_send.at[s], ids_recv.at[slot], targets[s])
-
-    for s in range(8):
-
-        @pl.when(jnp.logical_not(is_me(targets[s])))
+        return send(meth_ids, ids_all.at[:, slot_lanes], ids_send.at[s], ids_recv.at[slot], target(s))
+
+    def give_ids(s):
+        @pl.when(jnp.logical_not(is_me(target(s))))
         def _():
             ids_copy(s).start()
 
-        @pl.when(is_me(targets[s]))
+        @pl.when(is_me(target(s)))
         def _():
             local = pltpu.make_async_copy(meth_ids, ids_all.at[:, slot_lanes], local_sems.at[0])
             local.start()
             local.wait()
+
+    repeat(0, 8, give_ids)
 
     pair_copy = post(pairs, pair_all.at[x_hi], ring[2])
     pair_copy.start()
@@ -306,14 +319,17 @@
             def _():
                 arrival.wait_recv()
 
+        def tokens_of(p):
+            first = dy * ROWS + p * EMBED
+            ids = [ids_all[:, pl.ds(pl.multiple_of(first + 128 * g, 128), 128)] for g in range(EMBED // 128)]
+            return jnp.concatenate([jnp.concatenate(token_counts(part, 6, 0), axis=0) for part in ids], axis=1)
+
+        tokens = tokens_of(0)
         for p in range(ROWS // EMBED):
-            first = pl.multiple_of(dy * ROWS + p * EMBED, 128)
-            lanes = pl.ds(first, EMBED)
-            ids = [ids_all[:, pl.ds(pl.multiple_of(first + 128 * g, 128), 128)] for g in range(EMBED // 128)]
-            tokens = jnp.concatenate(
-                [jnp.concatenate(token_counts(part, 6, 0), axis=0) for part in ids], axis=1
-            )
+            lanes = pl.ds(pl.multiple_of(dy * ROWS + p * EMBED, 128), EMBED)
             pooled_m = jnp.dot(meth_tablet[...], tokens, preferred_element_type=F32)
+            if p + 1 < ROWS // EMBED:
+                tokens = tokens_of(p + 1)
             pooled_m = (pooled_m * 0.0625).astype(BF16)
             meth_pooled[:, lanes] = pooled_m
             raw = jnp.dot(meth_projt[...], pooled_m, preferred_element_type=F32)
@@ -482,11 +498,14 @@
 
     for copy in m_a:
         copy.wait_recv()
-    for b in range(4):
+
+    def add_first(b):
         part = m_acc[block_rows(core, at_a, b), half_lanes(core)]
         for o in range(7):
             part = part + m_first_in[o, b].astype(F32)
         m_second[b] = part
+
+    repeat(0, 4, add_first)
     m_b = [post(m_second.at[lax.rem(at_b + o, 4)], m_second_in.at[o - 1], axis_b[o]) for o in (1, 2, 3)]
     for copy in m_b:
         copy.start()
@@ -500,20 +519,24 @@
     third[6, 0] = jnp.zeros((16, 128), F32)
     third[7, 0] = jnp.zeros((16, 128), F32)
 
-    z_sum = [post(third.at[lax.rem(z + o, 8)], third_in.at[o - 1], along_z[o]) for o in range(1, 8)]
-    for copy in z_sum:
-        copy.start()
-    for copy in z_sum:
-        copy.wait_recv()
-    total = third[z]
-    for o in range(7):
-        total = total + third_in[o]
-    third_all[z] = total
-    z_back = [post(third_all.at[z], third_all.at[z], along_z[o]) for o in range(1, 8)]
-    for copy in z_back:
-        copy.start()
-    for copy in z_back:
-        copy.wait_recv()
+    def z_sum(o):
+        at = lax.rem(z + o, 8)
+        return send(third.at[at], third_in.at[o - 1], z_send.at[o - 1], z_recv.at[o - 1], device_at(at, y, x, core))
+
+    def z_back(o):
+        device = device_at(lax.rem(z + o, 8), y, x, core)
+        return send(third_all.at[z], third_all.at[z], z_send.at[6 + o], z_recv.at[6 + o], device)
+
+    def add_z(o):
+        z_sum(o).wait_recv()
+        total[...] = total[...] + third_in[o - 1]
+
+    repeat(1, 8, lambda o: z_sum(o).start())
+    total[...] = third[z]
+    repeat(1, 8, add_z)
+    third_all[z] = total[...]
+    repeat(1, 8, lambda o: z_back(o).start())
+    repeat(1, 8, lambda o: z_back(o).wait_recv())
 
     for s in range(8):
         d_slab[y, :, s * 128 : (s + 1) * 128] = third_all[s, 1]
@@ -587,14 +610,17 @@
     for copy in written:
         copy.wait()
 
-    for s in range(8):
-
-        @pl.when(jnp.logical_not(is_me(targets[s])))
+    def ids_left(s):
+        @pl.when(jnp.logical_not(is_me(target(s))))
         def _():
             ids_copy(s).wait_send()
 
+    repeat(0, 8, ids_left)
+
     for copy in taken:
         copy.wait_send()
+    repeat(1, 8, lambda o: z_sum(o).wait_send())
+    repeat(1, 8, lambda o: z_back(o).wait_send())
 
 
 def step_call(*args):
@@ -647,6 +673,7 @@
             f32(8, 2, 16, 128),
             f32(7, 2, 16, 128),
             f32(8, 2, 16, 128),
+            f32(2, 16, 128),
             bf16(E, ROWS),
             bf16(256, ROWS),
             bf16(4, 64, ROWS),
@@ -659,6 +686,8 @@
             f32(8, 4, 16, D_SLICE),
             dma((8,)),
             dma((8,)),
+            dma((14,)),
+            dma((14,)),
             dma((N_COPIES,)),
             dma((N_COPIES,)),
             dma((8,)),

time: 96.2 us -> 96.5 us (level)
  no operation moved by 1% of the time
where the time goes in v12:
time: 96.5 us; the launch traced here: 96.4 us
  Pallas kernels  94.3 us (98%)
  between operations  2.09 us (2%)
    pallas_call x1, Pallas kernels, step_call(): pl.pallas_call(step_kernel, out_shape=(jax.ShapeDtypeStruct((8, 4, 16, D_...  91.5 us
    pallas_call x1, Pallas kernels, hand_over(): pl.pallas_call(hand_over_kernel, out_shape=(jax.ShapeDtypeStruct((D_SLICE...  2.76 us

profile of v12, /device:TPU:1, one launch (start us, length us, event | category | flops | bytes accessed | tf_op | source)
XLA Modules:
  0.0 96.4 jit_solution(15607948741871033021)
XLA Ops:
  1.9 91.5 %contrastive_step.1 = (f32[8,4,16,256]{3,2,1,0:T(8,128)}, f32[2,768,256]{2,1,0:T(8,128)}) custom-call(s32[16,384]{1,0:T(8,128)} %bitcast.5, s32[16,384]{1,0:T(8,128)} %bitcast.6, s32[3,128]{1,0:T(4,128)} %bitcast.7, bf16[4096,256]{1,0:T(8,128)(2,1)} %dna_table_hbm.1, bf16[512,768]{1,0:T(8,128)(2,1)} %meth_table_hbm.1, bf16[256,512]{1,0:T(8,128)(2,1)} %dna_proj_hbm.1, ...), custom_call_target="tpu_custom_call" | custom-call | flops 19000000512 | bytes 8000000 | tf_op jit(solution)/shard_map/contrastive_step/pallas_call | solution.py:634
  93.5 2.8 %hand_over.1 = (f32[256,512]{1,0:T(8,128)}, f32[768,512]{1,0:T(8,128)}) custom-call(f32[512,256]{1,0:T(8,128)} %bitcast.4, f32[2,768,256]{2,1,0:T(8,128)} %get-tuple-element.5.m_in), custom_call_target="tpu_custom_call" | custom-call | tf_op jit(solution)/shard_map/hand_over/pallas_call | solution.py:727

commit v13 on v11

--- a/solution.py
+++ b/solution.py
@@ -19,6 +19,7 @@
 VOCAB_DNA = 4096
 VOCAB_METH = 512
 EMBED = 256
+PART = 256
 NIBBLES = 0x0F0F0F0F
 LOG2E = 1.4426950408889634
 E_HALF = 256
@@ -366,39 +367,62 @@
     def lanes_of(c):
         return slice(c * ROWS, (c + 1) * ROWS)
 
-    def probabilities(c, dots):
-        z_of, y_of = group(c)
-        partner = pair_wide[...] - (z_of * 4 + y_of) * ROWS
+    def part_of(c, p):
+        return slice(c * ROWS + p * PART, c * ROWS + (p + 1) * PART)
+
+    def logit_dots(c, p):
+        return jnp.dot(dna_rows[...], meth_rows[:, part_of(c, p)], preferred_element_type=F32)
+
+    def probabilities(c, p, partner, dots):
         lower = 1.0 + jnp.exp2(slope * dots + offset)
         prob = pl.reciprocal(lower, approx=True)
         prob = prob * (2.0 - lower * prob)
-        for g in range(ROWS // 128):
+        for g in range(PART // 128):
             part = prob[:, g * 128 : (g + 1) * 128]
-            lane = lax.broadcasted_iota(jnp.int32, (ROWS, 128), 1) + g * 128
-            first = c * ROWS + g * 128
+            low = p * PART + g * 128
+            lane = lax.broadcasted_iota(jnp.int32, (ROWS, 128), 1) + low
+            first = c * ROWS + low
             tiles[:, first : first + 128] = jnp.where(partner == lane, part - 1.0, part).astype(BF16)
 
-    def back_of(c, col_dots):
-        up = scale * col_dots
-        unit_m = meth_unit[:, lanes_of(c)]
+    def col_dots(c, p):
+        return jnp.dot(dna_rowst[...], tiles[:, part_of(c, p)], preferred_element_type=F32)
+
+    def back_of(c, p, dots):
+        up = scale * dots
+        unit_m = meth_unit[:, part_of(c, p)]
         inner = jnp.sum(unit_m * up, axis=0, keepdims=True)
-        return (meth_inv[:, lanes_of(c)] * (up - unit_m * inner)).astype(BF16)
-
-    def add_head(c, back):
+        return (meth_inv[:, part_of(c, p)] * (up - unit_m * inner)).astype(BF16)
+
+    def add_head(c, parts):
+        back = jnp.concatenate(parts, axis=1)
         part = lax.dot_general(meth_pooled[:, lanes_of(c)], back, NT, preferred_element_type=F32)
         m_acc[...] = part if c == 0 else m_acc[...] + part
 
+    def add_rows(c):
+        part = lax.dot_general(meth_rows[:, lanes_of(c)], tiles[:, lanes_of(c)], NT, preferred_element_type=F32)
+        row_acc[...] = part if c == 0 else row_acc[...] + part
+
     last = COLS // ROWS - 1
+    n_parts = ROWS // PART
+    dots = logit_dots(0, 0)
     for c in range(last + 1):
-        rows_m = meth_rows[:, lanes_of(c)]
-        dots = jnp.dot(dna_rows[...], rows_m, preferred_element_type=F32)
+        z_of, y_of = group(c)
+        partner = pair_wide[...] - (z_of * 4 + y_of) * ROWS
+        parts = []
+        for p in range(n_parts):
+            here = dots
+            if c > 0:
+                cols = col_dots(c - 1, p)
+            if p + 1 < n_parts:
+                dots = logit_dots(c, p + 1)
+            probabilities(c, p, partner, here)
+            if c > 0:
+                parts.append(back_of(c - 1, p, cols))
+        if c < last:
+            dots = logit_dots(c + 1, 0)
         if c > 0:
-            col_dots = jnp.dot(dna_rowst[...], tiles[:, lanes_of(c - 1)], preferred_element_type=F32)
-        probabilities(c, dots)
-        if c > 0:
-            add_head(c - 1, back_of(c - 1, col_dots))
-        part = lax.dot_general(rows_m, tiles[:, lanes_of(c)], NT, preferred_element_type=F32)
-        row_acc[...] = part if c == 0 else row_acc[...] + part
+            add_head(c - 1, parts)
+        add_rows(c)
 
     other = 1 - core
     up = scale * row_acc[...]
@@ -407,8 +431,7 @@
     back_swap = post(back_all.at[pl.ds(pl.multiple_of(other * 256, 16), 256)], back_sib, sibling)
     back_swap.start()
 
-    col_dots = jnp.dot(dna_rowst[...], tiles[:, lanes_of(last)], preferred_element_type=F32)
-    add_head(last, back_of(last, col_dots))
+    add_head(last, [back_of(last, p, col_dots(last, p)) for p in range(n_parts)])
 
     back_swap.wait_recv()
     for a in range(4):

time: 96.2 us -> 96.3 us (level)
  no operation moved by 1% of the time
where the time goes in v13:
time: 96.3 us; the launch traced here: 96.2 us
  Pallas kernels  94.1 us (98%)
  between operations  2.11 us (2%)
    pallas_call x1, Pallas kernels, step_call(): pl.pallas_call(step_kernel, out_shape=(jax.ShapeDtypeStruct((8, 4, 16, D_...  91.3 us
    pallas_call x1, Pallas kernels, hand_over(): pl.pallas_call(hand_over_kernel, out_shape=(jax.ShapeDtypeStruct((D_SLICE...  2.76 us

profile of v13, /device:TPU:1, one launch (start us, length us, event | category | flops | bytes accessed | tf_op | source)
XLA Modules:
  0.0 96.2 jit_solution(2776543733328636558)
XLA Ops:
  1.9 91.3 %contrastive_step.1 = (f32[8,4,16,256]{3,2,1,0:T(8,128)}, f32[2,768,256]{2,1,0:T(8,128)}) custom-call(s32[16,384]{1,0:T(8,128)} %bitcast.5, s32[16,384]{1,0:T(8,128)} %bitcast.6, s32[3,128]{1,0:T(4,128)} %bitcast.7, bf16[4096,256]{1,0:T(8,128)(2,1)} %dna_table_hbm.1, bf16[512,768]{1,0:T(8,128)(2,1)} %meth_table_hbm.1, bf16[256,512]{1,0:T(8,128)(2,1)} %dna_proj_hbm.1, ...), custom_call_target="tpu_custom_call" | custom-call | flops 19000000512 | bytes 8000000 | tf_op jit(solution)/shard_map/contrastive_step/pallas_call | solution.py:631
  93.2 2.8 %hand_over.1 = (f32[256,512]{1,0:T(8,128)}, f32[768,512]{1,0:T(8,128)}) custom-call(f32[512,256]{1,0:T(8,128)} %bitcast.4, f32[2,768,256]{2,1,0:T(8,128)} %get-tuple-element.5.m_in), custom_call_target="tpu_custom_call" | custom-call | tf_op jit(solution)/shard_map/hand_over/pallas_call | solution.py:721
